TPU v7x, 256 devices: a whole 4x4x8 slice. The times are simulated.
256 devices in a mesh: replica: 8 (over y, x_hi), fsdp: 32 (over x_lo, z, core).
Axes of the slice: x: 4 (x_hi: 2, x_lo: 2; x = x_hi * 2 + x_lo), y: 4, z: 8, core: 2. Of those that a mesh axis runs over, the one named last changes fastest.
Arguments:
- local_params: bfloat16 [8, 4096, 14336], P('replica', 'fsdp'), may hold values from -6 to 6
- outer_params: float32 [32, 32, 8, 14336], P('fsdp', None, None, 'replica'), may hold values from -6 to 6
- outer_momentum: float32 [32, 32, 8, 14336], P('fsdp', None, None, 'replica'), may hold values from -3 to 3
- block_lengths: int32 [32, 24], replicated, may hold values from 1 to 8, 128 in all within a row
- block_owners: int32 [32, 32], replicated, may hold values from 0 to 31, each once within a row
Outputs:
- new_outer: float32 [32, 32, 8, 14336], P('fsdp', None, None, 'replica')
- new_momentum: float32 [32, 32, 8, 14336], P('fsdp', None, None, 'replica')
- new_params: bfloat16 [4096, 14336], P('fsdp')
Inputs may be any that keep to these rules, and one draw needn't show every extreme that they name: `block_lengths`: each row sums to 128 and has a block of exactly 8 rows. `block_owners`: each row is a permutation; only its first 24 entries name owners, so an owner gets at most one block from each index.
All inputs are finite; a program needn't handle non-finite values.
Results may differ from a plain program's by a relative error of at most 0.014.
Values may be sent and summed in bfloat16 or wider, within the bound.
No kernel may reach another device: no remote copies, remote signals or barrier semaphores. Data moves between devices by JAX's collectives and lax.ppermute only.
A program may use at most 128 MiB of HBM per device.

v0:
```python
import jax
import jax.numpy as jnp
from jax import lax
from jax.sharding import PartitionSpec as P

outer_rate = 0.7
momentum_decay = 0.9


def tables(block_lengths, block_owners, owner_count):
    block_count = block_lengths.shape[1]
    offsets = jnp.cumsum(block_lengths, axis=1) - block_lengths
    heads = block_owners[:, :block_count]
    owner_ids = jnp.arange(owner_count, dtype=jnp.int32)
    match = (heads[:, :, None] == owner_ids[None, None, :]).astype(jnp.int32)
    counts = jnp.sum(match * block_lengths[:, :, None], axis=1)
    starts = jnp.sum(match * offsets[:, :, None], axis=1)
    return (offsets, counts, starts)


def locate(offsets, block_lengths, block_owners, row_count):
    row_ids = jnp.arange(row_count, dtype=jnp.int32)
    block_ends = offsets + block_lengths
    block_of_row = jnp.sum(
        (block_ends[:, None, :] <= row_ids[None, :, None]).astype(jnp.int32), axis=2
    )
    owner_of_row = jnp.take_along_axis(block_owners, block_of_row, axis=1)
    slot_of_row = row_ids[None, :] - jnp.take_along_axis(offsets, block_of_row, axis=1)
    return (owner_of_row, slot_of_row)


def body(local_params, outer_params, outer_momentum, block_lengths, block_owners):
    fsdp_count = lax.axis_size("fsdp")
    group_count = lax.axis_size("replica")
    my_index = lax.axis_index("fsdp")
    own_rows = local_params[0]
    row_count = own_rows.shape[0]
    slots = outer_params.shape[2]
    offsets, counts, starts = tables(block_lengths, block_owners, fsdp_count)
    slot_ids = jnp.arange(slots, dtype=jnp.int32)
    my_starts = lax.dynamic_index_in_dim(starts, my_index, 0, keepdims=False)
    my_counts = lax.dynamic_index_in_dim(counts, my_index, 0, keepdims=False)
    send_rows = (my_starts[:, None] + slot_ids[None, :]).reshape(-1)
    send_live = slot_ids[None, :] < my_counts[:, None]
    incoming = lax.dynamic_index_in_dim(counts, my_index, 1, keepdims=False)
    live_in = slot_ids[None, :] < incoming[:, None]
    my_offsets = lax.dynamic_slice_in_dim(offsets, my_index, 1, 0)
    my_lengths = lax.dynamic_slice_in_dim(block_lengths, my_index, 1, 0)
    my_owners = lax.dynamic_slice_in_dim(block_owners, my_index, 1, 0)
    owner_of_row, slot_of_row = locate(my_offsets, my_lengths, my_owners, row_count)
    back_index = owner_of_row[0] * slots + slot_of_row[0]
    picked = jnp.take(own_rows, send_rows, axis=0, mode="clip").reshape(
        fsdp_count, slots, own_rows.shape[1]
    )
    arrived = lax.all_to_all(
        jnp.where(send_live[:, :, None], picked, jnp.zeros((), own_rows.dtype)),
        "fsdp",
        split_axis=0,
        concat_axis=0,
        tiled=True,
    )
    summed = lax.psum_scatter(
        arrived.astype(jnp.float32).astype(jnp.bfloat16), "replica", scatter_dimension=2, tiled=True
    ).astype(jnp.float32)
    outer_here = outer_params[0]
    pseudo_grad = jnp.where(
        live_in[:, :, None], outer_here - summed / group_count, jnp.float32(0.0)
    )
    fresh_momentum = momentum_decay * outer_momentum[0] + pseudo_grad
    fresh_outer = outer_here - outer_rate * (pseudo_grad + momentum_decay * fresh_momentum)
    fresh_outer, fresh_momentum = (fresh_outer, fresh_momentum)
    complete = lax.all_gather(fresh_outer.astype(jnp.bfloat16), "replica", axis=2, tiled=True)
    returned = lax.all_to_all(complete, "fsdp", split_axis=0, concat_axis=0, tiled=True)
    fresh_rows = jnp.take(
        returned.reshape(fsdp_count * slots, returned.shape[2]), back_index, axis=0, mode="clip"
    )
    return (fresh_outer[None], fresh_momentum[None], fresh_rows)


def solution(mesh):
    in_specs = (
        P("replica", "fsdp", None),
        P("fsdp", None, None, "replica"),
        P("fsdp", None, None, "replica"),
        P(),
        P(),
    )
    out_specs = (
        P("fsdp", None, None, "replica"),
        P("fsdp", None, None, "replica"),
        P("fsdp", None),
    )
    return jax.shard_map(body, mesh=mesh, in_specs=in_specs, out_specs=out_specs, check_vma=False)
```

profile of v0, /device:TPU:40, one launch (start us, length us, event | category | flops | bytes accessed | tf_op | source)
XLA Modules:
  0.0 604.2 jit_solution(16588371810792551242)
XLA Ops:
  7.2 0.0 reduce-scatter.2.cloned.1.call-start
  7.2 0.8 copy.16
  8.0 0.2 reduce_window_sum.11
  8.2 1.2 select_reduce_fusion.1
  9.4 0.1 iota_compare_fusion.1
  9.5 0.1 iota_add_fusion
  9.5 0.1 reshape.273
  9.6 17.3 %gather_fusion = bf16[256,14336]{1,0:T(8,128)(2,1)} fusion(bf16[128,14336]{1,0:T(8,128)(2,1)} %bitcast.307, s32[1024]{0:T(1024)S(1)} %pad_clamp_fusion.2), kind=kCustom, calls=%fused_computation | custom fusion | bytes 14681088 | tf_op jit(solution)/shard_map/jit(_take)/gather | solution.py:52
  26.9 3.6 bitcast_select_fusion
  30.6 173.4 %all_to_all.10 = bf16[32,8,14336]{2,1,0:T(8,128)(2,1)} all-to-all(bf16[32,8,14336]{2,1,0:T(8,128)(2,1)S(1)} %bitcast_select_fusion), channel_id=1, replica_groups=mesh['replica'=8,'fsdp'=32] {'fsdp'}, dimensions={0} | all-to-all | bytes 14680064 | tf_op jit(solution)/shard_map/all_to_all | solution.py:55
  203.9 0.0 copy-start
  203.9 0.0 reduce-scatter.2.cloned.1.call-update
  204.0 0.0 all-gather.2.cloned.1.call-start
  204.0 0.2 dynamic-slice_reduce_fusion
  204.2 0.1 iota_compare_fusion.2
  204.3 107.4 %reduce-scatter.2.cloned.1.call-done = bf16[32,8,1792]{2,1,0:T(8,128)(2,1)} async-done(((bf16[32,8,14336]{2,1,0:T(8,128)(2,1)}), bf16[32,8,1792]{2,1,0:T(8,128)(2,1)}) %reduce-scatter.2.cloned.1.call-update) | async-done | bytes 917520 | tf_op jit(solution)/shard_map/reduce_scatter | solution.py:62
  311.7 0.0 copy-done
  311.7 4.5 fusion.13
  316.2 0.0 all-gather.2.cloned.1.call-update
  316.3 100.6 %all-gather.2.cloned.1.call-done = bf16[32,8,14336]{2,1,0:T(8,128)(2,1)} async-done(((bf16[32,8,1792]{2,1,0:T(8,128)(2,1)}), bf16[32,8,14336]{2,1,0:T(8,128)(2,1)}) %all-gather.2.cloned.1.call-update) | async-done | bytes 7340048 | tf_op jit(solution)/shard_map/all_gather | solution.py:72
  416.8 7.7 %all-to-all-start.1 = ((bf16[32,8,14336]{2,1,0:T(8,128)(2,1)}), bf16[32,8,14336]{2,1,0:T(8,128)(2,1)}, u32[]{:S(2)}, u32[]{:S(2)}) async-start(bf16[32,8,14336]{2,1,0:T(8,128)(2,1)} %all-gather.2.cloned.1.call-done), calls=%async_computation.2 | async-start | bytes 14680064 | tf_op jit(solution)/shard_map/all_to_all | solution.py:73
  424.5 0.7 fusion.2
  425.2 0.1 convert_reduce_fusion
  425.4 1.2 gather_fusion.1
  426.6 0.7 fusion.16
  427.2 0.7 fusion.15
  428.0 15.6 %fusion.11 = s32[128]{0:T(128)S(1)} fusion(s32[128]{0:T(128)S(1)} %convert_reduce_fusion, s32[128]{0:T(128)S(1)} %gather_fusion.1, s32[]{:T(128)} %bitcast.48, s32[]{:T(128)} %bitcast.49, s32[]{:T(128)} %bitcast.50, s32[]{:T(128)} %bitcast.51, s32[]{:T(128)} %bitcast.52, s32[]{:T(128)} %bitcast.54, s32[]{:T(128)} %bitcast.53, s32[]{:T(128)} %bitcast.15, ...), kind=kLoop, calls=%fused_computation.62 | loop fusion | flops 7936 | bytes 1632 | tf_op jit(solution)/shard_map/add | solution.py:51
  443.6 141.8 %all-to-all-done.1 = bf16[32,8,14336]{2,1,0:T(8,128)(2,1)} async-done(((bf16[32,8,14336]{2,1,0:T(8,128)(2,1)}), bf16[32,8,14336]{2,1,0:T(8,128)(2,1)}, u32[]{:S(2)}, u32[]{:S(2)}) %all-to-all-start.1) | async-done | bytes 7340064 | tf_op jit(solution)/shard_map/all_to_all | solution.py:73
  585.4 11.9 %gather_fusion.2 = bf16[128,14336]{1,0:T(8,128)(2,1)} fusion(bf16[256,14336]{1,0:T(8,128)(2,1)} %bitcast.8, s32[1024]{0:T(1024)S(1)} %pad_clamp_fusion), kind=kCustom, calls=%fused_computation.2 | custom fusion | bytes 7340544 | tf_op jit(solution)/shard_map/jit(_take)/gather | solution.py:74
  (7 shorter events, 0.1 us)
Async XLA Ops:
  7.2 304.6 %reduce-scatter.2.cloned.1.call-start = ((), (), s32[]{:S(2)}) async-start(), calls=%async_computation.3 | async-start | bytes 8257536 | tf_op jit(solution)/shard_map/reduce_scatter | solution.py:62
  203.9 107.8 %copy-start = (f32[1,32,8,1792]{3,2,1,0:T(8,128)S(1)}, f32[1,32,8,1792]{3,2,1,0:T(8,128)}, u32[]{:S(2)}) copy-start(f32[1,32,8,1792]{3,2,1,0:T(8,128)} %param.7) | copy-start | bytes 5505028
  204.0 212.9 %all-gather.2.cloned.1.call-start = ((), (), s32[]{:S(2)}) async-start(), calls=%async_computation.4 | async-start | bytes 8257536 | tf_op jit(solution)/shard_map/all_gather | solution.py:72
  416.8 168.5 %all-to-all-start.1 = ((bf16[32,8,14336]{2,1,0:T(8,128)(2,1)}), bf16[32,8,14336]{2,1,0:T(8,128)(2,1)}, u32[]{:S(2)}, u32[]{:S(2)}) async-start(bf16[32,8,14336]{2,1,0:T(8,128)(2,1)} %all-gather.2.cloned.1.call-done), calls=%async_computation.2 | async-start | bytes 14680064 | tf_op jit(solution)/shard_map/all_to_all | solution.py:73
Sparse Core Ops, SparseCore 0:
  204.1 107.5 reduce-scatter.1
  316.4 100.4 all-gather.1
where the time goes:
time: 610 us; the launch traced here: 604 us
  waiting for transfers between devices  350 us (57%)
  blocking collectives  173 us (28%)
  local copies, waits for them, and re-layouts  33.6 us (6%)
  other arithmetic  25.4 us (4%)
  between operations  14.1 us (2%)
  starting transfers between devices  7.77 us (1%)
    all_to_all x1, blocking collectives, body(): lax.all_to_all(jnp.where(send_live[:, :, None], picked, jnp.zeros((), own...  173 us
    all_to_all x1, waiting for transfers between devices, body(): lax.all_to_all(complete, 'fsdp', split_axis=0, concat_axis=0, tiled=True)  142 us
    reduce_scatter x1, waiting for transfers between devices, body(): lax.psum_scatter(arrived.astype(jnp.float32).astype(jnp.bfloat16), 'repli...  107 us
    all_gather x1, waiting for transfers between devices, body(): lax.all_gather(fresh_outer.astype(jnp.bfloat16), 'replica', axis=2, tiled...  101 us
    gather x1, local copies, waits for them, and re-layouts, body(): jnp.take(own_rows, send_rows, axis=0, mode='clip')  17.3 us
    add x1, other arithmetic, body(): back_index = owner_of_row[0] * slots + slot_of_row[0]  15.6 us
  transfers between devices with their start and end apart: 3, of which 3 were waited for; matrix products, arithmetic and copies ran while one was open for 3% of the time, Pallas kernels for 0%

commit v1 on v0

v1 whole, which is shorter than its diff:
```python
import jax
import jax.numpy as jnp
from jax import lax
from jax.sharding import PartitionSpec as P

outer_rate = 0.7
momentum_decay = 0.9


def tables(block_lengths, block_owners, owner_count):
    block_count = block_lengths.shape[1]
    block_ids = jnp.arange(block_count, dtype=jnp.int32)
    before = (block_ids[None, :] < block_ids[:, None]).astype(jnp.int32)
    offsets = jnp.sum(before[None] * block_lengths[:, None, :], axis=2)
    heads = block_owners[:, :block_count]
    owner_ids = jnp.arange(owner_count, dtype=jnp.int32)
    match = (heads[:, :, None] == owner_ids[None, None, :]).astype(jnp.int32)
    counts = jnp.sum(match * block_lengths[:, :, None], axis=1)
    starts = jnp.sum(match * offsets[:, :, None], axis=1)
    return counts, starts


def body(local_params, outer_params, outer_momentum, block_lengths, block_owners):
    fsdp_count = lax.axis_size("fsdp")
    group_count = lax.axis_size("replica")
    my_index = lax.axis_index("fsdp")
    own_rows = local_params[0]
    row_count = own_rows.shape[0]
    slots = outer_params.shape[2]
    columns = outer_params.shape[3]
    summed = lax.psum_scatter(own_rows, "replica", scatter_dimension=1, tiled=True)

    counts, starts = tables(block_lengths, block_owners, fsdp_count)
    slot_ids = jnp.arange(slots, dtype=jnp.int32)
    row_ids = jnp.arange(row_count, dtype=jnp.int32)
    my_starts = lax.dynamic_index_in_dim(starts, my_index, 0, keepdims=False)
    my_counts = lax.dynamic_index_in_dim(counts, my_index, 0, keepdims=False)
    incoming = lax.dynamic_index_in_dim(counts, my_index, 1, keepdims=False)
    live_in = slot_ids[None, :] < incoming[:, None]
    row_of_slot = jnp.where(
        slot_ids[None, :] < my_counts[:, None], my_starts[:, None] + slot_ids[None, :], -1
    ).reshape(-1)
    pick = (row_of_slot[:, None] == row_ids[None, :]).astype(own_rows.dtype)

    packed = jnp.dot(pick, summed, preferred_element_type=jnp.float32).astype(own_rows.dtype)
    arrived = lax.all_to_all(
        packed.reshape(fsdp_count, slots, columns), "fsdp", split_axis=0, concat_axis=0, tiled=True
    ).astype(jnp.float32)
    outer_here = outer_params[0]
    pseudo_grad = jnp.where(
        live_in[:, :, None], outer_here - arrived / group_count, jnp.float32(0.0)
    )
    fresh_momentum = momentum_decay * outer_momentum[0] + pseudo_grad
    fresh_outer = outer_here - outer_rate * (pseudo_grad + momentum_decay * fresh_momentum)
    returned = lax.all_to_all(
        fresh_outer.astype(jnp.bfloat16), "fsdp", split_axis=0, concat_axis=0, tiled=True
    )
    rows = lax.dot_general(
        pick,
        returned.reshape(fsdp_count * slots, columns),
        (((0,), (0,)), ((), ())),
        preferred_element_type=jnp.float32,
    ).astype(jnp.bfloat16)
    fresh_rows = lax.all_gather(rows, "replica", axis=1, tiled=True)
    return (fresh_outer[None], fresh_momentum[None], fresh_rows)


def solution(mesh):
    in_specs = (
        P("replica", "fsdp", None),
        P("fsdp", None, None, "replica"),
        P("fsdp", None, None, "replica"),
        P(),
        P(),
    )
    out_specs = (
        P("fsdp", None, None, "replica"),
        P("fsdp", None, None, "replica"),
        P("fsdp", None),
    )
    return jax.shard_map(body, mesh=mesh, in_specs=in_specs, out_specs=out_specs, check_vma=False)
```

time: 610 us -> 253 us (0.41)
  waiting for transfers between devices: 350 us -> 186 us
  blocking collectives: 173 us -> 29.4 us
  local copies, waits for them, and re-layouts: 33.6 us -> 4.65 us
  other arithmetic: 25.4 us -> 4.87 us
    all_to_all x1, blocking collectives: 173 us -> 29.4 us  [body(): lax.all_to_all(fresh_outer.astype(jnp.bfloat16), 'fsdp', split_axis=0, co...]
    all_to_all x1, waiting for transfers between devices: 142 us -> 25.9 us  [body(): lax.all_to_all(packed.reshape(fsdp_count, slots, columns), 'fsdp', split_...]
    all_gather x1, waiting for transfers between devices: 101 us -> 66.7 us  [body(): fresh_rows = lax.all_gather(rows, 'replica', axis=1, tiled=True)]
    gather x5 -> x0, local copies, waits for them, and re-layouts: 31.9 us -> none  [the longest x1 17.3 us: body(): jnp.take(own_rows, send_rows, axis=0, mode='clip')]
    add x2 -> x0, other arithmetic: 15.6 us -> none  [the longest x1 15.6 us: body(): back_index = owner_of_row[0] * slots + slot_of_row[0]]
    reduce_scatter x1, waiting for transfers between devices: 107 us -> 92.4 us  [body(): lax.psum_scatter(own_rows, 'replica', scatter_dimension=1, tiled=True)]
  transfers between devices with their start and end apart: 3 -> 3, of which waited for: 3 -> 3; matrix products, arithmetic and copies ran while one was open for 3% -> 0% of each run, Pallas kernels for 0% -> 0%
where the time goes in v1:
time: 253 us; the launch traced here: 250 us
  waiting for transfers between devices  186 us (74%)
  blocking collectives  29.4 us (12%)
  between operations  14.1 us (6%)
  starting transfers between devices  7.72 us (3%)
  other arithmetic  4.87 us (2%)
  local copies, waits for them, and re-layouts  4.65 us (2%)
  matrix products  3.56 us (1%)
    reduce_scatter x1, waiting for transfers between devices, body(): lax.psum_scatter(own_rows, 'replica', scatter_dimension=1, tiled=True)  92.4 us
    all_gather x1, waiting for transfers between devices, body(): fresh_rows = lax.all_gather(rows, 'replica', axis=1, tiled=True)  66.7 us
    all_to_all x1, blocking collectives, body(): lax.all_to_all(fresh_outer.astype(jnp.bfloat16), 'fsdp', split_axis=0, co...  29.4 us
    all_to_all x1, waiting for transfers between devices, body(): lax.all_to_all(packed.reshape(fsdp_count, slots, columns), 'fsdp', split_...  25.9 us
    all_to_all x1, starting transfers between devices, body(): lax.all_to_all(packed.reshape(fsdp_count, slots, columns), 'fsdp', split_...  7.64 us
  transfers between devices with their start and end apart: 3, of which 3 were waited for; matrix products, arithmetic and copies ran while one was open for 0% of the time, Pallas kernels for 0%

profile of v1, /device:TPU:40, one launch (start us, length us, event | category | flops | bytes accessed | tf_op | source)
XLA Modules:
  0.0 250.0 jit_solution(9460893973956743732)
XLA Ops:
  7.2 0.0 reduce-scatter.2.cloned.1.call-start
  7.2 0.0 copy-start.1
  7.2 0.0 copy-start.2
  7.2 0.7 reduce-scatter.2.cloned.1.call-update
  7.9 0.0 copy-start
  7.9 0.0 copy-done.1
  7.9 0.1 copy.12
  8.0 0.2 multiply_reduce_fusion
  8.2 0.1 copy.13
  8.2 0.0 copy-done.2
  8.2 0.5 select_reduce_fusion.1
  8.7 0.1 add_select_fusion
  8.8 0.1 select_n.24
  8.9 92.4 %reduce-scatter.2.cloned.1.call-done = bf16[128,1792]{1,0:T(8,128)(2,1)} async-done(((bf16[128,14336]{1,0:T(8,128)(2,1)}), bf16[128,1792]{1,0:T(8,128)(2,1)}) %reduce-scatter.2.cloned.1.call-update) | async-done | bytes 458768 | tf_op jit(solution)/shard_map/reduce_scatter | solution.py:31
  101.3 2.4 fusion
  103.7 7.6 %all-to-all-start = ((bf16[32,8,1792]{2,1,0:T(8,128)(2,1)}), bf16[32,8,1792]{2,1,0:T(8,128)(2,1)S(1)}, u32[]{:S(2)}, u32[]{:S(2)}) async-start(bf16[32,8,1792]{2,1,0:T(8,128)(2,1)} %fusion), calls=%async_computation.1 | async-start | bytes 1835008 | tf_op jit(solution)/shard_map/all_to_all | solution.py:46
  111.4 0.0 all-gather.2.cloned.1.call-start
  111.4 0.2 dynamic-slice_reduce_fusion
  111.6 0.1 iota_compare_fusion.5
  111.7 25.9 %all-to-all-done = bf16[32,8,1792]{2,1,0:T(8,128)(2,1)S(1)} async-done(((bf16[32,8,1792]{2,1,0:T(8,128)(2,1)}), bf16[32,8,1792]{2,1,0:T(8,128)(2,1)S(1)}, u32[]{:S(2)}, u32[]{:S(2)}) %all-to-all-start) | async-done | bytes 917536 | tf_op jit(solution)/shard_map/all_to_all | solution.py:46
  137.5 0.0 copy-done
  137.5 4.1 %fusion.9 = (bf16[32,8,1792]{2,1,0:T(8,128)(2,1)S(1)}, f32[1,32,8,1792]{3,2,1,0:T(8,128)}, f32[1,32,8,1792]{3,2,1,0:T(8,128)}) fusion(f32[1,32,8,1792]{3,2,1,0:T(8,128)S(1)} %copy-done, bf16[32,8,1792]{2,1,0:T(8,128)(2,1)S(1)} %all-to-all-done, pred[32,8]{1,0:T(8,128)(4,1)S(1)} %iota_compare_fusion.5, f32[1,32,8,1792]{3,2,1,0:T(8,128)} %param.6), kind=kLoop, calls=%fused_computation.26 | loop fusion | flops 5046272 | bytes 9175296 | tf_op jit(solution)/shard_map/convert_element_type | solution.py:56
  141.6 29.4 %all_to_all.10 = bf16[32,8,1792]{2,1,0:T(8,128)(2,1)S(1)} all-to-all(bf16[32,8,1792]{2,1,0:T(8,128)(2,1)S(1)} %get-tuple-element.5), channel_id=1, replica_groups=mesh['replica'=8,'fsdp'=32] {'fsdp'}, dimensions={0} | all-to-all | bytes 1835008 | tf_op jit(solution)/shard_map/all_to_all | solution.py:55
  171.1 1.2 convolution_convert_fusion.1
  172.2 0.0 all-gather.2.cloned.1.call-update
  172.3 66.7 %all-gather.2.cloned.1.call-done = bf16[128,14336]{1,0:T(8,128)(2,1)} async-done(((bf16[128,1792]{1,0:T(8,128)(2,1)}), bf16[128,14336]{1,0:T(8,128)(2,1)}) %all-gather.2.cloned.1.call-update) | async-done | bytes 3670032 | tf_op jit(solution)/shard_map/all_gather | solution.py:64
  239.0 4.2 %copy.15 = bf16[128,14336]{1,0:T(8,128)(2,1)} copy(bf16[128,14336]{1,0:T(8,128)(2,1)} %all-gather.2.cloned.1.call-done) | data formatting | bytes 7340032
  (2 shorter events, 0.0 us)
Async XLA Ops:
  7.2 94.2 %reduce-scatter.2.cloned.1.call-start = ((), (), s32[]{:S(2)}) async-start(), calls=%async_computation.3 | async-start | bytes 4128768 | tf_op jit(solution)/shard_map/reduce_scatter | solution.py:31
  7.2 0.7 copy-start.1
  7.2 1.0 copy-start.2
  7.9 129.6 %copy-start = (f32[1,32,8,1792]{3,2,1,0:T(8,128)S(1)}, f32[1,32,8,1792]{3,2,1,0:T(8,128)}, u32[]{:S(2)}) copy-start(f32[1,32,8,1792]{3,2,1,0:T(8,128)} %param.7) | copy-start | bytes 5505028
  103.7 33.8 %all-to-all-start = ((bf16[32,8,1792]{2,1,0:T(8,128)(2,1)}), bf16[32,8,1792]{2,1,0:T(8,128)(2,1)S(1)}, u32[]{:S(2)}, u32[]{:S(2)}) async-start(bf16[32,8,1792]{2,1,0:T(8,128)(2,1)} %fusion), calls=%async_computation.1 | async-start | bytes 1835008 | tf_op jit(solution)/shard_map/all_to_all | solution.py:46
  111.4 127.6 %all-gather.2.cloned.1.call-start = ((), (), s32[]{:S(2)}) async-start(), calls=%async_computation.4 | async-start | bytes 4128768 | tf_op jit(solution)/shard_map/all_gather | solution.py:64
Sparse Core Ops, SparseCore 0:
  12.2 89.0 reduce-scatter.1
  172.4 66.5 all-gather.1

commit v2 on v1

--- a/solution.py
+++ b/solution.py
@@ -1,10 +1,17 @@
+import functools
+
 import jax
 import jax.numpy as jnp
 from jax import lax
+from jax.experimental import pallas as pl
+from jax.experimental.pallas import tpu as pltpu
 from jax.sharding import PartitionSpec as P
 
 outer_rate = 0.7
 momentum_decay = 0.9
+pull = outer_rate * (1.0 + momentum_decay)
+keep = 1.0 - pull
+drag = outer_rate * momentum_decay * momentum_decay
 
 
 def tables(block_lengths, block_owners, owner_count):
@@ -20,6 +27,117 @@
     return counts, starts
 
 
+def split_columns(rows, group_count):
+    row_count, width = rows.shape
+    columns = width // group_count
+
+    def kernel(rows_ref, *refs):
+        outs, sems = refs[:group_count], refs[group_count]
+        me = lax.axis_index("replica")
+        copies = []
+        for k in range(group_count):
+            to = lax.rem(me + k, group_count)
+            copies.append(
+                pltpu.make_async_copy(
+                    rows_ref.at[:, pl.ds(pl.multiple_of(to * columns, 128), columns)],
+                    outs[k],
+                    sems.at[k],
+                )
+            )
+        for copy in copies:
+            copy.start()
+        for copy in copies:
+            copy.wait()
+
+    return pl.pallas_call(
+        kernel,
+        out_shape=[jax.ShapeDtypeStruct((row_count, columns), rows.dtype)] * group_count,
+        in_specs=[pl.BlockSpec(memory_space=pl.ANY)],
+        out_specs=[pl.BlockSpec(memory_space=pl.ANY)] * group_count,
+        scratch_shapes=[pltpu.SemaphoreType.DMA((group_count,))],
+        cost_estimate=pl.CostEstimate(flops=0, bytes_accessed=4 * row_count * width, transcendentals=0),
+        name="split_columns",
+    )(rows)
+
+
+def join_columns(chunks):
+    group_count = len(chunks)
+    row_count, columns = chunks[0].shape
+
+    def kernel(*refs):
+        ins, out, sems = refs[:group_count], refs[group_count], refs[group_count + 1]
+        me = lax.axis_index("replica")
+        copies = []
+        for k in range(group_count):
+            come = lax.rem(me + group_count - k, group_count)
+            copies.append(
+                pltpu.make_async_copy(
+                    ins[k],
+                    out.at[:, pl.ds(pl.multiple_of(come * columns, 128), columns)],
+                    sems.at[k],
+                )
+            )
+        for copy in copies:
+            copy.start()
+        for copy in copies:
+            copy.wait()
+
+    return pl.pallas_call(
+        kernel,
+        out_shape=jax.ShapeDtypeStruct((row_count, group_count * columns), chunks[0].dtype),
+        in_specs=[pl.BlockSpec(memory_space=pl.ANY)] * group_count,
+        out_specs=pl.BlockSpec(memory_space=pl.ANY),
+        scratch_shapes=[pltpu.SemaphoreType.DMA((group_count,))],
+        cost_estimate=pl.CostEstimate(
+            flops=0, bytes_accessed=4 * row_count * columns * group_count, transcendentals=0
+        ),
+        name="join_columns",
+    )(*chunks)
+
+
+def fresh_and_packed(parts, base, pick, group_count):
+    row_count, columns = parts[0].shape
+    slot_count = pick.shape[0]
+    width = 256
+
+    def kernel(*refs):
+        part_refs = refs[: len(parts)]
+        base_ref, pick_ref, rows_ref, slots_ref = refs[len(parts) :]
+        total = part_refs[0][...].astype(jnp.float32)
+        for ref in part_refs[1:]:
+            total = total + ref[...].astype(jnp.float32)
+        own_base = lax.dot_general(
+            pick_ref[...],
+            base_ref[...],
+            (((0,), (0,)), ((), ())),
+            preferred_element_type=jnp.float32,
+        )
+        rows_ref[...] = (own_base + (pull / group_count) * total).astype(rows_ref.dtype)
+        slots_ref[...] = jnp.dot(
+            pick_ref[...], total.astype(pick_ref.dtype), preferred_element_type=jnp.float32
+        ).astype(slots_ref.dtype)
+
+    block = pl.BlockSpec((row_count, width), lambda i: (0, i))
+    slot_block = pl.BlockSpec((slot_count, width), lambda i: (0, i))
+    return pl.pallas_call(
+        kernel,
+        grid=(columns // width,),
+        out_shape=[
+            jax.ShapeDtypeStruct((row_count, columns), jnp.bfloat16),
+            jax.ShapeDtypeStruct((slot_count, columns), jnp.bfloat16),
+        ],
+        in_specs=[block] * len(parts)
+        + [slot_block, pl.BlockSpec((slot_count, row_count), lambda i: (0, 0))],
+        out_specs=[block, slot_block],
+        cost_estimate=pl.CostEstimate(
+            flops=4 * row_count * slot_count * columns,
+            bytes_accessed=2 * columns * (row_count * (len(parts) + 1) + 2 * slot_count),
+            transcendentals=0,
+        ),
+        name="fresh_and_packed",
+    )(*parts, base, pick)
+
+
 def body(local_params, outer_params, outer_momentum, block_lengths, block_owners):
     fsdp_count = lax.axis_size("fsdp")
     group_count = lax.axis_size("replica")
@@ -28,7 +146,19 @@
     row_count = own_rows.shape[0]
     slots = outer_params.shape[2]
     columns = outer_params.shape[3]
-    summed = lax.psum_scatter(own_rows, "replica", scatter_dimension=1, tiled=True)
+    outer_here = outer_params[0]
+    momentum_here = outer_momentum[0]
+
+    def ahead(array, k):
+        return lax.ppermute(
+            array, "replica", [(i, (i + k) % group_count) for i in range(group_count)]
+        )
+
+    chunks = split_columns(own_rows, group_count)
+    parts = [chunks[0]] + [ahead(chunks[k], k) for k in range(1, group_count)]
+
+    base = (keep * outer_here - drag * momentum_here).astype(jnp.bfloat16)
+    own_base = lax.all_to_all(base, "fsdp", split_axis=0, concat_axis=0, tiled=True)
 
     counts, starts = tables(block_lengths, block_owners, fsdp_count)
     slot_ids = jnp.arange(slots, dtype=jnp.int32)
@@ -42,27 +172,19 @@
     ).reshape(-1)
     pick = (row_of_slot[:, None] == row_ids[None, :]).astype(own_rows.dtype)
 
-    packed = jnp.dot(pick, summed, preferred_element_type=jnp.float32).astype(own_rows.dtype)
+    rows, packed = fresh_and_packed(
+        parts, own_base.reshape(fsdp_count * slots, columns), pick, group_count
+    )
+    gathered = [rows] + [ahead(rows, k) for k in range(1, group_count)]
     arrived = lax.all_to_all(
         packed.reshape(fsdp_count, slots, columns), "fsdp", split_axis=0, concat_axis=0, tiled=True
     ).astype(jnp.float32)
-    outer_here = outer_params[0]
     pseudo_grad = jnp.where(
         live_in[:, :, None], outer_here - arrived / group_count, jnp.float32(0.0)
     )
-    fresh_momentum = momentum_decay * outer_momentum[0] + pseudo_grad
+    fresh_momentum = momentum_decay * momentum_here + pseudo_grad
     fresh_outer = outer_here - outer_rate * (pseudo_grad + momentum_decay * fresh_momentum)
-    returned = lax.all_to_all(
-        fresh_outer.astype(jnp.bfloat16), "fsdp", split_axis=0, concat_axis=0, tiled=True
-    )
-    rows = lax.dot_general(
-        pick,
-        returned.reshape(fsdp_count * slots, columns),
-        (((0,), (0,)), ((), ())),
-        preferred_element_type=jnp.float32,
-    ).astype(jnp.bfloat16)
-    fresh_rows = lax.all_gather(rows, "replica", axis=1, tiled=True)
-    return (fresh_outer[None], fresh_momentum[None], fresh_rows)
+    return (fresh_outer[None], fresh_momentum[None], join_columns(gathered))
 
 
 def solution(mesh):

time: 253 us -> 371 us (1.47)
  Pallas kernels: 0 us -> 231 us
  waiting for transfers between devices: 186 us -> 62.2 us
  starting transfers between devices: 7.72 us -> 61 us
  blocking collectives: 29.4 us -> 0 us
  between operations: 14.1 us -> 0.82 us
  other arithmetic: 4.87 us -> 8.8 us
    pallas_call x0 -> x3, Pallas kernels: none -> 231 us  [the longest x1 112 us: split_columns(): pl.pallas_call(kernel, out_shape=[jax.ShapeDtypeStruct((row_count, column...]
    reduce_scatter x1 -> x0, waiting for transfers between devices: 92.4 us -> none  [body(): lax.psum_scatter(own_rows, 'replica', scatter_dimension=1, tiled=True)]
    all_gather x1 -> x0, waiting for transfers between devices: 66.7 us -> none  [body(): fresh_rows = lax.all_gather(rows, 'replica', axis=1, tiled=True)]
    ppermute x0 -> x14, waiting for transfers between devices: none -> 62.2 us  [ahead(): lax.ppermute(array, 'replica', [(i, (i + k) % group_count) for i in range...]
    ppermute x0 -> x14, starting transfers between devices: none -> 43.5 us  [ahead(): lax.ppermute(array, 'replica', [(i, (i + k) % group_count) for i in range...]
    all_to_all x1 -> x0, blocking collectives: 29.4 us -> none  [body(): lax.all_to_all(fresh_outer.astype(jnp.bfloat16), 'fsdp', split_axis=0, co...]
    all_to_all x1, waiting for transfers between devices: 25.9 us -> 0.01 us  [body(): lax.all_to_all(packed.reshape(fsdp_count, slots, columns), 'fsdp', split_...]
    all_to_all x0 -> x1, starting transfers between devices: none -> 9.65 us  [body(): lax.all_to_all(base, 'fsdp', split_axis=0, concat_axis=0, tiled=True)]
  transfers between devices with their start and end apart: 3 -> 16, of which waited for: 3 -> 8; matrix products, arithmetic and copies ran while one was open for 0% -> 1% of each run, Pallas kernels for 0% -> 61%
where the time goes in v2:
time: 371 us; the launch traced here: 366 us
  Pallas kernels  231 us (62%)
  waiting for transfers between devices  62.2 us (17%)
  starting transfers between devices  61 us (16%)
  other arithmetic  8.8 us (2%)
    pallas_call x1, Pallas kernels, split_columns(): pl.pallas_call(kernel, out_shape=[jax.ShapeDtypeStruct((row_count, column...  112 us
    pallas_call x1, Pallas kernels, join_columns(): pl.pallas_call(kernel, out_shape=jax.ShapeDtypeStruct((row_count, group_c...  112 us
    ppermute x14, waiting for transfers between devices, ahead(): lax.ppermute(array, 'replica', [(i, (i + k) % group_count) for i in range...  62.2 us
    ppermute x14, starting transfers between devices, ahead(): lax.ppermute(array, 'replica', [(i, (i + k) % group_count) for i in range...  43.5 us
    all_to_all x1, starting transfers between devices, body(): lax.all_to_all(base, 'fsdp', split_axis=0, concat_axis=0, tiled=True)  9.65 us
    all_to_all x1, starting transfers between devices, body(): lax.all_to_all(packed.reshape(fsdp_count, slots, columns), 'fsdp', split_...  7.83 us
  transfers between devices with their start and end apart: 16, of which 8 were waited for; matrix products, arithmetic and copies ran while one was open for 1% of the time, Pallas kernels for 61%

profile of v2, /device:TPU:40, one launch (start us, length us, event | category | flops | bytes accessed | tf_op | source)
XLA Modules:
  0.0 366.2 jit_solution(1869311109702061466)
XLA Ops:
  0.6 3.2 fusion
  3.9 9.7 %all-to-all-start = ((bf16[32,8,1792]{2,1,0:T(8,128)(2,1)}), bf16[32,8,1792]{2,1,0:T(8,128)(2,1)S(1)}, u32[]{:S(2)}, u32[]{:S(2)}) async-start(bf16[32,8,1792]{2,1,0:T(8,128)(2,1)} %fusion), calls=%async_computation | async-start | bytes 1835008 | tf_op jit(solution)/shard_map/all_to_all | solution.py:161
  13.5 0.0 copy-start.14
  13.5 0.0 copy-start.15
  13.6 112.4 %split_columns.1 = (bf16[128,1792]{1,0:T(8,128)(2,1)}, bf16[128,1792]{1,0:T(8,128)(2,1)}, bf16[128,1792]{1,0:T(8,128)(2,1)}, bf16[128,1792]{1,0:T(8,128)(2,1)}, ...) custom-call(bf16[128,14336]{1,0:T(8,128)(2,1)} %bitcast.40), custom_call_target="tpu_custom_call" | custom-call | bytes 7340032 | tf_op jit(solution)/shard_map/split_columns/pallas_call | solution.py:52
  125.9 2.8 collective-permute-start
  128.7 1.6 collective-permute-start.1
  130.3 1.2 collective-permute-start.2
  131.5 2.6 collective-permute-start.3
  134.1 3.1 collective-permute-start.4
  137.2 0.1 copy.12
  137.3 0.2 multiply_reduce_fusion
  137.4 0.1 copy.13
  137.5 0.5 select_reduce_fusion.1
  138.0 4.1 %collective-permute-done.refs_1_ = bf16[128,1792]{1,0:T(8,128)(2,1)S(1)} collective-permute-done((bf16[128,1792]{1,0:T(8,128)(2,1)}, bf16[128,1792]{1,0:T(8,128)(2,1)S(1)}, u32[]{:S(2)}, u32[]{:S(2)}) %collective-permute-start) | collective-permute-done | bytes 458784 | tf_op jit(solution)/shard_map/ppermute | solution.py:153
  142.1 1.6 collective-permute-start.5
  143.7 17.2 %collective-permute-done.1.refs_2_ = bf16[128,1792]{1,0:T(8,128)(2,1)S(1)} collective-permute-done((bf16[128,1792]{1,0:T(8,128)(2,1)}, bf16[128,1792]{1,0:T(8,128)(2,1)S(1)}, u32[]{:S(2)}, u32[]{:S(2)}) %collective-permute-start.1) | collective-permute-done | bytes 458784 | tf_op jit(solution)/shard_map/ppermute | solution.py:153
  160.9 2.0 collective-permute-start.6
  162.9 0.1 add_select_fusion
  163.0 0.1 select_n.24
  163.1 0.7 fusion.4.refs_9_
  163.8 0.0 collective-permute-done.2.refs_3_
  163.8 2.7 collective-permute-done.3.refs_4_
  166.6 0.0 collective-permute-done.4.refs_5_
  166.6 8.0 %collective-permute-done.5.refs_6_ = bf16[128,1792]{1,0:T(8,128)(2,1)} collective-permute-done((bf16[128,1792]{1,0:T(8,128)(2,1)}, bf16[128,1792]{1,0:T(8,128)(2,1)}, u32[]{:S(2)}, u32[]{:S(2)}) %collective-permute-start.5) | collective-permute-done | bytes 458784 | tf_op jit(solution)/shard_map/ppermute | solution.py:153
  174.6 0.6 collective-permute-done.6.refs_7_
  175.2 0.0 all-to-all-done
  175.3 0.9 copy-done.1
  176.2 6.6 %fresh_and_packed.1 = (bf16[128,1792]{1,0:T(8,128)(2,1)}, bf16[256,1792]{1,0:T(8,128)(2,1)}) custom-call(bf16[128,1792]{1,0:T(8,128)(2,1)} %get-tuple-element.13.refs_0_, bf16[128,1792]{1,0:T(8,128)(2,1)} %copy-done.9, bf16[128,1792]{1,0:T(8,128)(2,1)} %copy-done.10, bf16[128,1792]{1,0:T(8,128)(2,1)} %copy-done.11, bf16[128,1792]{1,0:T(8,128)(2,1)} %copy-done.12, ...), custom_call_target="tpu_custom_call" | custom-call | flops 234881024 | bytes 5963776 | tf_op jit(solution)/shard_map/fresh_and_packed/pallas_call | solution.py:122
  182.8 7.8 %all-to-all-start.1 = ((bf16[32,8,1792]{2,1,0:T(8,128)(2,1)}), bf16[32,8,1792]{2,1,0:T(8,128)(2,1)S(1)}, u32[]{:S(2)}, u32[]{:S(2)}) async-start(bf16[32,8,1792]{2,1,0:T(8,128)(2,1)} %bitcast.42), calls=%async_computation.1 | async-start | bytes 1835008 | tf_op jit(solution)/shard_map/all_to_all | solution.py:179
  190.6 3.3 collective-permute-start.13
  193.9 2.7 collective-permute-start.12
  196.6 5.9 %collective-permute-start.11 = (bf16[128,1792]{1,0:T(8,128)(2,1)S(1)}, bf16[128,1792]{1,0:T(8,128)(2,1)S(1)}, u32[]{:S(2)}, u32[]{:S(2)}) collective-permute-start(bf16[128,1792]{1,0:T(8,128)(2,1)S(1)} %copy-done.2), channel_id=1, source_target_pairs={{0,160},{32,192},{64,224},{96,0},{128,32},{160,64},{192,96},{224,1... | collective-permute-start | bytes 1376264 | tf_op jit(solution)/shard_map/ppermute | solution.py:153
  202.5 3.6 collective-permute-start.9
  206.1 12.6 %collective-permute-done.13.refs_7_ = bf16[128,1792]{1,0:T(8,128)(2,1)S(1)} collective-permute-done((bf16[128,1792]{1,0:T(8,128)(2,1)S(1)}, bf16[128,1792]{1,0:T(8,128)(2,1)S(1)}, u32[]{:S(2)}, u32[]{:S(2)}) %collective-permute-start.13) | collective-permute-done | bytes 458784 | tf_op jit(solution)/shard_map/ppermute | solution.py:153
  218.7 1.1 collective-permute-start.8
  219.7 0.0 collective-permute-done.12.refs_6_
  219.7 12.1 %collective-permute-start.7 = (bf16[128,1792]{1,0:T(8,128)(2,1)S(1)}, bf16[128,1792]{1,0:T(8,128)(2,1)}, u32[]{:S(2)}, u32[]{:S(2)}) collective-permute-start(bf16[128,1792]{1,0:T(8,128)(2,1)S(1)} %copy-done.2), channel_id=1, source_target_pairs={{0,32},{32,64},{64,96},{96,128},{128,160},{160,192},{192,224},{224... | collective-permute-start | bytes 1376264 | tf_op jit(solution)/shard_map/ppermute | solution.py:153
  231.8 0.2 dynamic-slice_reduce_fusion
  232.0 0.1 iota_compare_fusion.3
  232.1 0.0 collective-permute-done.11.refs_5_
  232.1 11.9 %collective-permute-done.10.refs_4_ = bf16[128,1792]{1,0:T(8,128)(2,1)S(1)} collective-permute-done((bf16[128,1792]{1,0:T(8,128)(2,1)S(1)}, bf16[128,1792]{1,0:T(8,128)(2,1)S(1)}, u32[]{:S(2)}, u32[]{:S(2)}) %collective-permute-start.10) | collective-permute-done | bytes 458784 | tf_op jit(solution)/shard_map/ppermute | solution.py:153
  244.0 5.0 %collective-permute-done.8.refs_2_ = bf16[128,1792]{1,0:T(8,128)(2,1)S(1)} collective-permute-done((bf16[128,1792]{1,0:T(8,128)(2,1)S(1)}, bf16[128,1792]{1,0:T(8,128)(2,1)S(1)}, u32[]{:S(2)}, u32[]{:S(2)}) %collective-permute-start.8) | collective-permute-done | bytes 458784 | tf_op jit(solution)/shard_map/ppermute | solution.py:153
  249.0 0.0 copy-start.8
  249.0 0.8 copy-done.8
  249.8 0.0 collective-permute-done.7.refs_1_
  249.8 112.3 %join_columns.1 = bf16[128,14336]{1,0:T(8,128)(2,1)} custom-call(bf16[128,1792]{1,0:T(8,128)(2,1)} %get-tuple-element.22.refs_0_, bf16[128,1792]{1,0:T(8,128)(2,1)} %collective-permute-done.7.refs_1_, bf16[128,1792]{1,0:T(8,128)(2,1)} %copy-done.8, bf16[128,1792]{1,0:T(8,128)(2,1)} %copy-done.7, bf16[128,1792]{1,0:T(8,128)(2,1)} %copy-done.6, ...), custom_call_target="tpu_custom_call" | custom-call | bytes 7340032 | tf_op jit(solution)/shard_map/join_columns/pallas_call | solution.py:85
  362.2 4.0 %fusion.3 = (f32[1,32,8,1792]{3,2,1,0:T(8,128)}, f32[1,32,8,1792]{3,2,1,0:T(8,128)}) fusion(bf16[32,8,1792]{2,1,0:T(8,128)(2,1)S(1)} %all-to-all-done.1, f32[1,32,8,1792]{3,2,1,0:T(8,128)S(1)} %copy-done, f32[1,32,8,1792]{3,2,1,0:T(8,128)} %param.7, pred[32,8]{1,0:T(8,128)(4,1)S(1)} %iota_compare_fusion.3), kind=kLoop, calls=%fused_computation.8 | loop fusion | flops 4587520 | bytes 8257792 | tf_op jit(solution)/shard_map/broadcast_in_dim | solution.py:187
  (32 shorter events, 0.1 us)
Async XLA Ops:
  3.9 171.4 %all-to-all-start = ((bf16[32,8,1792]{2,1,0:T(8,128)(2,1)}), bf16[32,8,1792]{2,1,0:T(8,128)(2,1)S(1)}, u32[]{:S(2)}, u32[]{:S(2)}) async-start(bf16[32,8,1792]{2,1,0:T(8,128)(2,1)} %fusion), calls=%async_computation | async-start | bytes 1835008 | tf_op jit(solution)/shard_map/all_to_all | solution.py:161
  13.5 123.7 %copy-start.14 = (s32[32,24]{0,1:T(8,128)S(1)}, s32[32,24]{0,1:T(8,128)}, u32[]{:S(2)}) copy-start(s32[32,24]{0,1:T(8,128)} %param.8) | copy-start | bytes 9220
  13.5 124.0 %copy-start.15 = (s32[32,32]{1,0:T(8,128)S(1)}, s32[32,32]{1,0:T(8,128)}, u32[]{:S(2)}) copy-start(s32[32,32]{1,0:T(8,128)} %param.9) | copy-start | bytes 12292
  125.9 16.2 %collective-permute-start = (bf16[128,1792]{1,0:T(8,128)(2,1)}, bf16[128,1792]{1,0:T(8,128)(2,1)S(1)}, u32[]{:S(2)}, u32[]{:S(2)}) collective-permute-start(bf16[128,1792]{1,0:T(8,128)(2,1)} %get-tuple-element.14), channel_id=1, source_target_pairs={{0,32},{32,64},{64,96},{96,128},{128,160},{160,192},{192,224},{224... | collective-permute-start | bytes 1376264 | tf_op jit(solution)/shard_map/ppermute | solution.py:153
  128.7 32.2 %collective-permute-start.1 = (bf16[128,1792]{1,0:T(8,128)(2,1)}, bf16[128,1792]{1,0:T(8,128)(2,1)S(1)}, u32[]{:S(2)}, u32[]{:S(2)}) collective-permute-start(bf16[128,1792]{1,0:T(8,128)(2,1)} %get-tuple-element.15), channel_id=1, source_target_pairs={{0,64},{32,96},{64,128},{96,160},{128,192},{160,224},{192,0},{224,... | collective-permute-start | bytes 1376264 | tf_op jit(solution)/shard_map/ppermute | solution.py:153
  130.3 33.5 %collective-permute-start.2 = (bf16[128,1792]{1,0:T(8,128)(2,1)}, bf16[128,1792]{1,0:T(8,128)(2,1)S(1)}, u32[]{:S(2)}, u32[]{:S(2)}) collective-permute-start(bf16[128,1792]{1,0:T(8,128)(2,1)} %get-tuple-element.16), channel_id=1, source_target_pairs={{0,96},{32,128},{64,160},{96,192},{128,224},{160,0},{192,32},{224,... | collective-permute-start | bytes 1376264 | tf_op jit(solution)/shard_map/ppermute | solution.py:153
  131.5 35.1 %collective-permute-start.3 = (bf16[128,1792]{1,0:T(8,128)(2,1)}, bf16[128,1792]{1,0:T(8,128)(2,1)S(1)}, u32[]{:S(2)}, u32[]{:S(2)}) collective-permute-start(bf16[128,1792]{1,0:T(8,128)(2,1)} %get-tuple-element.17), channel_id=1, source_target_pairs={{0,128},{32,160},{64,192},{96,224},{128,0},{160,32},{192,64},{224,... | collective-permute-start | bytes 1376264 | tf_op jit(solution)/shard_map/ppermute | solution.py:153
  134.1 32.5 %collective-permute-start.4 = (bf16[128,1792]{1,0:T(8,128)(2,1)}, bf16[128,1792]{1,0:T(8,128)(2,1)S(1)}, u32[]{:S(2)}, u32[]{:S(2)}) collective-permute-start(bf16[128,1792]{1,0:T(8,128)(2,1)} %get-tuple-element.18), channel_id=1, source_target_pairs={{0,160},{32,192},{64,224},{96,0},{128,32},{160,64},{192,96},{224,1... | collective-permute-start | bytes 1376264 | tf_op jit(solution)/shard_map/ppermute | solution.py:153
  142.1 33.1 %copy-start.9 = (bf16[128,1792]{1,0:T(8,128)(2,1)}, bf16[128,1792]{1,0:T(8,128)(2,1)S(1)}, u32[]{:S(2)}) copy-start(bf16[128,1792]{1,0:T(8,128)(2,1)S(1)} %collective-permute-done.refs_1_) | copy-start | bytes 1376260
  142.1 32.5 %collective-permute-start.5 = (bf16[128,1792]{1,0:T(8,128)(2,1)}, bf16[128,1792]{1,0:T(8,128)(2,1)}, u32[]{:S(2)}, u32[]{:S(2)}) collective-permute-start(bf16[128,1792]{1,0:T(8,128)(2,1)} %get-tuple-element.19), channel_id=1, source_target_pairs={{0,192},{32,224},{64,0},{96,32},{128,64},{160,96},{192,128},{224,1... | collective-permute-start | bytes 1376264 | tf_op jit(solution)/shard_map/ppermute | solution.py:153
  160.9 14.3 %copy-start.10 = (bf16[128,1792]{1,0:T(8,128)(2,1)}, bf16[128,1792]{1,0:T(8,128)(2,1)S(1)}, u32[]{:S(2)}) copy-start(bf16[128,1792]{1,0:T(8,128)(2,1)S(1)} %collective-permute-done.1.refs_2_) | copy-start | bytes 1376260
  160.9 14.3 %collective-permute-start.6 = (bf16[128,1792]{1,0:T(8,128)(2,1)}, bf16[128,1792]{1,0:T(8,128)(2,1)}, u32[]{:S(2)}, u32[]{:S(2)}) collective-permute-start(bf16[128,1792]{1,0:T(8,128)(2,1)} %get-tuple-element.20), channel_id=1, source_target_pairs={{0,224},{32,0},{64,32},{96,64},{128,96},{160,128},{192,160},{224,1... | collective-permute-start | bytes 1376264 | tf_op jit(solution)/shard_map/ppermute | solution.py:153
  163.8 11.4 %copy-start.11 = (bf16[128,1792]{1,0:T(8,128)(2,1)}, bf16[128,1792]{1,0:T(8,128)(2,1)S(1)}, u32[]{:S(2)}) copy-start(bf16[128,1792]{1,0:T(8,128)(2,1)S(1)} %collective-permute-done.2.refs_3_) | copy-start | bytes 1376260
  166.6 8.7 %copy-start.12 = (bf16[128,1792]{1,0:T(8,128)(2,1)}, bf16[128,1792]{1,0:T(8,128)(2,1)S(1)}, u32[]{:S(2)}) copy-start(bf16[128,1792]{1,0:T(8,128)(2,1)S(1)} %collective-permute-done.3.refs_4_) | copy-start | bytes 1376260
  166.6 8.7 %copy-start.13 = (bf16[128,1792]{1,0:T(8,128)(2,1)}, bf16[128,1792]{1,0:T(8,128)(2,1)S(1)}, u32[]{:S(2)}) copy-start(bf16[128,1792]{1,0:T(8,128)(2,1)S(1)} %collective-permute-done.4.refs_5_) | copy-start | bytes 1376260
  175.2 0.9 copy-start.1
  182.7 7.8 %copy-start.2 = (bf16[128,1792]{1,0:T(8,128)(2,1)S(1)}, bf16[128,1792]{1,0:T(8,128)(2,1)}, u32[]{:S(2)}) copy-start(bf16[128,1792]{1,0:T(8,128)(2,1)} %get-tuple-element.22.refs_0_) | copy-start | bytes 1376260
  182.8 179.4 %all-to-all-start.1 = ((bf16[32,8,1792]{2,1,0:T(8,128)(2,1)}), bf16[32,8,1792]{2,1,0:T(8,128)(2,1)S(1)}, u32[]{:S(2)}, u32[]{:S(2)}) async-start(bf16[32,8,1792]{2,1,0:T(8,128)(2,1)} %bitcast.42), calls=%async_computation.1 | async-start | bytes 1835008 | tf_op jit(solution)/shard_map/all_to_all | solution.py:179
  190.6 28.1 %collective-permute-start.13 = (bf16[128,1792]{1,0:T(8,128)(2,1)S(1)}, bf16[128,1792]{1,0:T(8,128)(2,1)S(1)}, u32[]{:S(2)}, u32[]{:S(2)}) collective-permute-start(bf16[128,1792]{1,0:T(8,128)(2,1)S(1)} %copy-done.2), channel_id=1, source_target_pairs={{0,224},{32,0},{64,32},{96,64},{128,96},{160,128},{192,160},{224,1... | collective-permute-start | bytes 1376264 | tf_op jit(solution)/shard_map/ppermute | solution.py:153
  193.9 25.8 %collective-permute-start.12 = (bf16[128,1792]{1,0:T(8,128)(2,1)S(1)}, bf16[128,1792]{1,0:T(8,128)(2,1)S(1)}, u32[]{:S(2)}, u32[]{:S(2)}) collective-permute-start(bf16[128,1792]{1,0:T(8,128)(2,1)S(1)} %copy-done.2), channel_id=1, source_target_pairs={{0,192},{32,224},{64,0},{96,32},{128,64},{160,96},{192,128},{224,1... | collective-permute-start | bytes 1376264 | tf_op jit(solution)/shard_map/ppermute | solution.py:153
  196.6 35.5 %collective-permute-start.11 = (bf16[128,1792]{1,0:T(8,128)(2,1)S(1)}, bf16[128,1792]{1,0:T(8,128)(2,1)S(1)}, u32[]{:S(2)}, u32[]{:S(2)}) collective-permute-start(bf16[128,1792]{1,0:T(8,128)(2,1)S(1)} %copy-done.2), channel_id=1, source_target_pairs={{0,160},{32,192},{64,224},{96,0},{128,32},{160,64},{192,96},{224,1... | collective-permute-start | bytes 1376264 | tf_op jit(solution)/shard_map/ppermute | solution.py:153
  202.5 41.5 %collective-permute-start.10 = (bf16[128,1792]{1,0:T(8,128)(2,1)S(1)}, bf16[128,1792]{1,0:T(8,128)(2,1)S(1)}, u32[]{:S(2)}, u32[]{:S(2)}) collective-permute-start(bf16[128,1792]{1,0:T(8,128)(2,1)S(1)} %copy-done.2), channel_id=1, source_target_pairs={{0,128},{32,160},{64,192},{96,224},{128,0},{160,32},{192,64},{224,... | collective-permute-start | bytes 1376264 | tf_op jit(solution)/shard_map/ppermute | solution.py:153
  202.5 41.5 %collective-permute-start.9 = (bf16[128,1792]{1,0:T(8,128)(2,1)S(1)}, bf16[128,1792]{1,0:T(8,128)(2,1)S(1)}, u32[]{:S(2)}, u32[]{:S(2)}) collective-permute-start(bf16[128,1792]{1,0:T(8,128)(2,1)S(1)} %copy-done.2), channel_id=1, source_target_pairs={{0,96},{32,128},{64,160},{96,192},{128,224},{160,0},{192,32},{224,... | collective-permute-start | bytes 1376264 | tf_op jit(solution)/shard_map/ppermute | solution.py:153
  218.7 13.4 %copy-start.3 = (bf16[128,1792]{1,0:T(8,128)(2,1)}, bf16[128,1792]{1,0:T(8,128)(2,1)S(1)}, u32[]{:S(2)}) copy-start(bf16[128,1792]{1,0:T(8,128)(2,1)S(1)} %collective-permute-done.13.refs_7_) | copy-start | bytes 1376260
  218.7 30.4 %collective-permute-start.8 = (bf16[128,1792]{1,0:T(8,128)(2,1)S(1)}, bf16[128,1792]{1,0:T(8,128)(2,1)S(1)}, u32[]{:S(2)}, u32[]{:S(2)}) collective-permute-start(bf16[128,1792]{1,0:T(8,128)(2,1)S(1)} %copy-done.2), channel_id=1, source_target_pairs={{0,64},{32,96},{64,128},{96,160},{128,192},{160,224},{192,0},{224,... | collective-permute-start | bytes 1376264 | tf_op jit(solution)/shard_map/ppermute | solution.py:153
  219.7 12.3 %copy-start.4 = (bf16[128,1792]{1,0:T(8,128)(2,1)}, bf16[128,1792]{1,0:T(8,128)(2,1)S(1)}, u32[]{:S(2)}) copy-start(bf16[128,1792]{1,0:T(8,128)(2,1)S(1)} %collective-permute-done.12.refs_6_) | copy-start | bytes 1376260
  219.7 30.1 %collective-permute-start.7 = (bf16[128,1792]{1,0:T(8,128)(2,1)S(1)}, bf16[128,1792]{1,0:T(8,128)(2,1)}, u32[]{:S(2)}, u32[]{:S(2)}) collective-permute-start(bf16[128,1792]{1,0:T(8,128)(2,1)S(1)} %copy-done.2), channel_id=1, source_target_pairs={{0,32},{32,64},{64,96},{96,128},{128,160},{160,192},{192,224},{224... | collective-permute-start | bytes 1376264 | tf_op jit(solution)/shard_map/ppermute | solution.py:153
  232.1 130.1 %copy-start = (f32[1,32,8,1792]{3,2,1,0:T(8,128)S(1)}, f32[1,32,8,1792]{3,2,1,0:T(8,128)}, u32[]{:S(2)}) copy-start(f32[1,32,8,1792]{3,2,1,0:T(8,128)} %param.6) | copy-start | bytes 5505028
  232.1 16.9 %copy-start.5 = (bf16[128,1792]{1,0:T(8,128)(2,1)}, bf16[128,1792]{1,0:T(8,128)(2,1)S(1)}, u32[]{:S(2)}) copy-start(bf16[128,1792]{1,0:T(8,128)(2,1)S(1)} %collective-permute-done.11.refs_5_) | copy-start | bytes 1376260
  244.0 5.0 %copy-start.6 = (bf16[128,1792]{1,0:T(8,128)(2,1)}, bf16[128,1792]{1,0:T(8,128)(2,1)S(1)}, u32[]{:S(2)}) copy-start(bf16[128,1792]{1,0:T(8,128)(2,1)S(1)} %collective-permute-done.10.refs_4_) | copy-start | bytes 1376260
  244.0 5.0 %copy-start.7 = (bf16[128,1792]{1,0:T(8,128)(2,1)}, bf16[128,1792]{1,0:T(8,128)(2,1)S(1)}, u32[]{:S(2)}) copy-start(bf16[128,1792]{1,0:T(8,128)(2,1)S(1)} %collective-permute-done.9.refs_3_) | copy-start | bytes 1376260
  249.0 0.8 copy-start.8

commit v3 on v2

v3 whole, which is shorter than its diff:
```python
import jax
import jax.numpy as jnp
from jax import lax
from jax.experimental import pallas as pl
from jax.experimental.pallas import tpu as pltpu
from jax.sharding import PartitionSpec as P

outer_rate = 0.7
momentum_decay = 0.9
PACE = 1150000000000
pull = outer_rate * (1.0 + momentum_decay)
keep = 1.0 - pull
drag = outer_rate * momentum_decay * momentum_decay

STEPS = [(0, 0), (1, 0), (3, 0), (2, 0), (0, 1), (1, 1), (3, 1), (2, 1)]


def place(me, step):
    y, x = me // 2, me % 2
    return ((y + step[0]) % 4) * 2 + (x + step[1]) % 2


def place_traced(me, step):
    y, x = lax.div(me, 2), lax.rem(me, 2)
    return lax.rem(y + step[0], 4) * 2 + lax.rem(x + step[1], 2)


def send(array, step):
    return lax.ppermute(array, "replica", [(i, place(i, step)) for i in range(8)])


def tables(block_lengths, block_owners, owner_count):
    block_count = block_lengths.shape[1]
    block_ids = jnp.arange(block_count, dtype=jnp.int32)
    before = (block_ids[None, :] < block_ids[:, None]).astype(jnp.int32)
    offsets = jnp.sum(before[None] * block_lengths[:, None, :], axis=2)
    heads = block_owners[:, :block_count]
    owner_ids = jnp.arange(owner_count, dtype=jnp.int32)
    match = (heads[:, :, None] == owner_ids[None, None, :]).astype(jnp.int32)
    counts = jnp.sum(match * block_lengths[:, :, None], axis=1)
    starts = jnp.sum(match * offsets[:, :, None], axis=1)
    return counts, starts


def split_columns(rows):
    row_count, width = rows.shape
    parts = len(STEPS)
    columns = width // parts

    def kernel(rows_ref, *refs):
        outs, sems = refs[:parts], refs[parts]
        me = lax.axis_index("replica")
        copies = []
        for k, step in enumerate(STEPS):
            to = place_traced(me, step)
            copies.append(
                pltpu.make_async_copy(
                    rows_ref.at[:, pl.ds(pl.multiple_of(to * columns, 128), columns)],
                    outs[k],
                    sems.at[k],
                )
            )
        for copy in copies:
            copy.start()
        for copy in copies:
            copy.wait()

    chunks = pl.pallas_call(
        kernel,
        out_shape=[jax.ShapeDtypeStruct((row_count, columns), rows.dtype)] * parts,
        in_specs=[pl.BlockSpec(memory_space=pltpu.HBM)],
        out_specs=[pl.BlockSpec(memory_space=pltpu.VMEM)] * parts,
        scratch_shapes=[pltpu.SemaphoreType.DMA((parts,))],
        cost_estimate=pl.CostEstimate(
            flops=0, bytes_accessed=4 * row_count * width, transcendentals=0
        ),
        compiler_params=pltpu.CompilerParams(vmem_limit_bytes=8 * 1024 * 1024),
        name="split_columns",
    )(pltpu.with_memory_space_constraint(rows, pltpu.HBM))
    return dict(zip(STEPS, chunks))


def finish(chunks, arrived, outer, momentum, live, scale):
    parts = len(STEPS)
    row_count, columns = chunks[STEPS[0]].shape
    slot_count = arrived.shape[0]
    steps = 4
    block_rows = slot_count // steps

    def kernel(*refs):
        ins = refs[:parts]
        arrived_ref, outer_ref, momentum_ref, live_ref = refs[parts : parts + 4]
        new_outer_ref, new_momentum_ref, joined_ref, sems = refs[parts + 4 :]
        i = pl.program_id(0)
        me = lax.axis_index("replica")
        copies = []
        for k, step in enumerate(STEPS):
            come = place_traced(me, step)
            copies.append(
                pltpu.make_async_copy(
                    ins[k],
                    joined_ref.at[:, pl.ds(pl.multiple_of(come * columns, 128), columns)],
                    sems.at[k],
                )
            )

        @pl.when(i == 0)
        def _():
            for copy in copies:
                copy.start()

        at = pl.ds(pl.multiple_of(i * block_rows, block_rows), block_rows)
        alive = live_ref[at, :] > 0.0
        for start in range(0, columns, 128):
            cols = pl.ds(start, 128)
            mean = arrived_ref[at, cols].astype(jnp.float32) * scale
            old = outer_ref[at, cols]
            pseudo_grad = jnp.where(alive, old - mean, 0.0)
            fresh = momentum_decay * momentum_ref[at, cols] + pseudo_grad
            new_momentum_ref[:, cols] = fresh
            new_outer_ref[:, cols] = old - outer_rate * (pseudo_grad + momentum_decay * fresh)

        @pl.when(i == steps - 1)
        def _():
            for copy in copies:
                copy.wait()

    whole = pl.BlockSpec(memory_space=pltpu.VMEM)
    block = pl.BlockSpec((block_rows, columns), lambda i: (i, 0))
    return pl.pallas_call(
        kernel,
        grid=(steps,),
        out_shape=[jax.ShapeDtypeStruct((slot_count, columns), jnp.float32)] * 2
        + [jax.ShapeDtypeStruct((row_count, parts * columns), jnp.bfloat16)],
        in_specs=[whole] * (parts + 4),
        out_specs=[block, block, pl.BlockSpec(memory_space=pltpu.HBM)],
        scratch_shapes=[pltpu.SemaphoreType.DMA((parts,))],
        cost_estimate=pl.CostEstimate(
            flops=10 * slot_count * columns,
            bytes_accessed=4 * row_count * columns * parts + 18 * slot_count * columns,
            transcendentals=0,
        ),
        compiler_params=pltpu.CompilerParams(vmem_limit_bytes=14 * 1024 * 1024),
        name="finish",
    )(*[chunks[step] for step in STEPS], arrived, outer, momentum, live)


def fresh_rows(parts, base, unpick, pick, scale):
    row_count, columns = parts[0].shape
    slot_count = base.shape[0]
    width = 256

    def kernel(*refs):
        part_refs = refs[: len(parts)]
        base_ref, unpick_ref, pick_ref, rows_ref, slots_ref = refs[len(parts) :]
        for start in range(0, columns, width):
            at = (slice(None), pl.ds(start, width))
            total = part_refs[0][at].astype(jnp.float32)
            for ref in part_refs[1:]:
                total = total + ref[at].astype(jnp.float32)
            share = jnp.dot(unpick_ref[...], base_ref[at], preferred_element_type=jnp.float32)
            rows_ref[at] = (share + scale * total).astype(rows_ref.dtype)
            slots_ref[at] = jnp.dot(
                pick_ref[...], total.astype(jnp.bfloat16), preferred_element_type=jnp.float32
            ).astype(slots_ref.dtype)

    return pl.pallas_call(
        kernel,
        out_shape=[
            jax.ShapeDtypeStruct((row_count, columns), jnp.bfloat16),
            jax.ShapeDtypeStruct((slot_count, columns), jnp.bfloat16),
        ],
        in_specs=[pl.BlockSpec(memory_space=pltpu.VMEM)] * (len(parts) + 3),
        out_specs=[pl.BlockSpec(memory_space=pltpu.VMEM)] * 2,
        cost_estimate=pl.CostEstimate(
            flops=4 * row_count * slot_count * columns,
            bytes_accessed=2 * columns * (row_count * (len(parts) + 1) + 2 * slot_count),
            transcendentals=0,
        ),
        compiler_params=pltpu.CompilerParams(vmem_limit_bytes=8 * 1024 * 1024),
        name="fresh_rows",
    )(*parts, base, unpick, pick)


def partial_sums(*sums):
    row_count, columns = sums[0][0].shape
    width = 256

    def kernel(*refs):
        ins, outs = refs[: -len(sums)], refs[-len(sums) :]
        first = 0
        for terms, out in zip(sums, outs):
            term_refs = ins[first : first + len(terms)]
            first += len(terms)
            for start in range(0, columns, width):
                at = (slice(None), pl.ds(start, width))
                total = term_refs[0][at].astype(jnp.float32)
                for ref in term_refs[1:]:
                    total = total + ref[at].astype(jnp.float32)
                out[at] = total.astype(out.dtype)

    terms = [term for group in sums for term in group]
    return pl.pallas_call(
        kernel,
        out_shape=[jax.ShapeDtypeStruct((row_count, columns), jnp.bfloat16)] * len(sums),
        in_specs=[pl.BlockSpec(memory_space=pltpu.VMEM)] * len(terms),
        out_specs=[pl.BlockSpec(memory_space=pltpu.VMEM)] * len(sums),
        cost_estimate=pl.CostEstimate(
            flops=PACE,
            bytes_accessed=2 * columns * row_count * (len(terms) + len(sums)),
            transcendentals=0,
        ),
        compiler_params=pltpu.CompilerParams(vmem_limit_bytes=8 * 1024 * 1024),
        name="partial_sums",
    )(*terms)


def gate(*arrays):
    def kernel(*refs):
        pass

    return pl.pallas_call(
        kernel,
        out_shape=[jax.ShapeDtypeStruct(array.shape, array.dtype) for array in arrays],
        in_specs=[pl.BlockSpec(memory_space=pl.ANY)] * len(arrays),
        out_specs=[pl.BlockSpec(memory_space=pl.ANY)] * len(arrays),
        input_output_aliases={i: i for i in range(len(arrays))},
        cost_estimate=pl.CostEstimate(flops=PACE, bytes_accessed=0, transcendentals=0),
        compiler_params=pltpu.CompilerParams(vmem_limit_bytes=1024 * 1024),
        name="gate",
    )(*arrays)


def sum_over_replica(rows):
    own = split_columns(rows)
    up_far = send(own[1, 1], (1, 0))
    down_far = send(own[3, 1], (3, 0))
    across = send(own[2, 1], (0, 1))
    up = send(own[1, 0], (1, 0))
    down = send(own[3, 0], (3, 0))
    for_twice, for_beside = partial_sums((own[2, 0], across), (own[0, 1], up_far, down_far))
    twice = send(for_twice, (2, 0))
    beside = send(for_beside, (0, 1))
    return (own[0, 0], up, down, twice, beside), for_beside


def gather_over_replica(rows):
    got = {(0, 0): rows}
    got[0, 1] = send(rows, (0, 1))
    got[2, 0] = send(rows, (2, 0))
    got[3, 0] = send(rows, (1, 0))
    got[1, 0] = send(rows, (3, 0))
    near, far = got[0, 1], got[2, 0] = gate(got[0, 1], got[2, 0])
    got[3, 1] = send(near, (1, 0))
    got[1, 1] = send(near, (3, 0))
    got[2, 1] = send(far, (0, 1))
    return got


def body(local_params, outer_params, outer_momentum, block_lengths, block_owners):
    fsdp_count = lax.axis_size("fsdp")
    group_count = lax.axis_size("replica")
    my_index = lax.axis_index("fsdp")
    own_rows = local_params[0]
    row_count = own_rows.shape[0]
    slots = outer_params.shape[2]
    columns = outer_params.shape[3]
    outer_here = outer_params[0]
    momentum_here = outer_momentum[0]

    parts, halfway = sum_over_replica(own_rows)

    base = (keep * outer_here - drag * momentum_here).astype(jnp.bfloat16)
    own_base = lax.all_to_all(base, "fsdp", split_axis=0, concat_axis=0, tiled=True)

    block_lengths, _ = lax.optimization_barrier((block_lengths, halfway))
    counts, starts = tables(block_lengths, block_owners, fsdp_count)
    slot_ids = jnp.arange(slots, dtype=jnp.int32)
    row_ids = jnp.arange(row_count, dtype=jnp.int32)
    my_starts = lax.dynamic_index_in_dim(starts, my_index, 0, keepdims=False)
    my_counts = lax.dynamic_index_in_dim(counts, my_index, 0, keepdims=False)
    incoming = lax.dynamic_index_in_dim(counts, my_index, 1, keepdims=False)
    live_in = (slot_ids[None, :] < incoming[:, None]).astype(jnp.float32).reshape(-1, 1)
    live_in = jnp.broadcast_to(live_in, (fsdp_count * slots, 128))
    row_of_slot = jnp.where(
        slot_ids[None, :] < my_counts[:, None], my_starts[:, None] + slot_ids[None, :], -1
    ).reshape(-1)
    pick = (row_of_slot[:, None] == row_ids[None, :]).astype(own_rows.dtype)
    unpick = (row_ids[:, None] == row_of_slot[None, :]).astype(own_rows.dtype)
    rows, packed = fresh_rows(
        parts, own_base.reshape(fsdp_count * slots, columns), unpick, pick, pull / group_count
    )
    gathered = gather_over_replica(rows)
    arrived = lax.all_to_all(
        packed.reshape(fsdp_count, slots, columns), "fsdp", split_axis=0, concat_axis=0, tiled=True
    )
    flat = (fsdp_count * slots, columns)
    fresh_outer, fresh_momentum, joined = finish(
        gathered,
        arrived.reshape(flat),
        outer_here.reshape(flat),
        momentum_here.reshape(flat),
        live_in,
        1.0 / group_count,
    )
    return (
        fresh_outer.reshape(outer_params.shape),
        fresh_momentum.reshape(outer_params.shape),
        joined,
    )


def solution(mesh):
    in_specs = (
        P("replica", "fsdp", None),
        P("fsdp", None, None, "replica"),
        P("fsdp", None, None, "replica"),
        P(),
        P(),
    )
    out_specs = (
        P("fsdp", None, None, "replica"),
        P("fsdp", None, None, "replica"),
        P("fsdp", None),
    )
    return jax.shard_map(body, mesh=mesh, in_specs=in_specs, out_specs=out_specs, check_vma=False)
```

time: 371 us -> 96.4 us (0.26)
  Pallas kernels: 231 us -> 13.7 us
  waiting for transfers between devices: 62.2 us -> 37.5 us
  starting transfers between devices: 61 us -> 37.4 us
  other arithmetic: 8.8 us -> 2.68 us
    pallas_call x1, Pallas kernels: 112 us -> 3.33 us  [split_columns(): pl.pallas_call(kernel, out_shape=[jax.ShapeDtypeStruct((row_count, column...]
    pallas_call x2 -> x4, Pallas kernels: 119 us -> 10.4 us  [the longest x1 5.45 us: finish(): pl.pallas_call(kernel, grid=(steps,), out_shape=[jax.ShapeDtypeStruct((sl...]
    ppermute x14, waiting for transfers between devices: 62.2 us -> 32.3 us  [send(): lax.ppermute(array, 'replica', [(i, place(i, step)) for i in range(8)])]
    ppermute x14, starting transfers between devices: 43.5 us -> 21.9 us  [send(): lax.ppermute(array, 'replica', [(i, place(i, step)) for i in range(8)])]
    broadcast_in_dim x1 -> x0, other arithmetic: 4.04 us -> none  [body(): return (fresh_outer[None], fresh_momentum[None], join_columns(gathered))]
  transfers between devices with their start and end apart: 16 -> 16, of which waited for: 8 -> 9; matrix products, arithmetic and copies ran while one was open for 1% -> 3% of each run, Pallas kernels for 61% -> 2%
where the time goes in v3:
time: 96.4 us; the launch traced here: 94.7 us
  waiting for transfers between devices  37.5 us (39%)
  starting transfers between devices  37.4 us (39%)
  Pallas kernels  13.7 us (14%)
  other arithmetic  2.68 us (3%)
  local copies, waits for them, and re-layouts  2.63 us (3%)
    ppermute x14, waiting for transfers between devices, send(): lax.ppermute(array, 'replica', [(i, place(i, step)) for i in range(8)])  32.3 us
    ppermute x14, starting transfers between devices, send(): lax.ppermute(array, 'replica', [(i, place(i, step)) for i in range(8)])  21.9 us
    all_to_all x1, starting transfers between devices, body(): lax.all_to_all(base, 'fsdp', split_axis=0, concat_axis=0, tiled=True)  8.81 us
    all_to_all x1, starting transfers between devices, body(): lax.all_to_all(packed.reshape(fsdp_count, slots, columns), 'fsdp', split_...  6.69 us
    pallas_call x1, Pallas kernels, finish(): pl.pallas_call(kernel, grid=(steps,), out_shape=[jax.ShapeDtypeStruct((sl...  5.45 us
    all_to_all x1, waiting for transfers between devices, body(): lax.all_to_all(packed.reshape(fsdp_count, slots, columns), 'fsdp', split_...  3.6 us
    pallas_call x1, Pallas kernels, split_columns(): pl.pallas_call(kernel, out_shape=[jax.ShapeDtypeStruct((row_count, column...  3.33 us
    pallas_call x1, Pallas kernels, fresh_rows(): pl.pallas_call(kernel, out_shape=[jax.ShapeDtypeStruct((row_count, column...  3.03 us
  transfers between devices with their start and end apart: 16, of which 9 were waited for; matrix products, arithmetic and copies ran while one was open for 3% of the time, Pallas kernels for 2%

profile of v3, /device:TPU:40, one launch (start us, length us, event | category | flops | bytes accessed | tf_op | source)
XLA Modules:
  0.0 94.7 jit_solution(9195763858147019566)
XLA Ops:
  0.6 0.0 copy-start
  0.6 0.0 copy-start.2
  0.7 3.3 %split_columns.1 = (bf16[128,1792]{1,0:T(8,128)(2,1)S(1)}, bf16[128,1792]{1,0:T(8,128)(2,1)}, bf16[128,1792]{1,0:T(8,128)(2,1)}, bf16[128,1792]{1,0:T(8,128)(2,1...) custom-call(bf16[128,14336]{1,0:T(8,128)(2,1)} %bitcast.17), custom_call_target="tpu_custom_call" | custom-call | bytes 7340032 | tf_op jit(solution)/shard_map/split_columns/pallas_call | solution.py:68
  4.0 3.1 %collective-permute-start.2 = (bf16[128,1792]{1,0:T(8,128)(2,1)}, bf16[128,1792]{1,0:T(8,128)(2,1)S(1)}, u32[]{:S(2)}, u32[]{:S(2)}) collective-permute-start(bf16[128,1792]{1,0:T(8,128)(2,1)} %get-tuple-element.25), channel_id=1, source_target_pairs={{0,32},{32,0},{64,96},{96,64},{128,160},{160,128},{192,224},{224,1... | collective-permute-start | bytes 1376264 | tf_op jit(solution)/shard_map/ppermute | solution.py:29
  7.1 1.6 %collective-permute-start.3 = (bf16[128,1792]{1,0:T(8,128)(2,1)S(1)}, bf16[128,1792]{1,0:T(8,128)(2,1)S(1)}, u32[]{:S(2)}, u32[]{:S(2)}) collective-permute-start(bf16[128,1792]{1,0:T(8,128)(2,1)S(1)} %get-tuple-element.27), channel_id=1, source_target_pairs={{0,64},{32,96},{64,128},{96,160},{128,192},{160,224},{192,0},{224,... | collective-permute-start | bytes 1376264 | tf_op jit(solution)/shard_map/ppermute | solution.py:29
  8.7 0.4 collective-permute-start.4
  9.1 1.2 %fusion = bf16[32,8,1792]{2,1,0:T(8,128)(2,1)} fusion(f32[1,32,8,1792]{3,2,1,0:T(8,128)S(1)} %copy-done, f32[1,32,8,1792]{3,2,1,0:T(8,128)S(1)} %copy-done.2), kind=kLoop, calls=%fused_computation.1 | loop fusion | flops 1835008 | bytes 4587520 | tf_op jit(solution)/shard_map/convert_element_type | solution.py:273
  10.3 8.8 %all-to-all-start = ((bf16[32,8,1792]{2,1,0:T(8,128)(2,1)}), bf16[32,8,1792]{2,1,0:T(8,128)(2,1)}, u32[]{:S(2)}, u32[]{:S(2)}) async-start(bf16[32,8,1792]{2,1,0:T(8,128)(2,1)} %fusion), calls=%async_computation | async-start | bytes 1835008 | tf_op jit(solution)/shard_map/all_to_all | solution.py:274
  19.1 1.7 %collective-permute-start = (bf16[128,1792]{1,0:T(8,128)(2,1)}, bf16[128,1792]{1,0:T(8,128)(2,1)}, u32[]{:S(2)}, u32[]{:S(2)}) collective-permute-start(bf16[128,1792]{1,0:T(8,128)(2,1)} %get-tuple-element.22), channel_id=1, source_target_pairs={{0,64},{32,96},{64,128},{96,160},{128,192},{160,224},{192,0},{224,... | collective-permute-start | bytes 1376264 | tf_op jit(solution)/shard_map/ppermute | solution.py:29
  20.8 0.5 collective-permute-start.1
  21.2 0.6 fusion.4
  21.9 0.0 copy-start.6
  21.9 0.0 copy-start.8
  21.9 1.9 %partial_sums.1 = (bf16[128,1792]{1,0:T(8,128)(2,1)}, bf16[128,1792]{1,0:T(8,128)(2,1)S(1)}) custom-call(bf16[128,1792]{1,0:T(8,128)(2,1)S(1)} %get-tuple-element.24.refs_0_, bf16[128,1792]{1,0:T(8,128)(2,1)S(1)} %collective-permute-done.2.refs_1_, bf16[128,1792]{1,0:T(8,128)(2,1)S(1)} %get-tuple-element.26.refs_2_, ...), custom_call_target="tpu_custom_call" | custom-call | flops 1150000037888 | bytes 3211264 | tf_op jit(solution)/shard_map/partial_sums/pallas_call | solution.py:203
  23.8 2.0 %collective-permute-start.6 = (bf16[128,1792]{1,0:T(8,128)(2,1)S(1)}, bf16[128,1792]{1,0:T(8,128)(2,1)S(1)}, u32[]{:S(2)}, u32[]{:S(2)}) collective-permute-start(bf16[128,1792]{1,0:T(8,128)(2,1)S(1)} %get-tuple-element.30), channel_id=1, source_target_pairs={{0,32},{32,0},{64,96},{96,64},{128,160},{160,128},{192,224},{224,1... | collective-permute-start | bytes 1376264 | tf_op jit(solution)/shard_map/ppermute | solution.py:29
  25.8 0.1 copy.16
  25.9 0.2 multiply_reduce_fusion
  26.1 0.1 copy.17
  26.1 2.3 %collective-permute-start.5 = (bf16[128,1792]{1,0:T(8,128)(2,1)}, bf16[128,1792]{1,0:T(8,128)(2,1)S(1)}, u32[]{:S(2)}, u32[]{:S(2)}) collective-permute-start(bf16[128,1792]{1,0:T(8,128)(2,1)} %get-tuple-element.29), channel_id=1, source_target_pairs={{0,128},{32,160},{64,192},{96,224},{128,0},{160,32},{192,64},{224,... | collective-permute-start | bytes 1376264 | tf_op jit(solution)/shard_map/ppermute | solution.py:29
  28.5 0.5 select_reduce_fusion.1
  29.0 0.1 add_select_fusion
  29.0 0.5 copy-done.4
  29.5 0.1 select_n.24
  29.6 0.1 fusion.2.refs_7_
  29.8 3.1 %collective-permute-done.refs_1_ = bf16[128,1792]{1,0:T(8,128)(2,1)} collective-permute-done((bf16[128,1792]{1,0:T(8,128)(2,1)}, bf16[128,1792]{1,0:T(8,128)(2,1)}, u32[]{:S(2)}, u32[]{:S(2)}) %collective-permute-start) | collective-permute-done | bytes 458784 | tf_op jit(solution)/shard_map/ppermute | solution.py:29
  32.9 0.9 collective-permute-done.1.refs_2_
  33.8 10.1 %collective-permute-done.5.refs_3_ = bf16[128,1792]{1,0:T(8,128)(2,1)S(1)} collective-permute-done((bf16[128,1792]{1,0:T(8,128)(2,1)}, bf16[128,1792]{1,0:T(8,128)(2,1)S(1)}, u32[]{:S(2)}, u32[]{:S(2)}) %collective-permute-start.5) | collective-permute-done | bytes 458784 | tf_op jit(solution)/shard_map/ppermute | solution.py:29
  43.8 1.5 %all-to-all-done = bf16[32,8,1792]{2,1,0:T(8,128)(2,1)} async-done(((bf16[32,8,1792]{2,1,0:T(8,128)(2,1)}), bf16[32,8,1792]{2,1,0:T(8,128)(2,1)}, u32[]{:S(2)}, u32[]{:S(2)}) %all-to-all-start) | async-done | bytes 917536 | tf_op jit(solution)/shard_map/all_to_all | solution.py:274
  45.4 3.0 %fresh_rows.1 = (bf16[128,1792]{1,0:T(8,128)(2,1)}, bf16[256,1792]{1,0:T(8,128)(2,1)}) custom-call(bf16[128,1792]{1,0:T(8,128)(2,1)S(1)} %get-tuple-element.21.refs_0_, bf16[128,1792]{1,0:T(8,128)(2,1)} %collective-permute-done.refs_1_, bf16[128,1792]{1,0:T(8,128)(2,1)} %collective-permute-done.1.refs_2_, ...), custom_call_target="tpu_custom_call" | custom-call | flops 234881024 | bytes 4587520 | tf_op jit(solution)/shard_map/fresh_rows/pallas_call | solution.py:167
  48.4 2.3 %collective-permute-start.10 = (bf16[128,1792]{1,0:T(8,128)(2,1)}, bf16[128,1792]{1,0:T(8,128)(2,1)}, u32[]{:S(2)}, u32[]{:S(2)}) collective-permute-start(bf16[128,1792]{1,0:T(8,128)(2,1)} %get-tuple-element.32.refs_0_), channel_id=1, source_target_pairs={{0,128},{32,160},{64,192},{96,224},{128,0},{160,32},{192,64},{224,... | collective-permute-start | bytes 1376264 | tf_op jit(solution)/shard_map/ppermute | solution.py:29
  50.7 2.0 %collective-permute-start.9 = (bf16[128,1792]{1,0:T(8,128)(2,1)}, bf16[128,1792]{1,0:T(8,128)(2,1)}, u32[]{:S(2)}, u32[]{:S(2)}) collective-permute-start(bf16[128,1792]{1,0:T(8,128)(2,1)} %get-tuple-element.32.refs_0_), channel_id=1, source_target_pairs={{0,32},{32,0},{64,96},{96,64},{128,160},{160,128},{192,224},{224,1... | collective-permute-start | bytes 1376264 | tf_op jit(solution)/shard_map/ppermute | solution.py:29
  52.7 0.8 collective-permute-start.8
  53.5 1.2 %collective-permute-start.7 = (bf16[128,1792]{1,0:T(8,128)(2,1)}, bf16[128,1792]{1,0:T(8,128)(2,1)}, u32[]{:S(2)}, u32[]{:S(2)}) collective-permute-start(bf16[128,1792]{1,0:T(8,128)(2,1)} %get-tuple-element.32.refs_0_), channel_id=1, source_target_pairs={{0,192},{32,224},{64,0},{96,32},{128,64},{160,96},{192,128},{224,1... | collective-permute-start | bytes 1376264 | tf_op jit(solution)/shard_map/ppermute | solution.py:29
  54.7 6.7 %all-to-all-start.1 = ((bf16[32,8,1792]{2,1,0:T(8,128)(2,1)}), bf16[32,8,1792]{2,1,0:T(8,128)(2,1)}, u32[]{:S(2)}, u32[]{:S(2)}) async-start(bf16[32,8,1792]{2,1,0:T(8,128)(2,1)} %bitcast.5), calls=%async_computation.1 | async-start | bytes 1835008 | tf_op jit(solution)/shard_map/all_to_all | solution.py:294
  61.4 2.3 %collective-permute-done.10.refs_1_ = bf16[128,1792]{1,0:T(8,128)(2,1)} collective-permute-done((bf16[128,1792]{1,0:T(8,128)(2,1)}, bf16[128,1792]{1,0:T(8,128)(2,1)}, u32[]{:S(2)}, u32[]{:S(2)}) %collective-permute-start.10) | collective-permute-done | bytes 458784 | tf_op jit(solution)/shard_map/ppermute | solution.py:29
  63.7 0.2 collective-permute-done.9.refs_0_
  64.0 2.0 %collective-permute-start.13 = (bf16[128,1792]{1,0:T(8,128)(2,1)}, bf16[128,1792]{1,0:T(8,128)(2,1)S(1)}, u32[]{:S(2)}, u32[]{:S(2)}) collective-permute-start(bf16[128,1792]{1,0:T(8,128)(2,1)} %get-tuple-element.33.refs_3_), channel_id=1, source_target_pairs={{0,32},{32,0},{64,96},{96,64},{128,160},{160,128},{192,224},{224,1... | collective-permute-start | bytes 1376264 | tf_op jit(solution)/shard_map/ppermute | solution.py:29
  66.0 1.4 %collective-permute-start.12 = (bf16[128,1792]{1,0:T(8,128)(2,1)}, bf16[128,1792]{1,0:T(8,128)(2,1)S(1)}, u32[]{:S(2)}, u32[]{:S(2)}) collective-permute-start(bf16[128,1792]{1,0:T(8,128)(2,1)} %get-tuple-element.34.refs_4_), channel_id=1, source_target_pairs={{0,64},{32,96},{64,128},{96,160},{128,192},{160,224},{192,0},{224,... | collective-permute-start | bytes 1376264 | tf_op jit(solution)/shard_map/ppermute | solution.py:29
  67.4 0.6 collective-permute-start.11
  68.0 0.2 dynamic-slice_reduce_fusion
  68.2 0.1 fusion.3
  68.3 0.1 reshape.129
  68.4 5.3 %collective-permute-done.8.refs_2_ = bf16[128,1792]{1,0:T(8,128)(2,1)} collective-permute-done((bf16[128,1792]{1,0:T(8,128)(2,1)}, bf16[128,1792]{1,0:T(8,128)(2,1)}, u32[]{:S(2)}, u32[]{:S(2)}) %collective-permute-start.8) | collective-permute-done | bytes 458784 | tf_op jit(solution)/shard_map/ppermute | solution.py:29
  73.7 10.4 %collective-permute-done.13.refs_7_ = bf16[128,1792]{1,0:T(8,128)(2,1)S(1)} collective-permute-done((bf16[128,1792]{1,0:T(8,128)(2,1)}, bf16[128,1792]{1,0:T(8,128)(2,1)S(1)}, u32[]{:S(2)}, u32[]{:S(2)}) %collective-permute-start.13) | collective-permute-done | bytes 458784 | tf_op jit(solution)/shard_map/ppermute | solution.py:29
  84.1 3.6 %all-to-all-done.1 = bf16[32,8,1792]{2,1,0:T(8,128)(2,1)} async-done(((bf16[32,8,1792]{2,1,0:T(8,128)(2,1)}), bf16[32,8,1792]{2,1,0:T(8,128)(2,1)}, u32[]{:S(2)}, u32[]{:S(2)}) %all-to-all-start.1) | async-done | bytes 917536 | tf_op jit(solution)/shard_map/all_to_all | solution.py:294
  87.7 0.1 broadcast_in_dim.6.refs_11_
  87.8 1.5 %copy-done.3 = f32[1,32,8,1792]{3,2,1,0:T(8,128)S(1)} copy-done((f32[1,32,8,1792]{3,2,1,0:T(8,128)S(1)}, f32[1,32,8,1792]{3,2,1,0:T(8,128)}, u32[]{:S(2)}) %copy-start.3) | copy-done | bytes 1835032
  89.3 5.5 %finish.1 = (f32[256,1792]{1,0:T(8,128)}, f32[256,1792]{1,0:T(8,128)}, bf16[128,14336]{1,0:T(8,128)(2,1)}) custom-call(bf16[128,1792]{1,0:T(8,128)(2,1)} %get-tuple-element.32.refs_0_, bf16[128,1792]{1,0:T(8,128)(2,1)} %collective-permute-done.7.refs_1_, bf16[128,1792]{1,0:T(8,128)(2,1)} %collective-permute-done.8.refs_2_, ...), custom_call_target="tpu_custom_call" | custom-call | flops 4587520 | bytes 15597568 | tf_op jit(solution)/shard_map/finish/pallas_call | solution.py:130
  (22 shorter events, 0.1 us)
Async XLA Ops:
  0.6 8.5 %copy-start = (f32[1,32,8,1792]{3,2,1,0:T(8,128)S(1)}, f32[1,32,8,1792]{3,2,1,0:T(8,128)}, u32[]{:S(2)}) copy-start(f32[1,32,8,1792]{3,2,1,0:T(8,128)} %param.7) | copy-start | bytes 5505028
  0.6 8.5 %copy-start.2 = (f32[1,32,8,1792]{3,2,1,0:T(8,128)S(1)}, f32[1,32,8,1792]{3,2,1,0:T(8,128)}, u32[]{:S(2)}) copy-start(f32[1,32,8,1792]{3,2,1,0:T(8,128)} %param.6) | copy-start | bytes 5505028
  4.0 17.9 %collective-permute-start.2 = (bf16[128,1792]{1,0:T(8,128)(2,1)}, bf16[128,1792]{1,0:T(8,128)(2,1)S(1)}, u32[]{:S(2)}, u32[]{:S(2)}) collective-permute-start(bf16[128,1792]{1,0:T(8,128)(2,1)} %get-tuple-element.25), channel_id=1, source_target_pairs={{0,32},{32,0},{64,96},{96,64},{128,160},{160,128},{192,224},{224,1... | collective-permute-start | bytes 1376264 | tf_op jit(solution)/shard_map/ppermute | solution.py:29
  7.1 14.7 %collective-permute-start.3 = (bf16[128,1792]{1,0:T(8,128)(2,1)S(1)}, bf16[128,1792]{1,0:T(8,128)(2,1)S(1)}, u32[]{:S(2)}, u32[]{:S(2)}) collective-permute-start(bf16[128,1792]{1,0:T(8,128)(2,1)S(1)} %get-tuple-element.27), channel_id=1, source_target_pairs={{0,64},{32,96},{64,128},{96,160},{128,192},{160,224},{192,0},{224,... | collective-permute-start | bytes 1376264 | tf_op jit(solution)/shard_map/ppermute | solution.py:29
  8.7 13.2 %collective-permute-start.4 = (bf16[128,1792]{1,0:T(8,128)(2,1)S(1)}, bf16[128,1792]{1,0:T(8,128)(2,1)}, u32[]{:S(2)}, u32[]{:S(2)}) collective-permute-start(bf16[128,1792]{1,0:T(8,128)(2,1)S(1)} %get-tuple-element.28), channel_id=1, source_target_pairs={{0,192},{32,224},{64,0},{96,32},{128,64},{160,96},{192,128},{224,1... | collective-permute-start | bytes 1376264 | tf_op jit(solution)/shard_map/ppermute | solution.py:29
  10.3 35.1 %all-to-all-start = ((bf16[32,8,1792]{2,1,0:T(8,128)(2,1)}), bf16[32,8,1792]{2,1,0:T(8,128)(2,1)}, u32[]{:S(2)}, u32[]{:S(2)}) async-start(bf16[32,8,1792]{2,1,0:T(8,128)(2,1)} %fusion), calls=%async_computation | async-start | bytes 1835008 | tf_op jit(solution)/shard_map/all_to_all | solution.py:274
  19.1 13.8 %collective-permute-start = (bf16[128,1792]{1,0:T(8,128)(2,1)}, bf16[128,1792]{1,0:T(8,128)(2,1)}, u32[]{:S(2)}, u32[]{:S(2)}) collective-permute-start(bf16[128,1792]{1,0:T(8,128)(2,1)} %get-tuple-element.22), channel_id=1, source_target_pairs={{0,64},{32,96},{64,128},{96,160},{128,192},{160,224},{192,0},{224,... | collective-permute-start | bytes 1376264 | tf_op jit(solution)/shard_map/ppermute | solution.py:29
  20.8 13.0 %collective-permute-start.1 = (bf16[128,1792]{1,0:T(8,128)(2,1)}, bf16[128,1792]{1,0:T(8,128)(2,1)}, u32[]{:S(2)}, u32[]{:S(2)}) collective-permute-start(bf16[128,1792]{1,0:T(8,128)(2,1)} %get-tuple-element.23), channel_id=1, source_target_pairs={{0,192},{32,224},{64,0},{96,32},{128,64},{160,96},{192,128},{224,1... | collective-permute-start | bytes 1376264 | tf_op jit(solution)/shard_map/ppermute | solution.py:29
  21.9 4.0 %copy-start.6 = (s32[32,24]{0,1:T(8,128)S(1)}, s32[32,24]{0,1:T(8,128)}, u32[]{:S(2)}) copy-start(s32[32,24]{0,1:T(8,128)} %param.8) | copy-start | bytes 9220
  21.9 4.0 %copy-start.7 = (s32[24,24]{1,0:T(8,128)S(1)}, s32[24,24]{1,0:T(8,128)}, u32[]{:S(2)}) copy-start(s32[24,24]{1,0:T(8,128)} %fusion.4) | copy-start | bytes 6916
  21.9 6.6 %copy-start.8 = (s32[32,32]{1,0:T(8,128)S(1)}, s32[32,32]{1,0:T(8,128)}, u32[]{:S(2)}) copy-start(s32[32,32]{1,0:T(8,128)} %param.9) | copy-start | bytes 12292
  23.8 20.0 %collective-permute-start.6 = (bf16[128,1792]{1,0:T(8,128)(2,1)S(1)}, bf16[128,1792]{1,0:T(8,128)(2,1)S(1)}, u32[]{:S(2)}, u32[]{:S(2)}) collective-permute-start(bf16[128,1792]{1,0:T(8,128)(2,1)S(1)} %get-tuple-element.30), channel_id=1, source_target_pairs={{0,32},{32,0},{64,96},{96,64},{128,160},{160,128},{192,224},{224,1... | collective-permute-start | bytes 1376264 | tf_op jit(solution)/shard_map/ppermute | solution.py:29
  26.1 17.7 %collective-permute-start.5 = (bf16[128,1792]{1,0:T(8,128)(2,1)}, bf16[128,1792]{1,0:T(8,128)(2,1)S(1)}, u32[]{:S(2)}, u32[]{:S(2)}) collective-permute-start(bf16[128,1792]{1,0:T(8,128)(2,1)} %get-tuple-element.29), channel_id=1, source_target_pairs={{0,128},{32,160},{64,192},{96,224},{128,0},{160,32},{192,64},{224,... | collective-permute-start | bytes 1376264 | tf_op jit(solution)/shard_map/ppermute | solution.py:29
  28.9 0.6 copy-start.4
  48.4 15.3 %collective-permute-start.10 = (bf16[128,1792]{1,0:T(8,128)(2,1)}, bf16[128,1792]{1,0:T(8,128)(2,1)}, u32[]{:S(2)}, u32[]{:S(2)}) collective-permute-start(bf16[128,1792]{1,0:T(8,128)(2,1)} %get-tuple-element.32.refs_0_), channel_id=1, source_target_pairs={{0,128},{32,160},{64,192},{96,224},{128,0},{160,32},{192,64},{224,... | collective-permute-start | bytes 1376264 | tf_op jit(solution)/shard_map/ppermute | solution.py:29
  50.7 13.3 %collective-permute-start.9 = (bf16[128,1792]{1,0:T(8,128)(2,1)}, bf16[128,1792]{1,0:T(8,128)(2,1)}, u32[]{:S(2)}, u32[]{:S(2)}) collective-permute-start(bf16[128,1792]{1,0:T(8,128)(2,1)} %get-tuple-element.32.refs_0_), channel_id=1, source_target_pairs={{0,32},{32,0},{64,96},{96,64},{128,160},{160,128},{192,224},{224,1... | collective-permute-start | bytes 1376264 | tf_op jit(solution)/shard_map/ppermute | solution.py:29
  52.7 21.0 %collective-permute-start.8 = (bf16[128,1792]{1,0:T(8,128)(2,1)}, bf16[128,1792]{1,0:T(8,128)(2,1)}, u32[]{:S(2)}, u32[]{:S(2)}) collective-permute-start(bf16[128,1792]{1,0:T(8,128)(2,1)} %get-tuple-element.32.refs_0_), channel_id=1, source_target_pairs={{0,64},{32,96},{64,128},{96,160},{128,192},{160,224},{192,0},{224,... | collective-permute-start | bytes 1376264 | tf_op jit(solution)/shard_map/ppermute | solution.py:29
  53.5 20.1 %collective-permute-start.7 = (bf16[128,1792]{1,0:T(8,128)(2,1)}, bf16[128,1792]{1,0:T(8,128)(2,1)}, u32[]{:S(2)}, u32[]{:S(2)}) collective-permute-start(bf16[128,1792]{1,0:T(8,128)(2,1)} %get-tuple-element.32.refs_0_), channel_id=1, source_target_pairs={{0,192},{32,224},{64,0},{96,32},{128,64},{160,96},{192,128},{224,1... | collective-permute-start | bytes 1376264 | tf_op jit(solution)/shard_map/ppermute | solution.py:29
  54.7 32.9 %all-to-all-start.1 = ((bf16[32,8,1792]{2,1,0:T(8,128)(2,1)}), bf16[32,8,1792]{2,1,0:T(8,128)(2,1)}, u32[]{:S(2)}, u32[]{:S(2)}) async-start(bf16[32,8,1792]{2,1,0:T(8,128)(2,1)} %bitcast.5), calls=%async_computation.1 | async-start | bytes 1835008 | tf_op jit(solution)/shard_map/all_to_all | solution.py:294
  64.0 4.0 %copy-start.5 = (s32[32,32]{1,0:T(8,128)S(1)}, s32[32,32]{1,0:T(8,128)}, u32[]{:S(2)}) copy-start(s32[32,32]{1,0:T(8,128)} %copy-done.4) | copy-start | bytes 12292
  64.0 23.8 %copy-start.1 = (f32[1,32,8,1792]{3,2,1,0:T(8,128)S(1)}, f32[1,32,8,1792]{3,2,1,0:T(8,128)}, u32[]{:S(2)}) copy-start(f32[1,32,8,1792]{3,2,1,0:T(8,128)} %param.7) | copy-start | bytes 5505028
  64.0 20.1 %collective-permute-start.13 = (bf16[128,1792]{1,0:T(8,128)(2,1)}, bf16[128,1792]{1,0:T(8,128)(2,1)S(1)}, u32[]{:S(2)}, u32[]{:S(2)}) collective-permute-start(bf16[128,1792]{1,0:T(8,128)(2,1)} %get-tuple-element.33.refs_3_), channel_id=1, source_target_pairs={{0,32},{32,0},{64,96},{96,64},{128,160},{160,128},{192,224},{224,1... | collective-permute-start | bytes 1376264 | tf_op jit(solution)/shard_map/ppermute | solution.py:29
  66.0 18.1 %collective-permute-start.12 = (bf16[128,1792]{1,0:T(8,128)(2,1)}, bf16[128,1792]{1,0:T(8,128)(2,1)S(1)}, u32[]{:S(2)}, u32[]{:S(2)}) collective-permute-start(bf16[128,1792]{1,0:T(8,128)(2,1)} %get-tuple-element.34.refs_4_), channel_id=1, source_target_pairs={{0,64},{32,96},{64,128},{96,160},{128,192},{160,224},{192,0},{224,... | collective-permute-start | bytes 1376264 | tf_op jit(solution)/shard_map/ppermute | solution.py:29
  67.4 16.7 %collective-permute-start.11 = (bf16[128,1792]{1,0:T(8,128)(2,1)}, bf16[128,1792]{1,0:T(8,128)(2,1)S(1)}, u32[]{:S(2)}, u32[]{:S(2)}) collective-permute-start(bf16[128,1792]{1,0:T(8,128)(2,1)} %get-tuple-element.34.refs_4_), channel_id=1, source_target_pairs={{0,192},{32,224},{64,0},{96,32},{128,64},{160,96},{192,128},{224,1... | collective-permute-start | bytes 1376264 | tf_op jit(solution)/shard_map/ppermute | solution.py:29
  87.8 1.5 %copy-start.3 = (f32[1,32,8,1792]{3,2,1,0:T(8,128)S(1)}, f32[1,32,8,1792]{3,2,1,0:T(8,128)}, u32[]{:S(2)}) copy-start(f32[1,32,8,1792]{3,2,1,0:T(8,128)} %param.6) | copy-start | bytes 5505028

commit v4 on v3

--- a/solution.py
+++ b/solution.py
@@ -8,6 +8,7 @@
 outer_rate = 0.7
 momentum_decay = 0.9
 PACE = 1150000000000
+GATE_PACE = 11500000000
 pull = outer_rate * (1.0 + momentum_decay)
 keep = 1.0 - pull
 drag = outer_rate * momentum_decay * momentum_decay
@@ -80,21 +81,63 @@
     return dict(zip(STEPS, chunks))
 
 
-def finish(chunks, arrived, outer, momentum, live, scale):
-    parts = len(STEPS)
-    row_count, columns = chunks[STEPS[0]].shape
+def join_columns(chunks, into=None):
+    steps = list(chunks)
+    row_count, columns = chunks[steps[0]].shape
+
+    def kernel(*refs):
+        ins, out, sems = refs[: len(steps)], refs[-2], refs[-1]
+        me = lax.axis_index("replica")
+        copies = []
+        for k, step in enumerate(steps):
+            come = place_traced(me, step)
+            copies.append(
+                pltpu.make_async_copy(
+                    ins[k],
+                    out.at[:, pl.ds(pl.multiple_of(come * columns, 128), columns)],
+                    sems.at[k],
+                )
+            )
+        for copy in copies:
+            copy.start()
+        for copy in copies:
+            copy.wait()
+
+    args = [chunks[step] for step in steps]
+    specs = [pl.BlockSpec(memory_space=pltpu.VMEM)] * len(steps)
+    if into is not None:
+        args.append(into)
+        specs.append(pl.BlockSpec(memory_space=pltpu.HBM))
+    return pl.pallas_call(
+        kernel,
+        out_shape=jax.ShapeDtypeStruct((row_count, columns * len(STEPS)), jnp.bfloat16),
+        in_specs=specs,
+        out_specs=pl.BlockSpec(memory_space=pltpu.HBM),
+        input_output_aliases={} if into is None else {len(steps): 0},
+        scratch_shapes=[pltpu.SemaphoreType.DMA((len(steps),))],
+        cost_estimate=pl.CostEstimate(
+            flops=0, bytes_accessed=4 * row_count * columns * len(steps), transcendentals=0
+        ),
+        compiler_params=pltpu.CompilerParams(vmem_limit_bytes=8 * 1024 * 1024),
+        name="join_columns",
+    )(*args)
+
+
+def finish(chunks, into, arrived, outer, momentum, live, scale):
+    steps = list(chunks)
+    row_count, columns = chunks[steps[0]].shape
     slot_count = arrived.shape[0]
-    steps = 4
-    block_rows = slot_count // steps
+    blocks = 4
+    rows = slot_count // blocks
 
     def kernel(*refs):
-        ins = refs[:parts]
-        arrived_ref, outer_ref, momentum_ref, live_ref = refs[parts : parts + 4]
-        new_outer_ref, new_momentum_ref, joined_ref, sems = refs[parts + 4 :]
+        ins = refs[: len(steps)]
+        arrived_ref, outer_ref, momentum_ref, live_ref, _ = refs[len(steps) : len(steps) + 5]
+        new_outer_ref, new_momentum_ref, joined_ref, sems = refs[len(steps) + 5 :]
         i = pl.program_id(0)
         me = lax.axis_index("replica")
         copies = []
-        for k, step in enumerate(STEPS):
+        for k, step in enumerate(steps):
             come = place_traced(me, step)
             copies.append(
                 pltpu.make_async_copy(
@@ -109,77 +152,81 @@
             for copy in copies:
                 copy.start()
 
-        at = pl.ds(pl.multiple_of(i * block_rows, block_rows), block_rows)
-        alive = live_ref[at, :] > 0.0
+        alive = live_ref[...] > 0.0
+        at = pl.ds(pl.multiple_of(i * rows, rows), rows)
         for start in range(0, columns, 128):
             cols = pl.ds(start, 128)
-            mean = arrived_ref[at, cols].astype(jnp.float32) * scale
-            old = outer_ref[at, cols]
+            mean = arrived_ref[:, cols].astype(jnp.float32) * scale
+            old = outer_ref[:, cols]
             pseudo_grad = jnp.where(alive, old - mean, 0.0)
             fresh = momentum_decay * momentum_ref[at, cols] + pseudo_grad
             new_momentum_ref[:, cols] = fresh
             new_outer_ref[:, cols] = old - outer_rate * (pseudo_grad + momentum_decay * fresh)
 
-        @pl.when(i == steps - 1)
+        @pl.when(i == blocks - 1)
         def _():
             for copy in copies:
                 copy.wait()
 
     whole = pl.BlockSpec(memory_space=pltpu.VMEM)
-    block = pl.BlockSpec((block_rows, columns), lambda i: (i, 0))
-    return pl.pallas_call(
-        kernel,
-        grid=(steps,),
+    in_hbm = pl.BlockSpec(memory_space=pltpu.HBM)
+    block = pl.BlockSpec((rows, columns), lambda i: (i, 0))
+    return pl.pallas_call(
+        kernel,
+        grid=(blocks,),
         out_shape=[jax.ShapeDtypeStruct((slot_count, columns), jnp.float32)] * 2
-        + [jax.ShapeDtypeStruct((row_count, parts * columns), jnp.bfloat16)],
-        in_specs=[whole] * (parts + 4),
-        out_specs=[block, block, pl.BlockSpec(memory_space=pltpu.HBM)],
-        scratch_shapes=[pltpu.SemaphoreType.DMA((parts,))],
+        + [jax.ShapeDtypeStruct(into.shape, into.dtype)],
+        in_specs=[whole] * len(steps)
+        + [block, block, whole, pl.BlockSpec((rows, 128), lambda i: (i, 0)), in_hbm],
+        out_specs=[block, block, in_hbm],
+        input_output_aliases={len(steps) + 4: 2},
+        scratch_shapes=[pltpu.SemaphoreType.DMA((len(steps),))],
         cost_estimate=pl.CostEstimate(
             flops=10 * slot_count * columns,
-            bytes_accessed=4 * row_count * columns * parts + 18 * slot_count * columns,
+            bytes_accessed=4 * row_count * columns * len(steps) + 18 * slot_count * columns,
             transcendentals=0,
         ),
-        compiler_params=pltpu.CompilerParams(vmem_limit_bytes=14 * 1024 * 1024),
+        compiler_params=pltpu.CompilerParams(vmem_limit_bytes=12 * 1024 * 1024),
         name="finish",
-    )(*[chunks[step] for step in STEPS], arrived, outer, momentum, live)
-
-
-def fresh_rows(parts, base, unpick, pick, scale):
-    row_count, columns = parts[0].shape
-    slot_count = base.shape[0]
+    )(
+        *[chunks[step] for step in steps],
+        arrived,
+        pltpu.with_memory_space_constraint(outer, pltpu.HBM),
+        momentum,
+        live,
+        into,
+    )
+
+
+def fresh_rows(parts, share, scale):
+    row_count, columns = share.shape
     width = 256
 
     def kernel(*refs):
         part_refs = refs[: len(parts)]
-        base_ref, unpick_ref, pick_ref, rows_ref, slots_ref = refs[len(parts) :]
+        share_ref, rows_ref, total_ref = refs[len(parts) :]
         for start in range(0, columns, width):
             at = (slice(None), pl.ds(start, width))
             total = part_refs[0][at].astype(jnp.float32)
             for ref in part_refs[1:]:
                 total = total + ref[at].astype(jnp.float32)
-            share = jnp.dot(unpick_ref[...], base_ref[at], preferred_element_type=jnp.float32)
-            rows_ref[at] = (share + scale * total).astype(rows_ref.dtype)
-            slots_ref[at] = jnp.dot(
-                pick_ref[...], total.astype(jnp.bfloat16), preferred_element_type=jnp.float32
-            ).astype(slots_ref.dtype)
-
-    return pl.pallas_call(
-        kernel,
-        out_shape=[
-            jax.ShapeDtypeStruct((row_count, columns), jnp.bfloat16),
-            jax.ShapeDtypeStruct((slot_count, columns), jnp.bfloat16),
-        ],
-        in_specs=[pl.BlockSpec(memory_space=pltpu.VMEM)] * (len(parts) + 3),
+            more = share_ref[at].astype(jnp.float32)
+            rows_ref[at] = (more + scale * total).astype(rows_ref.dtype)
+            total_ref[at] = total.astype(total_ref.dtype)
+
+    return pl.pallas_call(
+        kernel,
+        out_shape=[jax.ShapeDtypeStruct((row_count, columns), jnp.bfloat16)] * 2,
+        in_specs=[pl.BlockSpec(memory_space=pltpu.VMEM)] * (len(parts) + 1),
         out_specs=[pl.BlockSpec(memory_space=pltpu.VMEM)] * 2,
         cost_estimate=pl.CostEstimate(
-            flops=4 * row_count * slot_count * columns,
-            bytes_accessed=2 * columns * (row_count * (len(parts) + 1) + 2 * slot_count),
+            flops=row_count * columns * (len(parts) + 2),
+            bytes_accessed=2 * columns * row_count * (len(parts) + 3),
             transcendentals=0,
         ),
         compiler_params=pltpu.CompilerParams(vmem_limit_bytes=8 * 1024 * 1024),
         name="fresh_rows",
-    )(*parts, base, unpick, pick)
+    )(*parts, share)
 
 
 def partial_sums(*sums):
@@ -215,6 +262,32 @@
     )(*terms)
 
 
+def pick_rows(pick, array, name):
+    count, columns = pick.shape[0], array.shape[1]
+    width = 256
+
+    def kernel(pick_ref, array_ref, out_ref):
+        for start in range(0, columns, width):
+            cols = pl.ds(start, width)
+            out_ref[:, cols] = jnp.dot(
+                pick_ref[...], array_ref[:, cols], preferred_element_type=jnp.float32
+            ).astype(out_ref.dtype)
+
+    return pl.pallas_call(
+        kernel,
+        out_shape=jax.ShapeDtypeStruct((count, columns), array.dtype),
+        in_specs=[pl.BlockSpec(memory_space=pltpu.VMEM)] * 2,
+        out_specs=pl.BlockSpec(memory_space=pltpu.VMEM),
+        cost_estimate=pl.CostEstimate(
+            flops=2 * count * array.shape[0] * columns,
+            bytes_accessed=2 * columns * (count + array.shape[0]),
+            transcendentals=0,
+        ),
+        compiler_params=pltpu.CompilerParams(vmem_limit_bytes=4 * 1024 * 1024),
+        name=name,
+    )(pick, array)
+
+
 def gate(*arrays):
     def kernel(*refs):
         pass
@@ -225,7 +298,7 @@
         in_specs=[pl.BlockSpec(memory_space=pl.ANY)] * len(arrays),
         out_specs=[pl.BlockSpec(memory_space=pl.ANY)] * len(arrays),
         input_output_aliases={i: i for i in range(len(arrays))},
-        cost_estimate=pl.CostEstimate(flops=PACE, bytes_accessed=0, transcendentals=0),
+        cost_estimate=pl.CostEstimate(flops=GATE_PACE, bytes_accessed=0, transcendentals=0),
         compiler_params=pltpu.CompilerParams(vmem_limit_bytes=1024 * 1024),
         name="gate",
     )(*arrays)
@@ -287,16 +360,19 @@
     ).reshape(-1)
     pick = (row_of_slot[:, None] == row_ids[None, :]).astype(own_rows.dtype)
     unpick = (row_ids[:, None] == row_of_slot[None, :]).astype(own_rows.dtype)
-    rows, packed = fresh_rows(
-        parts, own_base.reshape(fsdp_count * slots, columns), unpick, pick, pull / group_count
-    )
+    share = pick_rows(unpick, own_base.reshape(-1, columns), "own_share")
+    rows, total = fresh_rows(parts, share, pull / group_count)
+    packed = pick_rows(pick, total, "pack_slots")
     gathered = gather_over_replica(rows)
     arrived = lax.all_to_all(
         packed.reshape(fsdp_count, slots, columns), "fsdp", split_axis=0, concat_axis=0, tiled=True
     )
     flat = (fsdp_count * slots, columns)
+    first = [(0, 0), (0, 1), (2, 0), (1, 0), (3, 0)]
+    joined = join_columns({step: gathered[step] for step in first})
     fresh_outer, fresh_momentum, joined = finish(
-        gathered,
+        {step: gathered[step] for step in STEPS if step not in first},
+        joined,
         arrived.reshape(flat),
         outer_here.reshape(flat),
         momentum_here.reshape(flat),

time: 96.4 us -> 91.1 us (0.945); the launches traced: 94.7 us -> 90.7 us
  waiting for transfers between devices: 37.5 us -> 32.4 us
  Pallas kernels: 13.7 us -> 16.8 us
  local copies, waits for them, and re-layouts: 2.63 us -> 0.65 us
    ppermute x14, waiting for transfers between devices: 32.3 us -> 13.5 us  [send(): lax.ppermute(array, 'replica', [(i, place(i, step)) for i in range(8)])]
    all_to_all x1, waiting for transfers between devices: 1.53 us -> 16.8 us  [body(): lax.all_to_all(base, 'fsdp', split_axis=0, concat_axis=0, tiled=True)]
    pallas_call x1 -> x4, Pallas kernels: 5.45 us -> 10.6 us  [the longest x1 5.02 us: finish(): pl.pallas_call(kernel, grid=(blocks,), out_shape=[jax.ShapeDtypeStruct((s...]
    unnamed x18 -> x12, local copies, waits for them, and re-layouts: 2.03 us -> 0.04 us
    all_to_all x1, starting transfers between devices: 6.69 us -> 5.11 us  [body(): lax.all_to_all(packed.reshape(fsdp_count, slots, columns), 'fsdp', split_...]
    pallas_call x1, Pallas kernels: 3.03 us -> 1.55 us  [fresh_rows(): pl.pallas_call(kernel, out_shape=[jax.ShapeDtypeStruct((row_count, column...]
    ppermute x14, starting transfers between devices: 21.9 us -> 23.3 us  [send(): lax.ppermute(array, 'replica', [(i, place(i, step)) for i in range(8)])]
    all_to_all x1, waiting for transfers between devices: 3.6 us -> 2.23 us  [body(): lax.all_to_all(packed.reshape(fsdp_count, slots, columns), 'fsdp', split_...]
  transfers between devices with their start and end apart: 16 -> 16, of which waited for: 9 -> 7; matrix products, arithmetic and copies ran while one was open for 3% -> 4% of each run, Pallas kernels for 2% -> 8%
where the time goes in v4:
time: 91.1 us; the launch traced here: 90.7 us
  starting transfers between devices  37.3 us (41%)
  waiting for transfers between devices  32.4 us (36%)
  Pallas kernels  16.8 us (18%)
  other arithmetic  2.68 us (3%)
    ppermute x14, starting transfers between devices, send(): lax.ppermute(array, 'replica', [(i, place(i, step)) for i in range(8)])  23.3 us
    all_to_all x1, waiting for transfers between devices, body(): lax.all_to_all(base, 'fsdp', split_axis=0, concat_axis=0, tiled=True)  16.8 us
    ppermute x14, waiting for transfers between devices, send(): lax.ppermute(array, 'replica', [(i, place(i, step)) for i in range(8)])  13.5 us
    all_to_all x1, starting transfers between devices, body(): lax.all_to_all(base, 'fsdp', split_axis=0, concat_axis=0, tiled=True)  8.81 us
    all_to_all x1, starting transfers between devices, body(): lax.all_to_all(packed.reshape(fsdp_count, slots, columns), 'fsdp', split_...  5.11 us
    pallas_call x1, Pallas kernels, finish(): pl.pallas_call(kernel, grid=(blocks,), out_shape=[jax.ShapeDtypeStruct((s...  5.02 us
    pallas_call x1, Pallas kernels, split_columns(): pl.pallas_call(kernel, out_shape=[jax.ShapeDtypeStruct((row_count, column...  3.3 us
    pallas_call x1, Pallas kernels, join_columns(): pl.pallas_call(kernel, out_shape=jax.ShapeDtypeStruct((row_count, columns...  2.85 us
  transfers between devices with their start and end apart: 16, of which 7 were waited for; matrix products, arithmetic and copies ran while one was open for 4% of the time, Pallas kernels for 8%

profile of v4, /device:TPU:40, one launch (start us, length us, event | category | flops | bytes accessed | tf_op | source)
XLA Modules:
  0.0 90.7 jit_solution(1371686194521025374)
XLA Ops:
  0.6 0.0 copy-start
  0.6 0.0 copy-start.2
  0.7 3.3 %split_columns.1 = (bf16[128,1792]{1,0:T(8,128)(2,1)S(1)}, bf16[128,1792]{1,0:T(8,128)(2,1)}, bf16[128,1792]{1,0:T(8,128)(2,1)}, bf16[128,1792]{1,0:T(8,128)(2,1...) custom-call(bf16[128,14336]{1,0:T(8,128)(2,1)} %bitcast.18), custom_call_target="tpu_custom_call" | custom-call | bytes 7340032 | tf_op jit(solution)/shard_map/split_columns/pallas_call | solution.py:69
  4.0 3.1 %collective-permute-start.2 = (bf16[128,1792]{1,0:T(8,128)(2,1)}, bf16[128,1792]{1,0:T(8,128)(2,1)S(1)}, u32[]{:S(2)}, u32[]{:S(2)}) collective-permute-start(bf16[128,1792]{1,0:T(8,128)(2,1)} %get-tuple-element.25), channel_id=1, source_target_pairs={{0,32},{32,0},{64,96},{96,64},{128,160},{160,128},{192,224},{224,1... | collective-permute-start | bytes 1376264 | tf_op jit(solution)/shard_map/ppermute | solution.py:30
  7.1 1.6 %collective-permute-start.3 = (bf16[128,1792]{1,0:T(8,128)(2,1)S(1)}, bf16[128,1792]{1,0:T(8,128)(2,1)S(1)}, u32[]{:S(2)}, u32[]{:S(2)}) collective-permute-start(bf16[128,1792]{1,0:T(8,128)(2,1)S(1)} %get-tuple-element.27), channel_id=1, source_target_pairs={{0,64},{32,96},{64,128},{96,160},{128,192},{160,224},{192,0},{224,... | collective-permute-start | bytes 1376264 | tf_op jit(solution)/shard_map/ppermute | solution.py:30
  8.7 0.4 collective-permute-start.4
  9.1 1.2 %fusion = bf16[32,8,1792]{2,1,0:T(8,128)(2,1)} fusion(f32[1,32,8,1792]{3,2,1,0:T(8,128)S(1)} %copy-done, f32[1,32,8,1792]{3,2,1,0:T(8,128)S(1)} %copy-done.2), kind=kLoop, calls=%fused_computation.1 | loop fusion | flops 1835008 | bytes 4587520 | tf_op jit(solution)/shard_map/convert_element_type | solution.py:346
  10.3 8.8 %all-to-all-start = ((bf16[32,8,1792]{2,1,0:T(8,128)(2,1)}), bf16[32,8,1792]{2,1,0:T(8,128)(2,1)}, u32[]{:S(2)}, u32[]{:S(2)}) async-start(bf16[32,8,1792]{2,1,0:T(8,128)(2,1)} %fusion), calls=%async_computation | async-start | bytes 1835008 | tf_op jit(solution)/shard_map/all_to_all | solution.py:347
  19.1 1.7 %collective-permute-start = (bf16[128,1792]{1,0:T(8,128)(2,1)}, bf16[128,1792]{1,0:T(8,128)(2,1)}, u32[]{:S(2)}, u32[]{:S(2)}) collective-permute-start(bf16[128,1792]{1,0:T(8,128)(2,1)} %get-tuple-element.22), channel_id=1, source_target_pairs={{0,64},{32,96},{64,128},{96,160},{128,192},{160,224},{192,0},{224,... | collective-permute-start | bytes 1376264 | tf_op jit(solution)/shard_map/ppermute | solution.py:30
  20.8 0.5 collective-permute-start.1
  21.2 0.6 fusion.4
  21.8 0.0 copy-start.3
  21.9 0.0 copy-start.5
  21.9 1.3 %partial_sums.1 = (bf16[128,1792]{1,0:T(8,128)(2,1)S(1)}, bf16[128,1792]{1,0:T(8,128)(2,1)S(1)}) custom-call(bf16[128,1792]{1,0:T(8,128)(2,1)S(1)} %get-tuple-element.24.refs_0_, bf16[128,1792]{1,0:T(8,128)(2,1)S(1)} %collective-permute-done.2.refs_1_, bf16[128,1792]{1,0:T(8,128)(2,1)S(1)} %get-tuple-element.26.refs_2_, ...), custom_call_target="tpu_custom_call" | custom-call | flops 1150000037888 | bytes 3211264 | tf_op jit(solution)/shard_map/partial_sums/pallas_call | solution.py:250
  23.2 2.1 %collective-permute-start.6 = (bf16[128,1792]{1,0:T(8,128)(2,1)S(1)}, bf16[128,1792]{1,0:T(8,128)(2,1)S(1)}, u32[]{:S(2)}, u32[]{:S(2)}) collective-permute-start(bf16[128,1792]{1,0:T(8,128)(2,1)S(1)} %get-tuple-element.30), channel_id=1, source_target_pairs={{0,32},{32,0},{64,96},{96,64},{128,160},{160,128},{192,224},{224,1... | collective-permute-start | bytes 1376264 | tf_op jit(solution)/shard_map/ppermute | solution.py:30
  25.3 0.1 copy.17
  25.3 0.2 multiply_reduce_fusion
  25.5 0.1 copy.18
  25.6 2.3 %collective-permute-start.5 = (bf16[128,1792]{1,0:T(8,128)(2,1)S(1)}, bf16[128,1792]{1,0:T(8,128)(2,1)S(1)}, u32[]{:S(2)}, u32[]{:S(2)}) collective-permute-start(bf16[128,1792]{1,0:T(8,128)(2,1)S(1)} %get-tuple-element.29), channel_id=1, source_target_pairs={{0,128},{32,160},{64,192},{96,224},{128,0},{160,32},{192,64},{224,... | collective-permute-start | bytes 1376264 | tf_op jit(solution)/shard_map/ppermute | solution.py:30
  27.9 0.5 select_reduce_fusion.1
  28.4 0.1 add_select_fusion
  28.5 0.1 select_n.24
  28.6 16.8 %all-to-all-done = bf16[32,8,1792]{2,1,0:T(8,128)(2,1)} async-done(((bf16[32,8,1792]{2,1,0:T(8,128)(2,1)}), bf16[32,8,1792]{2,1,0:T(8,128)(2,1)}, u32[]{:S(2)}, u32[]{:S(2)}) %all-to-all-start) | async-done | bytes 917536 | tf_op jit(solution)/shard_map/all_to_all | solution.py:347
  45.4 1.5 %own_share.1.refs_5_ = bf16[128,1792]{1,0:T(8,128)(2,1)S(1)} custom-call(bf16[128,256]{1,0:T(8,128)(2,1)S(1)} %fusion.1.pick_ref, bf16[256,1792]{1,0:T(8,128)(2,1)} %bitcast.4.array_ref), custom_call_target="tpu_custom_call" | custom-call | flops 117440512 | bytes 1376256 | tf_op jit(solution)/shard_map/own_share/pallas_call | solution.py:276
  46.9 1.5 %fresh_rows.1 = (bf16[128,1792]{1,0:T(8,128)(2,1)S(1)}, bf16[128,1792]{1,0:T(8,128)(2,1)S(1)}) custom-call(bf16[128,1792]{1,0:T(8,128)(2,1)S(1)} %get-tuple-element.21.refs_0_, bf16[128,1792]{1,0:T(8,128)(2,1)} %collective-permute-done.refs_1_, bf16[128,1792]{1,0:T(8,128)(2,1)} %collective-permute-done.1.refs_2_, ...), custom_call_target="tpu_custom_call" | custom-call | flops 1605632 | bytes 3670016 | tf_op jit(solution)/shard_map/fresh_rows/pallas_call | solution.py:217
  48.4 2.4 %collective-permute-start.8 = (bf16[128,1792]{1,0:T(8,128)(2,1)S(1)}, bf16[128,1792]{1,0:T(8,128)(2,1)}, u32[]{:S(2)}, u32[]{:S(2)}) collective-permute-start(bf16[128,1792]{1,0:T(8,128)(2,1)S(1)} %get-tuple-element.32.refs_0_), channel_id=1, source_target_pairs={{0,128},{32,160},{64,192},{96,224},{128,0},{160,32},{192,64},{224,... | collective-permute-start | bytes 1376264 | tf_op jit(solution)/shard_map/ppermute | solution.py:30
  50.8 2.0 %collective-permute-start.7 = (bf16[128,1792]{1,0:T(8,128)(2,1)S(1)}, bf16[128,1792]{1,0:T(8,128)(2,1)}, u32[]{:S(2)}, u32[]{:S(2)}) collective-permute-start(bf16[128,1792]{1,0:T(8,128)(2,1)S(1)} %get-tuple-element.32.refs_0_), channel_id=1, source_target_pairs={{0,32},{32,0},{64,96},{96,64},{128,160},{160,128},{192,224},{224,1... | collective-permute-start | bytes 1376264 | tf_op jit(solution)/shard_map/ppermute | solution.py:30
  52.8 0.1 fusion.2.pick_ref
  52.9 1.3 %pack_slots.1 = bf16[256,1792]{1,0:T(8,128)(2,1)} custom-call(bf16[256,128]{1,0:T(8,128)(2,1)S(1)} %fusion.2.pick_ref, bf16[128,1792]{1,0:T(8,128)(2,1)S(1)} %get-tuple-element.35.array_ref), custom_call_target="tpu_custom_call" | custom-call | flops 117440512 | bytes 1376256 | tf_op jit(solution)/shard_map/pack_slots/pallas_call | solution.py:276
  54.2 5.1 %all-to-all-start.1 = ((bf16[32,8,1792]{2,1,0:T(8,128)(2,1)}), bf16[32,8,1792]{2,1,0:T(8,128)(2,1)S(1)}, u32[]{:S(2)}, u32[]{:S(2)}) async-start(bf16[32,8,1792]{2,1,0:T(8,128)(2,1)} %bitcast.5), calls=%async_computation.1 | async-start | bytes 1835008 | tf_op jit(solution)/shard_map/all_to_all | solution.py:367
  59.4 0.4 collective-permute-start.13
  59.8 1.7 %collective-permute-start.12 = (bf16[128,1792]{1,0:T(8,128)(2,1)S(1)}, bf16[128,1792]{1,0:T(8,128)(2,1)}, u32[]{:S(2)}, u32[]{:S(2)}) collective-permute-start(bf16[128,1792]{1,0:T(8,128)(2,1)S(1)} %get-tuple-element.32.refs_0_), channel_id=1, source_target_pairs={{0,192},{32,224},{64,0},{96,32},{128,64},{160,96},{192,128},{224,1... | collective-permute-start | bytes 1376264 | tf_op jit(solution)/shard_map/ppermute | solution.py:30
  61.5 0.4 collective-permute-done.8.refs_1_
  61.8 2.5 %collective-permute-done.7.refs_0_ = bf16[128,1792]{1,0:T(8,128)(2,1)} collective-permute-done((bf16[128,1792]{1,0:T(8,128)(2,1)S(1)}, bf16[128,1792]{1,0:T(8,128)(2,1)}, u32[]{:S(2)}, u32[]{:S(2)}) %collective-permute-start.7) | collective-permute-done | bytes 458784 | tf_op jit(solution)/shard_map/ppermute | solution.py:30
  64.4 3.0 %collective-permute-start.11 = (bf16[128,1792]{1,0:T(8,128)(2,1)}, bf16[128,1792]{1,0:T(8,128)(2,1)}, u32[]{:S(2)}, u32[]{:S(2)}) collective-permute-start(bf16[128,1792]{1,0:T(8,128)(2,1)} %get-tuple-element.34.refs_2_), channel_id=1, source_target_pairs={{0,32},{32,0},{64,96},{96,64},{128,160},{160,128},{192,224},{224,1... | collective-permute-start | bytes 1376264 | tf_op jit(solution)/shard_map/ppermute | solution.py:30
  67.4 1.2 %collective-permute-start.10 = (bf16[128,1792]{1,0:T(8,128)(2,1)}, bf16[128,1792]{1,0:T(8,128)(2,1)}, u32[]{:S(2)}, u32[]{:S(2)}) collective-permute-start(bf16[128,1792]{1,0:T(8,128)(2,1)} %get-tuple-element.33.refs_1_), channel_id=1, source_target_pairs={{0,64},{32,96},{64,128},{96,160},{128,192},{160,224},{192,0},{224,... | collective-permute-start | bytes 1376264 | tf_op jit(solution)/shard_map/ppermute | solution.py:30
  68.5 1.0 %collective-permute-start.9 = (bf16[128,1792]{1,0:T(8,128)(2,1)}, bf16[128,1792]{1,0:T(8,128)(2,1)}, u32[]{:S(2)}, u32[]{:S(2)}) collective-permute-start(bf16[128,1792]{1,0:T(8,128)(2,1)} %get-tuple-element.33.refs_1_), channel_id=1, source_target_pairs={{0,192},{32,224},{64,0},{96,32},{128,64},{160,96},{192,128},{224,1... | collective-permute-start | bytes 1376264 | tf_op jit(solution)/shard_map/ppermute | solution.py:30
  69.5 0.2 dynamic-slice_reduce_fusion
  69.7 0.1 fusion.3
  69.8 0.1 reshape.129
  69.9 0.0 copy-start.1
  69.9 3.0 %collective-permute-done.13.refs_4_ = bf16[128,1792]{1,0:T(8,128)(2,1)} collective-permute-done((bf16[128,1792]{1,0:T(8,128)(2,1)S(1)}, bf16[128,1792]{1,0:T(8,128)(2,1)}, u32[]{:S(2)}, u32[]{:S(2)}) %collective-permute-start.13) | collective-permute-done | bytes 458784 | tf_op jit(solution)/shard_map/ppermute | solution.py:30
  72.9 0.4 collective-permute-done.12.refs_3_
  73.3 2.8 %join_columns.1.refs_7_ = bf16[128,14336]{1,0:T(8,128)(2,1)} custom-call(bf16[128,1792]{1,0:T(8,128)(2,1)S(1)} %get-tuple-element.32.refs_0_, bf16[128,1792]{1,0:T(8,128)(2,1)} %get-tuple-element.33.refs_1_, bf16[128,1792]{1,0:T(8,128)(2,1)} %get-tuple-element.34.refs_2_, bf16[128,1792]{1,0:T(8,128)(2,1)} %collective-permute-done.12.refs_3_, ...), custom_call_target="tpu_custom_call" | custom-call | bytes 4587520 | tf_op jit(solution)/shard_map/join_columns/pallas_call | solution.py:111
  76.1 7.2 %collective-permute-done.11.refs_2_ = bf16[128,1792]{1,0:T(8,128)(2,1)} collective-permute-done((bf16[128,1792]{1,0:T(8,128)(2,1)}, bf16[128,1792]{1,0:T(8,128)(2,1)}, u32[]{:S(2)}, u32[]{:S(2)}) %collective-permute-start.11) | collective-permute-done | bytes 458784 | tf_op jit(solution)/shard_map/ppermute | solution.py:30
  83.3 2.2 %all-to-all-done.1 = bf16[32,8,1792]{2,1,0:T(8,128)(2,1)S(1)} async-done(((bf16[32,8,1792]{2,1,0:T(8,128)(2,1)}), bf16[32,8,1792]{2,1,0:T(8,128)(2,1)S(1)}, u32[]{:S(2)}, u32[]{:S(2)}) %all-to-all-start.1) | async-done | bytes 917536 | tf_op jit(solution)/shard_map/all_to_all | solution.py:367
  85.5 0.1 broadcast_in_dim.6.refs_6_
  85.6 5.0 %finish.1 = (f32[256,1792]{1,0:T(8,128)}, f32[256,1792]{1,0:T(8,128)}, bf16[128,14336]{1,0:T(8,128)(2,1)}) custom-call(bf16[128,1792]{1,0:T(8,128)(2,1)} %collective-permute-done.9.refs_0_, bf16[128,1792]{1,0:T(8,128)(2,1)} %collective-permute-done.10.refs_1_, bf16[128,1792]{1,0:T(8,128)(2,1)} %collective-permute-done.11.refs_2_, ...), custom_call_target="tpu_custom_call", output_to_operand_aliasing={{2}: (7, {})} | custom-call | flops 4587520 | bytes 11010048 | tf_op jit(solution)/shard_map/finish/pallas_call | solution.py:174
  (19 shorter events, 0.1 us)
Async XLA Ops:
  0.6 8.5 %copy-start = (f32[1,32,8,1792]{3,2,1,0:T(8,128)S(1)}, f32[1,32,8,1792]{3,2,1,0:T(8,128)}, u32[]{:S(2)}) copy-start(f32[1,32,8,1792]{3,2,1,0:T(8,128)} %param.7) | copy-start | bytes 5505028
  0.6 8.5 %copy-start.2 = (f32[1,32,8,1792]{3,2,1,0:T(8,128)S(1)}, f32[1,32,8,1792]{3,2,1,0:T(8,128)}, u32[]{:S(2)}) copy-start(f32[1,32,8,1792]{3,2,1,0:T(8,128)} %param.6) | copy-start | bytes 5505028
  4.0 17.9 %collective-permute-start.2 = (bf16[128,1792]{1,0:T(8,128)(2,1)}, bf16[128,1792]{1,0:T(8,128)(2,1)S(1)}, u32[]{:S(2)}, u32[]{:S(2)}) collective-permute-start(bf16[128,1792]{1,0:T(8,128)(2,1)} %get-tuple-element.25), channel_id=1, source_target_pairs={{0,32},{32,0},{64,96},{96,64},{128,160},{160,128},{192,224},{224,1... | collective-permute-start | bytes 1376264 | tf_op jit(solution)/shard_map/ppermute | solution.py:30
  7.1 14.8 %collective-permute-start.3 = (bf16[128,1792]{1,0:T(8,128)(2,1)S(1)}, bf16[128,1792]{1,0:T(8,128)(2,1)S(1)}, u32[]{:S(2)}, u32[]{:S(2)}) collective-permute-start(bf16[128,1792]{1,0:T(8,128)(2,1)S(1)} %get-tuple-element.27), channel_id=1, source_target_pairs={{0,64},{32,96},{64,128},{96,160},{128,192},{160,224},{192,0},{224,... | collective-permute-start | bytes 1376264 | tf_op jit(solution)/shard_map/ppermute | solution.py:30
  8.7 13.2 %collective-permute-start.4 = (bf16[128,1792]{1,0:T(8,128)(2,1)S(1)}, bf16[128,1792]{1,0:T(8,128)(2,1)}, u32[]{:S(2)}, u32[]{:S(2)}) collective-permute-start(bf16[128,1792]{1,0:T(8,128)(2,1)S(1)} %get-tuple-element.28), channel_id=1, source_target_pairs={{0,192},{32,224},{64,0},{96,32},{128,64},{160,96},{192,128},{224,1... | collective-permute-start | bytes 1376264 | tf_op jit(solution)/shard_map/ppermute | solution.py:30
  10.3 35.1 %all-to-all-start = ((bf16[32,8,1792]{2,1,0:T(8,128)(2,1)}), bf16[32,8,1792]{2,1,0:T(8,128)(2,1)}, u32[]{:S(2)}, u32[]{:S(2)}) async-start(bf16[32,8,1792]{2,1,0:T(8,128)(2,1)} %fusion), calls=%async_computation | async-start | bytes 1835008 | tf_op jit(solution)/shard_map/all_to_all | solution.py:347
  19.1 27.7 %collective-permute-start = (bf16[128,1792]{1,0:T(8,128)(2,1)}, bf16[128,1792]{1,0:T(8,128)(2,1)}, u32[]{:S(2)}, u32[]{:S(2)}) collective-permute-start(bf16[128,1792]{1,0:T(8,128)(2,1)} %get-tuple-element.22), channel_id=1, source_target_pairs={{0,64},{32,96},{64,128},{96,160},{128,192},{160,224},{192,0},{224,... | collective-permute-start | bytes 1376264 | tf_op jit(solution)/shard_map/ppermute | solution.py:30
  20.8 26.1 %collective-permute-start.1 = (bf16[128,1792]{1,0:T(8,128)(2,1)}, bf16[128,1792]{1,0:T(8,128)(2,1)}, u32[]{:S(2)}, u32[]{:S(2)}) collective-permute-start(bf16[128,1792]{1,0:T(8,128)(2,1)} %get-tuple-element.23), channel_id=1, source_target_pairs={{0,192},{32,224},{64,0},{96,32},{128,64},{160,96},{192,128},{224,1... | collective-permute-start | bytes 1376264 | tf_op jit(solution)/shard_map/ppermute | solution.py:30
  21.8 3.4 %copy-start.3 = (s32[32,24]{0,1:T(8,128)S(1)}, s32[32,24]{0,1:T(8,128)}, u32[]{:S(2)}) copy-start(s32[32,24]{0,1:T(8,128)} %param.8) | copy-start | bytes 9220
  21.8 3.5 %copy-start.4 = (s32[24,24]{1,0:T(8,128)S(1)}, s32[24,24]{1,0:T(8,128)}, u32[]{:S(2)}) copy-start(s32[24,24]{1,0:T(8,128)} %fusion.4) | copy-start | bytes 6916
  21.9 6.1 %copy-start.5 = (s32[32,32]{1,0:T(8,128)S(1)}, s32[32,32]{1,0:T(8,128)}, u32[]{:S(2)}) copy-start(s32[32,32]{1,0:T(8,128)} %param.9) | copy-start | bytes 12292
  23.2 23.7 %collective-permute-start.6 = (bf16[128,1792]{1,0:T(8,128)(2,1)S(1)}, bf16[128,1792]{1,0:T(8,128)(2,1)S(1)}, u32[]{:S(2)}, u32[]{:S(2)}) collective-permute-start(bf16[128,1792]{1,0:T(8,128)(2,1)S(1)} %get-tuple-element.30), channel_id=1, source_target_pairs={{0,32},{32,0},{64,96},{96,64},{128,160},{160,128},{192,224},{224,1... | collective-permute-start | bytes 1376264 | tf_op jit(solution)/shard_map/ppermute | solution.py:30
  25.6 21.3 %collective-permute-start.5 = (bf16[128,1792]{1,0:T(8,128)(2,1)S(1)}, bf16[128,1792]{1,0:T(8,128)(2,1)S(1)}, u32[]{:S(2)}, u32[]{:S(2)}) collective-permute-start(bf16[128,1792]{1,0:T(8,128)(2,1)S(1)} %get-tuple-element.29), channel_id=1, source_target_pairs={{0,128},{32,160},{64,192},{96,224},{128,0},{160,32},{192,64},{224,... | collective-permute-start | bytes 1376264 | tf_op jit(solution)/shard_map/ppermute | solution.py:30
  48.4 13.4 %collective-permute-start.8 = (bf16[128,1792]{1,0:T(8,128)(2,1)S(1)}, bf16[128,1792]{1,0:T(8,128)(2,1)}, u32[]{:S(2)}, u32[]{:S(2)}) collective-permute-start(bf16[128,1792]{1,0:T(8,128)(2,1)S(1)} %get-tuple-element.32.refs_0_), channel_id=1, source_target_pairs={{0,128},{32,160},{64,192},{96,224},{128,0},{160,32},{192,64},{224,... | collective-permute-start | bytes 1376264 | tf_op jit(solution)/shard_map/ppermute | solution.py:30
  50.8 13.6 %collective-permute-start.7 = (bf16[128,1792]{1,0:T(8,128)(2,1)S(1)}, bf16[128,1792]{1,0:T(8,128)(2,1)}, u32[]{:S(2)}, u32[]{:S(2)}) collective-permute-start(bf16[128,1792]{1,0:T(8,128)(2,1)S(1)} %get-tuple-element.32.refs_0_), channel_id=1, source_target_pairs={{0,32},{32,0},{64,96},{96,64},{128,160},{160,128},{192,224},{224,1... | collective-permute-start | bytes 1376264 | tf_op jit(solution)/shard_map/ppermute | solution.py:30
  54.2 31.3 %all-to-all-start.1 = ((bf16[32,8,1792]{2,1,0:T(8,128)(2,1)}), bf16[32,8,1792]{2,1,0:T(8,128)(2,1)S(1)}, u32[]{:S(2)}, u32[]{:S(2)}) async-start(bf16[32,8,1792]{2,1,0:T(8,128)(2,1)} %bitcast.5), calls=%async_computation.1 | async-start | bytes 1835008 | tf_op jit(solution)/shard_map/all_to_all | solution.py:367
  59.4 13.5 %collective-permute-start.13 = (bf16[128,1792]{1,0:T(8,128)(2,1)S(1)}, bf16[128,1792]{1,0:T(8,128)(2,1)}, u32[]{:S(2)}, u32[]{:S(2)}) collective-permute-start(bf16[128,1792]{1,0:T(8,128)(2,1)S(1)} %get-tuple-element.32.refs_0_), channel_id=1, source_target_pairs={{0,64},{32,96},{64,128},{96,160},{128,192},{160,224},{192,0},{224,... | collective-permute-start | bytes 1376264 | tf_op jit(solution)/shard_map/ppermute | solution.py:30
  59.8 13.5 %collective-permute-start.12 = (bf16[128,1792]{1,0:T(8,128)(2,1)S(1)}, bf16[128,1792]{1,0:T(8,128)(2,1)}, u32[]{:S(2)}, u32[]{:S(2)}) collective-permute-start(bf16[128,1792]{1,0:T(8,128)(2,1)S(1)} %get-tuple-element.32.refs_0_), channel_id=1, source_target_pairs={{0,192},{32,224},{64,0},{96,32},{128,64},{160,96},{192,128},{224,1... | collective-permute-start | bytes 1376264 | tf_op jit(solution)/shard_map/ppermute | solution.py:30
  64.4 18.9 %collective-permute-start.11 = (bf16[128,1792]{1,0:T(8,128)(2,1)}, bf16[128,1792]{1,0:T(8,128)(2,1)}, u32[]{:S(2)}, u32[]{:S(2)}) collective-permute-start(bf16[128,1792]{1,0:T(8,128)(2,1)} %get-tuple-element.34.refs_2_), channel_id=1, source_target_pairs={{0,32},{32,0},{64,96},{96,64},{128,160},{160,128},{192,224},{224,1... | collective-permute-start | bytes 1376264 | tf_op jit(solution)/shard_map/ppermute | solution.py:30
  67.4 15.9 %collective-permute-start.10 = (bf16[128,1792]{1,0:T(8,128)(2,1)}, bf16[128,1792]{1,0:T(8,128)(2,1)}, u32[]{:S(2)}, u32[]{:S(2)}) collective-permute-start(bf16[128,1792]{1,0:T(8,128)(2,1)} %get-tuple-element.33.refs_1_), channel_id=1, source_target_pairs={{0,64},{32,96},{64,128},{96,160},{128,192},{160,224},{192,0},{224,... | collective-permute-start | bytes 1376264 | tf_op jit(solution)/shard_map/ppermute | solution.py:30
  68.5 14.8 %collective-permute-start.9 = (bf16[128,1792]{1,0:T(8,128)(2,1)}, bf16[128,1792]{1,0:T(8,128)(2,1)}, u32[]{:S(2)}, u32[]{:S(2)}) collective-permute-start(bf16[128,1792]{1,0:T(8,128)(2,1)} %get-tuple-element.33.refs_1_), channel_id=1, source_target_pairs={{0,192},{32,224},{64,0},{96,32},{128,64},{160,96},{192,128},{224,1... | collective-permute-start | bytes 1376264 | tf_op jit(solution)/shard_map/ppermute | solution.py:30
  69.9 15.7 %copy-start.1 = (f32[1,32,8,1792]{3,2,1,0:T(8,128)S(1)}, f32[1,32,8,1792]{3,2,1,0:T(8,128)}, u32[]{:S(2)}) copy-start(f32[1,32,8,1792]{3,2,1,0:T(8,128)} %param.7) | copy-start | bytes 5505028

commit v5 on v4

--- a/solution.py
+++ b/solution.py
@@ -32,9 +32,7 @@
 
 def tables(block_lengths, block_owners, owner_count):
     block_count = block_lengths.shape[1]
-    block_ids = jnp.arange(block_count, dtype=jnp.int32)
-    before = (block_ids[None, :] < block_ids[:, None]).astype(jnp.int32)
-    offsets = jnp.sum(before[None] * block_lengths[:, None, :], axis=2)
+    offsets = jnp.cumsum(block_lengths, axis=1) - block_lengths
     heads = block_owners[:, :block_count]
     owner_ids = jnp.arange(owner_count, dtype=jnp.int32)
     match = (heads[:, :, None] == owner_ids[None, None, :]).astype(jnp.int32)

time: 91.1 us -> 91.2 us (level)
  transfers between devices with their start and end apart: 16 -> 16, of which waited for: 7 -> 7; matrix products, arithmetic and copies ran while one was open for 4% -> 3% of each run, Pallas kernels for 8% -> 8%
where the time goes in v5:
time: 91.2 us; the launch traced here: 90.7 us
  starting transfers between devices  37.7 us (41%)
  waiting for transfers between devices  32.7 us (36%)
  Pallas kernels  16.8 us (18%)
  other arithmetic  2.11 us (2%)
    ppermute x14, starting transfers between devices, send(): lax.ppermute(array, 'replica', [(i, place(i, step)) for i in range(8)])  23.8 us
    all_to_all x1, waiting for transfers between devices, body(): lax.all_to_all(base, 'fsdp', split_axis=0, concat_axis=0, tiled=True)  17.4 us
    ppermute x14, waiting for transfers between devices, send(): lax.ppermute(array, 'replica', [(i, place(i, step)) for i in range(8)])  13.1 us
    all_to_all x1, starting transfers between devices, body(): lax.all_to_all(base, 'fsdp', split_axis=0, concat_axis=0, tiled=True)  8.81 us
    all_to_all x1, starting transfers between devices, body(): lax.all_to_all(packed.reshape(fsdp_count, slots, columns), 'fsdp', split_...  5.11 us
    pallas_call x1, Pallas kernels, finish(): pl.pallas_call(kernel, grid=(blocks,), out_shape=[jax.ShapeDtypeStruct((s...  5.02 us
    pallas_call x1, Pallas kernels, split_columns(): pl.pallas_call(kernel, out_shape=[jax.ShapeDtypeStruct((row_count, column...  3.32 us
    pallas_call x1, Pallas kernels, join_columns(): pl.pallas_call(kernel, out_shape=jax.ShapeDtypeStruct((row_count, columns...  2.85 us
  transfers between devices with their start and end apart: 16, of which 7 were waited for; matrix products, arithmetic and copies ran while one was open for 3% of the time, Pallas kernels for 8%

profile of v5, /device:TPU:40, one launch (start us, length us, event | category | flops | bytes accessed | tf_op | source)
XLA Modules:
  0.0 90.7 jit_solution(13662901769923925233)
XLA Ops:
  0.6 0.0 copy-start
  0.6 0.0 copy-start.2
  0.7 3.3 %split_columns.1 = (bf16[128,1792]{1,0:T(8,128)(2,1)S(1)}, bf16[128,1792]{1,0:T(8,128)(2,1)}, bf16[128,1792]{1,0:T(8,128)(2,1)}, bf16[128,1792]{1,0:T(8,128)(2,1...) custom-call(bf16[128,14336]{1,0:T(8,128)(2,1)} %bitcast.18), custom_call_target="tpu_custom_call" | custom-call | bytes 7340032 | tf_op jit(solution)/shard_map/split_columns/pallas_call | solution.py:67
  4.0 3.1 %collective-permute-start.2 = (bf16[128,1792]{1,0:T(8,128)(2,1)}, bf16[128,1792]{1,0:T(8,128)(2,1)S(1)}, u32[]{:S(2)}, u32[]{:S(2)}) collective-permute-start(bf16[128,1792]{1,0:T(8,128)(2,1)} %get-tuple-element.25), channel_id=1, source_target_pairs={{0,32},{32,0},{64,96},{96,64},{128,160},{160,128},{192,224},{224,1... | collective-permute-start | bytes 1376264 | tf_op jit(solution)/shard_map/ppermute | solution.py:30
  7.1 1.6 %collective-permute-start.3 = (bf16[128,1792]{1,0:T(8,128)(2,1)S(1)}, bf16[128,1792]{1,0:T(8,128)(2,1)S(1)}, u32[]{:S(2)}, u32[]{:S(2)}) collective-permute-start(bf16[128,1792]{1,0:T(8,128)(2,1)S(1)} %get-tuple-element.27), channel_id=1, source_target_pairs={{0,64},{32,96},{64,128},{96,160},{128,192},{160,224},{192,0},{224,... | collective-permute-start | bytes 1376264 | tf_op jit(solution)/shard_map/ppermute | solution.py:30
  8.7 0.4 collective-permute-start.4
  9.1 1.2 %fusion = bf16[32,8,1792]{2,1,0:T(8,128)(2,1)} fusion(f32[1,32,8,1792]{3,2,1,0:T(8,128)S(1)} %copy-done, f32[1,32,8,1792]{3,2,1,0:T(8,128)S(1)} %copy-done.2), kind=kLoop, calls=%fused_computation.1 | loop fusion | flops 1835008 | bytes 4587520 | tf_op jit(solution)/shard_map/convert_element_type | solution.py:344
  10.3 8.8 %all-to-all-start = ((bf16[32,8,1792]{2,1,0:T(8,128)(2,1)}), bf16[32,8,1792]{2,1,0:T(8,128)(2,1)}, u32[]{:S(2)}, u32[]{:S(2)}) async-start(bf16[32,8,1792]{2,1,0:T(8,128)(2,1)} %fusion), calls=%async_computation | async-start | bytes 1835008 | tf_op jit(solution)/shard_map/all_to_all | solution.py:345
  19.1 1.7 %collective-permute-start = (bf16[128,1792]{1,0:T(8,128)(2,1)}, bf16[128,1792]{1,0:T(8,128)(2,1)}, u32[]{:S(2)}, u32[]{:S(2)}) collective-permute-start(bf16[128,1792]{1,0:T(8,128)(2,1)} %get-tuple-element.22), channel_id=1, source_target_pairs={{0,64},{32,96},{64,128},{96,160},{128,192},{160,224},{192,0},{224,... | collective-permute-start | bytes 1376264 | tf_op jit(solution)/shard_map/ppermute | solution.py:30
  20.8 0.5 collective-permute-start.1
  21.2 0.0 collective-permute-done.3.refs_3_
  21.2 0.0 collective-permute-done.4.refs_4_
  21.2 0.0 copy-start.4
  21.3 0.0 copy-start.3
  21.3 1.3 %partial_sums.1 = (bf16[128,1792]{1,0:T(8,128)(2,1)S(1)}, bf16[128,1792]{1,0:T(8,128)(2,1)S(1)}) custom-call(bf16[128,1792]{1,0:T(8,128)(2,1)S(1)} %get-tuple-element.24.refs_0_, bf16[128,1792]{1,0:T(8,128)(2,1)S(1)} %collective-permute-done.2.refs_1_, bf16[128,1792]{1,0:T(8,128)(2,1)S(1)} %get-tuple-element.26.refs_2_, ...), custom_call_target="tpu_custom_call" | custom-call | flops 1150000037888 | bytes 3211264 | tf_op jit(solution)/shard_map/partial_sums/pallas_call | solution.py:248
  22.6 2.1 %collective-permute-start.6 = (bf16[128,1792]{1,0:T(8,128)(2,1)S(1)}, bf16[128,1792]{1,0:T(8,128)(2,1)S(1)}, u32[]{:S(2)}, u32[]{:S(2)}) collective-permute-start(bf16[128,1792]{1,0:T(8,128)(2,1)S(1)} %get-tuple-element.30), channel_id=1, source_target_pairs={{0,32},{32,0},{64,96},{96,64},{128,160},{160,128},{192,224},{224,1... | collective-permute-start | bytes 1376264 | tf_op jit(solution)/shard_map/ppermute | solution.py:30
  24.7 0.1 copy.20
  24.7 0.2 reduce_window_sum.11
  24.9 2.4 %collective-permute-start.5 = (bf16[128,1792]{1,0:T(8,128)(2,1)S(1)}, bf16[128,1792]{1,0:T(8,128)(2,1)S(1)}, u32[]{:S(2)}, u32[]{:S(2)}) collective-permute-start(bf16[128,1792]{1,0:T(8,128)(2,1)S(1)} %get-tuple-element.29), channel_id=1, source_target_pairs={{0,128},{32,160},{64,192},{96,224},{128,0},{160,32},{192,64},{224,... | collective-permute-start | bytes 1376264 | tf_op jit(solution)/shard_map/ppermute | solution.py:30
  27.3 0.5 select_reduce_fusion.1
  27.8 0.1 add_select_fusion
  27.9 0.1 select_n.24
  28.0 17.4 %all-to-all-done = bf16[32,8,1792]{2,1,0:T(8,128)(2,1)} async-done(((bf16[32,8,1792]{2,1,0:T(8,128)(2,1)}), bf16[32,8,1792]{2,1,0:T(8,128)(2,1)}, u32[]{:S(2)}, u32[]{:S(2)}) %all-to-all-start) | async-done | bytes 917536 | tf_op jit(solution)/shard_map/all_to_all | solution.py:345
  45.4 1.5 %own_share.1.refs_5_ = bf16[128,1792]{1,0:T(8,128)(2,1)S(1)} custom-call(bf16[128,256]{1,0:T(8,128)(2,1)S(1)} %fusion.1.pick_ref, bf16[256,1792]{1,0:T(8,128)(2,1)} %bitcast.4.array_ref), custom_call_target="tpu_custom_call" | custom-call | flops 117440512 | bytes 1376256 | tf_op jit(solution)/shard_map/own_share/pallas_call | solution.py:274
  46.9 1.5 %fresh_rows.1 = (bf16[128,1792]{1,0:T(8,128)(2,1)S(1)}, bf16[128,1792]{1,0:T(8,128)(2,1)S(1)}) custom-call(bf16[128,1792]{1,0:T(8,128)(2,1)S(1)} %get-tuple-element.21.refs_0_, bf16[128,1792]{1,0:T(8,128)(2,1)} %collective-permute-done.refs_1_, bf16[128,1792]{1,0:T(8,128)(2,1)} %collective-permute-done.1.refs_2_, ...), custom_call_target="tpu_custom_call" | custom-call | flops 1605632 | bytes 3670016 | tf_op jit(solution)/shard_map/fresh_rows/pallas_call | solution.py:215
  48.4 2.4 %collective-permute-start.8 = (bf16[128,1792]{1,0:T(8,128)(2,1)S(1)}, bf16[128,1792]{1,0:T(8,128)(2,1)}, u32[]{:S(2)}, u32[]{:S(2)}) collective-permute-start(bf16[128,1792]{1,0:T(8,128)(2,1)S(1)} %get-tuple-element.32.refs_0_), channel_id=1, source_target_pairs={{0,128},{32,160},{64,192},{96,224},{128,0},{160,32},{192,64},{224,... | collective-permute-start | bytes 1376264 | tf_op jit(solution)/shard_map/ppermute | solution.py:30
  50.8 2.0 %collective-permute-start.7 = (bf16[128,1792]{1,0:T(8,128)(2,1)S(1)}, bf16[128,1792]{1,0:T(8,128)(2,1)}, u32[]{:S(2)}, u32[]{:S(2)}) collective-permute-start(bf16[128,1792]{1,0:T(8,128)(2,1)S(1)} %get-tuple-element.32.refs_0_), channel_id=1, source_target_pairs={{0,32},{32,0},{64,96},{96,64},{128,160},{160,128},{192,224},{224,1... | collective-permute-start | bytes 1376264 | tf_op jit(solution)/shard_map/ppermute | solution.py:30
  52.8 0.1 fusion.2.pick_ref
  52.9 1.3 %pack_slots.1 = bf16[256,1792]{1,0:T(8,128)(2,1)} custom-call(bf16[256,128]{1,0:T(8,128)(2,1)S(1)} %fusion.2.pick_ref, bf16[128,1792]{1,0:T(8,128)(2,1)S(1)} %get-tuple-element.35.array_ref), custom_call_target="tpu_custom_call" | custom-call | flops 117440512 | bytes 1376256 | tf_op jit(solution)/shard_map/pack_slots/pallas_call | solution.py:274
  54.3 5.1 %all-to-all-start.1 = ((bf16[32,8,1792]{2,1,0:T(8,128)(2,1)}), bf16[32,8,1792]{2,1,0:T(8,128)(2,1)S(1)}, u32[]{:S(2)}, u32[]{:S(2)}) async-start(bf16[32,8,1792]{2,1,0:T(8,128)(2,1)} %bitcast.5), calls=%async_computation.1 | async-start | bytes 1835008 | tf_op jit(solution)/shard_map/all_to_all | solution.py:365
  59.4 0.1 collective-permute-start.13
  59.5 2.0 %collective-permute-start.12 = (bf16[128,1792]{1,0:T(8,128)(2,1)S(1)}, bf16[128,1792]{1,0:T(8,128)(2,1)}, u32[]{:S(2)}, u32[]{:S(2)}) collective-permute-start(bf16[128,1792]{1,0:T(8,128)(2,1)S(1)} %get-tuple-element.32.refs_0_), channel_id=1, source_target_pairs={{0,192},{32,224},{64,0},{96,32},{128,64},{160,96},{192,128},{224,1... | collective-permute-start | bytes 1376264 | tf_op jit(solution)/shard_map/ppermute | solution.py:30
  61.5 0.4 collective-permute-done.8.refs_1_
  61.9 2.5 %collective-permute-done.7.refs_0_ = bf16[128,1792]{1,0:T(8,128)(2,1)} collective-permute-done((bf16[128,1792]{1,0:T(8,128)(2,1)S(1)}, bf16[128,1792]{1,0:T(8,128)(2,1)}, u32[]{:S(2)}, u32[]{:S(2)}) %collective-permute-start.7) | collective-permute-done | bytes 458784 | tf_op jit(solution)/shard_map/ppermute | solution.py:30
  64.4 3.0 %collective-permute-start.11 = (bf16[128,1792]{1,0:T(8,128)(2,1)}, bf16[128,1792]{1,0:T(8,128)(2,1)}, u32[]{:S(2)}, u32[]{:S(2)}) collective-permute-start(bf16[128,1792]{1,0:T(8,128)(2,1)} %get-tuple-element.34.refs_2_), channel_id=1, source_target_pairs={{0,32},{32,0},{64,96},{96,64},{128,160},{160,128},{192,224},{224,1... | collective-permute-start | bytes 1376264 | tf_op jit(solution)/shard_map/ppermute | solution.py:30
  67.4 1.2 %collective-permute-start.10 = (bf16[128,1792]{1,0:T(8,128)(2,1)}, bf16[128,1792]{1,0:T(8,128)(2,1)}, u32[]{:S(2)}, u32[]{:S(2)}) collective-permute-start(bf16[128,1792]{1,0:T(8,128)(2,1)} %get-tuple-element.33.refs_1_), channel_id=1, source_target_pairs={{0,64},{32,96},{64,128},{96,160},{128,192},{160,224},{192,0},{224,... | collective-permute-start | bytes 1376264 | tf_op jit(solution)/shard_map/ppermute | solution.py:30
  68.6 1.3 %collective-permute-start.9 = (bf16[128,1792]{1,0:T(8,128)(2,1)}, bf16[128,1792]{1,0:T(8,128)(2,1)}, u32[]{:S(2)}, u32[]{:S(2)}) collective-permute-start(bf16[128,1792]{1,0:T(8,128)(2,1)} %get-tuple-element.33.refs_1_), channel_id=1, source_target_pairs={{0,192},{32,224},{64,0},{96,32},{128,64},{160,96},{192,128},{224,1... | collective-permute-start | bytes 1376264 | tf_op jit(solution)/shard_map/ppermute | solution.py:30
  69.9 0.2 dynamic-slice_reduce_fusion
  70.1 0.1 fusion.3
  70.2 0.1 reshape.115
  70.3 0.0 copy-start.1
  70.3 2.6 %collective-permute-done.13.refs_4_ = bf16[128,1792]{1,0:T(8,128)(2,1)} collective-permute-done((bf16[128,1792]{1,0:T(8,128)(2,1)S(1)}, bf16[128,1792]{1,0:T(8,128)(2,1)}, u32[]{:S(2)}, u32[]{:S(2)}) %collective-permute-start.13) | collective-permute-done | bytes 458784 | tf_op jit(solution)/shard_map/ppermute | solution.py:30
  72.9 0.1 collective-permute-done.12.refs_3_
  73.0 2.8 %join_columns.1.refs_7_ = bf16[128,14336]{1,0:T(8,128)(2,1)} custom-call(bf16[128,1792]{1,0:T(8,128)(2,1)S(1)} %get-tuple-element.32.refs_0_, bf16[128,1792]{1,0:T(8,128)(2,1)} %get-tuple-element.33.refs_1_, bf16[128,1792]{1,0:T(8,128)(2,1)} %get-tuple-element.34.refs_2_, bf16[128,1792]{1,0:T(8,128)(2,1)} %collective-permute-done.12.refs_3_, ...), custom_call_target="tpu_custom_call" | custom-call | bytes 4587520 | tf_op jit(solution)/shard_map/join_columns/pallas_call | solution.py:109
  75.9 7.5 %collective-permute-done.11.refs_2_ = bf16[128,1792]{1,0:T(8,128)(2,1)} collective-permute-done((bf16[128,1792]{1,0:T(8,128)(2,1)}, bf16[128,1792]{1,0:T(8,128)(2,1)}, u32[]{:S(2)}, u32[]{:S(2)}) %collective-permute-start.11) | collective-permute-done | bytes 458784 | tf_op jit(solution)/shard_map/ppermute | solution.py:30
  83.3 2.2 %all-to-all-done.1 = bf16[32,8,1792]{2,1,0:T(8,128)(2,1)S(1)} async-done(((bf16[32,8,1792]{2,1,0:T(8,128)(2,1)}), bf16[32,8,1792]{2,1,0:T(8,128)(2,1)S(1)}, u32[]{:S(2)}, u32[]{:S(2)}) %all-to-all-start.1) | async-done | bytes 917536 | tf_op jit(solution)/shard_map/all_to_all | solution.py:365
  85.6 0.1 broadcast_in_dim.6.refs_6_
  85.7 5.0 %finish.1 = (f32[256,1792]{1,0:T(8,128)}, f32[256,1792]{1,0:T(8,128)}, bf16[128,14336]{1,0:T(8,128)(2,1)}) custom-call(bf16[128,1792]{1,0:T(8,128)(2,1)} %collective-permute-done.9.refs_0_, bf16[128,1792]{1,0:T(8,128)(2,1)} %collective-permute-done.10.refs_1_, bf16[128,1792]{1,0:T(8,128)(2,1)} %collective-permute-done.11.refs_2_, ...), custom_call_target="tpu_custom_call", output_to_operand_aliasing={{2}: (7, {})} | custom-call | flops 4587520 | bytes 11010048 | tf_op jit(solution)/shard_map/finish/pallas_call | solution.py:172
  (16 shorter events, 0.1 us)
Async XLA Ops:
  0.6 8.5 %copy-start = (f32[1,32,8,1792]{3,2,1,0:T(8,128)S(1)}, f32[1,32,8,1792]{3,2,1,0:T(8,128)}, u32[]{:S(2)}) copy-start(f32[1,32,8,1792]{3,2,1,0:T(8,128)} %param.7) | copy-start | bytes 5505028
  0.6 8.5 %copy-start.2 = (f32[1,32,8,1792]{3,2,1,0:T(8,128)S(1)}, f32[1,32,8,1792]{3,2,1,0:T(8,128)}, u32[]{:S(2)}) copy-start(f32[1,32,8,1792]{3,2,1,0:T(8,128)} %param.6) | copy-start | bytes 5505028
  4.0 17.3 %collective-permute-start.2 = (bf16[128,1792]{1,0:T(8,128)(2,1)}, bf16[128,1792]{1,0:T(8,128)(2,1)S(1)}, u32[]{:S(2)}, u32[]{:S(2)}) collective-permute-start(bf16[128,1792]{1,0:T(8,128)(2,1)} %get-tuple-element.25), channel_id=1, source_target_pairs={{0,32},{32,0},{64,96},{96,64},{128,160},{160,128},{192,224},{224,1... | collective-permute-start | bytes 1376264 | tf_op jit(solution)/shard_map/ppermute | solution.py:30
  7.1 14.1 %collective-permute-start.3 = (bf16[128,1792]{1,0:T(8,128)(2,1)S(1)}, bf16[128,1792]{1,0:T(8,128)(2,1)S(1)}, u32[]{:S(2)}, u32[]{:S(2)}) collective-permute-start(bf16[128,1792]{1,0:T(8,128)(2,1)S(1)} %get-tuple-element.27), channel_id=1, source_target_pairs={{0,64},{32,96},{64,128},{96,160},{128,192},{160,224},{192,0},{224,... | collective-permute-start | bytes 1376264 | tf_op jit(solution)/shard_map/ppermute | solution.py:30
  8.7 12.6 %collective-permute-start.4 = (bf16[128,1792]{1,0:T(8,128)(2,1)S(1)}, bf16[128,1792]{1,0:T(8,128)(2,1)}, u32[]{:S(2)}, u32[]{:S(2)}) collective-permute-start(bf16[128,1792]{1,0:T(8,128)(2,1)S(1)} %get-tuple-element.28), channel_id=1, source_target_pairs={{0,192},{32,224},{64,0},{96,32},{128,64},{160,96},{192,128},{224,1... | collective-permute-start | bytes 1376264 | tf_op jit(solution)/shard_map/ppermute | solution.py:30
  10.3 35.1 %all-to-all-start = ((bf16[32,8,1792]{2,1,0:T(8,128)(2,1)}), bf16[32,8,1792]{2,1,0:T(8,128)(2,1)}, u32[]{:S(2)}, u32[]{:S(2)}) async-start(bf16[32,8,1792]{2,1,0:T(8,128)(2,1)} %fusion), calls=%async_computation | async-start | bytes 1835008 | tf_op jit(solution)/shard_map/all_to_all | solution.py:345
  19.1 27.7 %collective-permute-start = (bf16[128,1792]{1,0:T(8,128)(2,1)}, bf16[128,1792]{1,0:T(8,128)(2,1)}, u32[]{:S(2)}, u32[]{:S(2)}) collective-permute-start(bf16[128,1792]{1,0:T(8,128)(2,1)} %get-tuple-element.22), channel_id=1, source_target_pairs={{0,64},{32,96},{64,128},{96,160},{128,192},{160,224},{192,0},{224,... | collective-permute-start | bytes 1376264 | tf_op jit(solution)/shard_map/ppermute | solution.py:30
  20.8 26.1 %collective-permute-start.1 = (bf16[128,1792]{1,0:T(8,128)(2,1)}, bf16[128,1792]{1,0:T(8,128)(2,1)}, u32[]{:S(2)}, u32[]{:S(2)}) collective-permute-start(bf16[128,1792]{1,0:T(8,128)(2,1)} %get-tuple-element.23), channel_id=1, source_target_pairs={{0,192},{32,224},{64,0},{96,32},{128,64},{160,96},{192,128},{224,1... | collective-permute-start | bytes 1376264 | tf_op jit(solution)/shard_map/ppermute | solution.py:30
  21.2 3.4 %copy-start.4 = (s32[32,24]{0,1:T(8,128)S(1)}, s32[32,24]{0,1:T(8,128)}, u32[]{:S(2)}) copy-start(s32[32,24]{0,1:T(8,128)} %param.8) | copy-start | bytes 9220
  21.3 6.0 %copy-start.3 = (s32[32,32]{1,0:T(8,128)S(1)}, s32[32,32]{1,0:T(8,128)}, u32[]{:S(2)}) copy-start(s32[32,32]{1,0:T(8,128)} %param.9) | copy-start | bytes 12292
  22.6 24.3 %collective-permute-start.6 = (bf16[128,1792]{1,0:T(8,128)(2,1)S(1)}, bf16[128,1792]{1,0:T(8,128)(2,1)S(1)}, u32[]{:S(2)}, u32[]{:S(2)}) collective-permute-start(bf16[128,1792]{1,0:T(8,128)(2,1)S(1)} %get-tuple-element.30), channel_id=1, source_target_pairs={{0,32},{32,0},{64,96},{96,64},{128,160},{160,128},{192,224},{224,1... | collective-permute-start | bytes 1376264 | tf_op jit(solution)/shard_map/ppermute | solution.py:30
  24.9 21.9 %collective-permute-start.5 = (bf16[128,1792]{1,0:T(8,128)(2,1)S(1)}, bf16[128,1792]{1,0:T(8,128)(2,1)S(1)}, u32[]{:S(2)}, u32[]{:S(2)}) collective-permute-start(bf16[128,1792]{1,0:T(8,128)(2,1)S(1)} %get-tuple-element.29), channel_id=1, source_target_pairs={{0,128},{32,160},{64,192},{96,224},{128,0},{160,32},{192,64},{224,... | collective-permute-start | bytes 1376264 | tf_op jit(solution)/shard_map/ppermute | solution.py:30
  48.4 13.4 %collective-permute-start.8 = (bf16[128,1792]{1,0:T(8,128)(2,1)S(1)}, bf16[128,1792]{1,0:T(8,128)(2,1)}, u32[]{:S(2)}, u32[]{:S(2)}) collective-permute-start(bf16[128,1792]{1,0:T(8,128)(2,1)S(1)} %get-tuple-element.32.refs_0_), channel_id=1, source_target_pairs={{0,128},{32,160},{64,192},{96,224},{128,0},{160,32},{192,64},{224,... | collective-permute-start | bytes 1376264 | tf_op jit(solution)/shard_map/ppermute | solution.py:30
  50.8 13.6 %collective-permute-start.7 = (bf16[128,1792]{1,0:T(8,128)(2,1)S(1)}, bf16[128,1792]{1,0:T(8,128)(2,1)}, u32[]{:S(2)}, u32[]{:S(2)}) collective-permute-start(bf16[128,1792]{1,0:T(8,128)(2,1)S(1)} %get-tuple-element.32.refs_0_), channel_id=1, source_target_pairs={{0,32},{32,0},{64,96},{96,64},{128,160},{160,128},{192,224},{224,1... | collective-permute-start | bytes 1376264 | tf_op jit(solution)/shard_map/ppermute | solution.py:30
  54.3 31.3 %all-to-all-start.1 = ((bf16[32,8,1792]{2,1,0:T(8,128)(2,1)}), bf16[32,8,1792]{2,1,0:T(8,128)(2,1)S(1)}, u32[]{:S(2)}, u32[]{:S(2)}) async-start(bf16[32,8,1792]{2,1,0:T(8,128)(2,1)} %bitcast.5), calls=%async_computation.1 | async-start | bytes 1835008 | tf_op jit(solution)/shard_map/all_to_all | solution.py:365
  59.4 13.5 %collective-permute-start.13 = (bf16[128,1792]{1,0:T(8,128)(2,1)S(1)}, bf16[128,1792]{1,0:T(8,128)(2,1)}, u32[]{:S(2)}, u32[]{:S(2)}) collective-permute-start(bf16[128,1792]{1,0:T(8,128)(2,1)S(1)} %get-tuple-element.32.refs_0_), channel_id=1, source_target_pairs={{0,64},{32,96},{64,128},{96,160},{128,192},{160,224},{192,0},{224,... | collective-permute-start | bytes 1376264 | tf_op jit(solution)/shard_map/ppermute | solution.py:30
  59.5 13.5 %collective-permute-start.12 = (bf16[128,1792]{1,0:T(8,128)(2,1)S(1)}, bf16[128,1792]{1,0:T(8,128)(2,1)}, u32[]{:S(2)}, u32[]{:S(2)}) collective-permute-start(bf16[128,1792]{1,0:T(8,128)(2,1)S(1)} %get-tuple-element.32.refs_0_), channel_id=1, source_target_pairs={{0,192},{32,224},{64,0},{96,32},{128,64},{160,96},{192,128},{224,1... | collective-permute-start | bytes 1376264 | tf_op jit(solution)/shard_map/ppermute | solution.py:30
  64.4 18.9 %collective-permute-start.11 = (bf16[128,1792]{1,0:T(8,128)(2,1)}, bf16[128,1792]{1,0:T(8,128)(2,1)}, u32[]{:S(2)}, u32[]{:S(2)}) collective-permute-start(bf16[128,1792]{1,0:T(8,128)(2,1)} %get-tuple-element.34.refs_2_), channel_id=1, source_target_pairs={{0,32},{32,0},{64,96},{96,64},{128,160},{160,128},{192,224},{224,1... | collective-permute-start | bytes 1376264 | tf_op jit(solution)/shard_map/ppermute | solution.py:30
  67.4 15.9 %collective-permute-start.10 = (bf16[128,1792]{1,0:T(8,128)(2,1)}, bf16[128,1792]{1,0:T(8,128)(2,1)}, u32[]{:S(2)}, u32[]{:S(2)}) collective-permute-start(bf16[128,1792]{1,0:T(8,128)(2,1)} %get-tuple-element.33.refs_1_), channel_id=1, source_target_pairs={{0,64},{32,96},{64,128},{96,160},{128,192},{160,224},{192,0},{224,... | collective-permute-start | bytes 1376264 | tf_op jit(solution)/shard_map/ppermute | solution.py:30
  68.6 14.7 %collective-permute-start.9 = (bf16[128,1792]{1,0:T(8,128)(2,1)}, bf16[128,1792]{1,0:T(8,128)(2,1)}, u32[]{:S(2)}, u32[]{:S(2)}) collective-permute-start(bf16[128,1792]{1,0:T(8,128)(2,1)} %get-tuple-element.33.refs_1_), channel_id=1, source_target_pairs={{0,192},{32,224},{64,0},{96,32},{128,64},{160,96},{192,128},{224,1... | collective-permute-start | bytes 1376264 | tf_op jit(solution)/shard_map/ppermute | solution.py:30
  70.3 15.4 %copy-start.1 = (f32[1,32,8,1792]{3,2,1,0:T(8,128)S(1)}, f32[1,32,8,1792]{3,2,1,0:T(8,128)}, u32[]{:S(2)}) copy-start(f32[1,32,8,1792]{3,2,1,0:T(8,128)} %param.7) | copy-start | bytes 5505028

commit v6 on v5

--- a/solution.py
+++ b/solution.py
@@ -125,7 +125,7 @@
     steps = list(chunks)
     row_count, columns = chunks[steps[0]].shape
     slot_count = arrived.shape[0]
-    blocks = 4
+    blocks = 8
     rows = slot_count // blocks
 
     def kernel(*refs):

time: 91.2 us -> 93.2 us (1.022)
  Pallas kernels: 16.8 us -> 18.8 us
    pallas_call x1, Pallas kernels: 5.02 us -> 6.99 us  [finish(): pl.pallas_call(kernel, grid=(blocks,), out_shape=[jax.ShapeDtypeStruct((s...]
  transfers between devices with their start and end apart: 16 -> 16, of which waited for: 7 -> 7; matrix products, arithmetic and copies ran while one was open for 3% -> 3% of each run, Pallas kernels for 8% -> 7%
where the time goes in v6:
time: 93.2 us; the launch traced here: 92.7 us
  starting transfers between devices  37.7 us (40%)
  waiting for transfers between devices  32.7 us (35%)
  Pallas kernels  18.8 us (20%)
  other arithmetic  2.11 us (2%)
    ppermute x14, starting transfers between devices, send(): lax.ppermute(array, 'replica', [(i, place(i, step)) for i in range(8)])  23.8 us
    all_to_all x1, waiting for transfers between devices, body(): lax.all_to_all(base, 'fsdp', split_axis=0, concat_axis=0, tiled=True)  17.4 us
    ppermute x14, waiting for transfers between devices, send(): lax.ppermute(array, 'replica', [(i, place(i, step)) for i in range(8)])  13.1 us
    all_to_all x1, starting transfers between devices, body(): lax.all_to_all(base, 'fsdp', split_axis=0, concat_axis=0, tiled=True)  8.81 us
    pallas_call x1, Pallas kernels, finish(): pl.pallas_call(kernel, grid=(blocks,), out_shape=[jax.ShapeDtypeStruct((s...  6.99 us
    all_to_all x1, starting transfers between devices, body(): lax.all_to_all(packed.reshape(fsdp_count, slots, columns), 'fsdp', split_...  5.11 us
    pallas_call x1, Pallas kernels, split_columns(): pl.pallas_call(kernel, out_shape=[jax.ShapeDtypeStruct((row_count, column...  3.32 us
    pallas_call x1, Pallas kernels, join_columns(): pl.pallas_call(kernel, out_shape=jax.ShapeDtypeStruct((row_count, columns...  2.85 us
  transfers between devices with their start and end apart: 16, of which 7 were waited for; matrix products, arithmetic and copies ran while one was open for 3% of the time, Pallas kernels for 7%

profile of v6, /device:TPU:40, one launch (start us, length us, event | category | flops | bytes accessed | tf_op | source)
XLA Modules:
  0.0 92.7 jit_solution(8026787323265810980)
XLA Ops:
  0.6 0.0 copy-start
  0.6 0.0 copy-start.2
  0.7 3.3 %split_columns.1 = (bf16[128,1792]{1,0:T(8,128)(2,1)S(1)}, bf16[128,1792]{1,0:T(8,128)(2,1)}, bf16[128,1792]{1,0:T(8,128)(2,1)}, bf16[128,1792]{1,0:T(8,128)(2,1...) custom-call(bf16[128,14336]{1,0:T(8,128)(2,1)} %bitcast.18), custom_call_target="tpu_custom_call" | custom-call | bytes 7340032 | tf_op jit(solution)/shard_map/split_columns/pallas_call | solution.py:67
  4.0 3.1 %collective-permute-start.2 = (bf16[128,1792]{1,0:T(8,128)(2,1)}, bf16[128,1792]{1,0:T(8,128)(2,1)S(1)}, u32[]{:S(2)}, u32[]{:S(2)}) collective-permute-start(bf16[128,1792]{1,0:T(8,128)(2,1)} %get-tuple-element.25), channel_id=1, source_target_pairs={{0,32},{32,0},{64,96},{96,64},{128,160},{160,128},{192,224},{224,1... | collective-permute-start | bytes 1376264 | tf_op jit(solution)/shard_map/ppermute | solution.py:30
  7.1 1.6 %collective-permute-start.3 = (bf16[128,1792]{1,0:T(8,128)(2,1)S(1)}, bf16[128,1792]{1,0:T(8,128)(2,1)S(1)}, u32[]{:S(2)}, u32[]{:S(2)}) collective-permute-start(bf16[128,1792]{1,0:T(8,128)(2,1)S(1)} %get-tuple-element.27), channel_id=1, source_target_pairs={{0,64},{32,96},{64,128},{96,160},{128,192},{160,224},{192,0},{224,... | collective-permute-start | bytes 1376264 | tf_op jit(solution)/shard_map/ppermute | solution.py:30
  8.7 0.4 collective-permute-start.4
  9.1 1.2 %fusion = bf16[32,8,1792]{2,1,0:T(8,128)(2,1)} fusion(f32[1,32,8,1792]{3,2,1,0:T(8,128)S(1)} %copy-done, f32[1,32,8,1792]{3,2,1,0:T(8,128)S(1)} %copy-done.2), kind=kLoop, calls=%fused_computation.1 | loop fusion | flops 1835008 | bytes 4587520 | tf_op jit(solution)/shard_map/convert_element_type | solution.py:344
  10.3 8.8 %all-to-all-start = ((bf16[32,8,1792]{2,1,0:T(8,128)(2,1)}), bf16[32,8,1792]{2,1,0:T(8,128)(2,1)}, u32[]{:S(2)}, u32[]{:S(2)}) async-start(bf16[32,8,1792]{2,1,0:T(8,128)(2,1)} %fusion), calls=%async_computation | async-start | bytes 1835008 | tf_op jit(solution)/shard_map/all_to_all | solution.py:345
  19.1 1.7 %collective-permute-start = (bf16[128,1792]{1,0:T(8,128)(2,1)}, bf16[128,1792]{1,0:T(8,128)(2,1)}, u32[]{:S(2)}, u32[]{:S(2)}) collective-permute-start(bf16[128,1792]{1,0:T(8,128)(2,1)} %get-tuple-element.22), channel_id=1, source_target_pairs={{0,64},{32,96},{64,128},{96,160},{128,192},{160,224},{192,0},{224,... | collective-permute-start | bytes 1376264 | tf_op jit(solution)/shard_map/ppermute | solution.py:30
  20.8 0.5 collective-permute-start.1
  21.2 0.0 collective-permute-done.3.refs_3_
  21.2 0.0 collective-permute-done.4.refs_4_
  21.2 0.0 copy-start.4
  21.3 0.0 copy-start.3
  21.3 1.3 %partial_sums.1 = (bf16[128,1792]{1,0:T(8,128)(2,1)S(1)}, bf16[128,1792]{1,0:T(8,128)(2,1)S(1)}) custom-call(bf16[128,1792]{1,0:T(8,128)(2,1)S(1)} %get-tuple-element.24.refs_0_, bf16[128,1792]{1,0:T(8,128)(2,1)S(1)} %collective-permute-done.2.refs_1_, bf16[128,1792]{1,0:T(8,128)(2,1)S(1)} %get-tuple-element.26.refs_2_, ...), custom_call_target="tpu_custom_call" | custom-call | flops 1150000037888 | bytes 3211264 | tf_op jit(solution)/shard_map/partial_sums/pallas_call | solution.py:248
  22.6 2.1 %collective-permute-start.6 = (bf16[128,1792]{1,0:T(8,128)(2,1)S(1)}, bf16[128,1792]{1,0:T(8,128)(2,1)S(1)}, u32[]{:S(2)}, u32[]{:S(2)}) collective-permute-start(bf16[128,1792]{1,0:T(8,128)(2,1)S(1)} %get-tuple-element.30), channel_id=1, source_target_pairs={{0,32},{32,0},{64,96},{96,64},{128,160},{160,128},{192,224},{224,1... | collective-permute-start | bytes 1376264 | tf_op jit(solution)/shard_map/ppermute | solution.py:30
  24.7 0.1 copy.20
  24.7 0.2 reduce_window_sum.11
  24.9 2.4 %collective-permute-start.5 = (bf16[128,1792]{1,0:T(8,128)(2,1)S(1)}, bf16[128,1792]{1,0:T(8,128)(2,1)S(1)}, u32[]{:S(2)}, u32[]{:S(2)}) collective-permute-start(bf16[128,1792]{1,0:T(8,128)(2,1)S(1)} %get-tuple-element.29), channel_id=1, source_target_pairs={{0,128},{32,160},{64,192},{96,224},{128,0},{160,32},{192,64},{224,... | collective-permute-start | bytes 1376264 | tf_op jit(solution)/shard_map/ppermute | solution.py:30
  27.3 0.5 select_reduce_fusion.1
  27.8 0.1 add_select_fusion
  27.9 0.1 select_n.24
  28.0 17.4 %all-to-all-done = bf16[32,8,1792]{2,1,0:T(8,128)(2,1)} async-done(((bf16[32,8,1792]{2,1,0:T(8,128)(2,1)}), bf16[32,8,1792]{2,1,0:T(8,128)(2,1)}, u32[]{:S(2)}, u32[]{:S(2)}) %all-to-all-start) | async-done | bytes 917536 | tf_op jit(solution)/shard_map/all_to_all | solution.py:345
  45.4 1.5 %own_share.1.refs_5_ = bf16[128,1792]{1,0:T(8,128)(2,1)S(1)} custom-call(bf16[128,256]{1,0:T(8,128)(2,1)S(1)} %fusion.1.pick_ref, bf16[256,1792]{1,0:T(8,128)(2,1)} %bitcast.4.array_ref), custom_call_target="tpu_custom_call" | custom-call | flops 117440512 | bytes 1376256 | tf_op jit(solution)/shard_map/own_share/pallas_call | solution.py:274
  46.9 1.5 %fresh_rows.1 = (bf16[128,1792]{1,0:T(8,128)(2,1)S(1)}, bf16[128,1792]{1,0:T(8,128)(2,1)S(1)}) custom-call(bf16[128,1792]{1,0:T(8,128)(2,1)S(1)} %get-tuple-element.21.refs_0_, bf16[128,1792]{1,0:T(8,128)(2,1)} %collective-permute-done.refs_1_, bf16[128,1792]{1,0:T(8,128)(2,1)} %collective-permute-done.1.refs_2_, ...), custom_call_target="tpu_custom_call" | custom-call | flops 1605632 | bytes 3670016 | tf_op jit(solution)/shard_map/fresh_rows/pallas_call | solution.py:215
  48.4 2.4 %collective-permute-start.8 = (bf16[128,1792]{1,0:T(8,128)(2,1)S(1)}, bf16[128,1792]{1,0:T(8,128)(2,1)}, u32[]{:S(2)}, u32[]{:S(2)}) collective-permute-start(bf16[128,1792]{1,0:T(8,128)(2,1)S(1)} %get-tuple-element.32.refs_0_), channel_id=1, source_target_pairs={{0,128},{32,160},{64,192},{96,224},{128,0},{160,32},{192,64},{224,... | collective-permute-start | bytes 1376264 | tf_op jit(solution)/shard_map/ppermute | solution.py:30
  50.8 2.0 %collective-permute-start.7 = (bf16[128,1792]{1,0:T(8,128)(2,1)S(1)}, bf16[128,1792]{1,0:T(8,128)(2,1)}, u32[]{:S(2)}, u32[]{:S(2)}) collective-permute-start(bf16[128,1792]{1,0:T(8,128)(2,1)S(1)} %get-tuple-element.32.refs_0_), channel_id=1, source_target_pairs={{0,32},{32,0},{64,96},{96,64},{128,160},{160,128},{192,224},{224,1... | collective-permute-start | bytes 1376264 | tf_op jit(solution)/shard_map/ppermute | solution.py:30
  52.8 0.1 fusion.2.pick_ref
  52.9 1.3 %pack_slots.1 = bf16[256,1792]{1,0:T(8,128)(2,1)} custom-call(bf16[256,128]{1,0:T(8,128)(2,1)S(1)} %fusion.2.pick_ref, bf16[128,1792]{1,0:T(8,128)(2,1)S(1)} %get-tuple-element.35.array_ref), custom_call_target="tpu_custom_call" | custom-call | flops 117440512 | bytes 1376256 | tf_op jit(solution)/shard_map/pack_slots/pallas_call | solution.py:274
  54.3 5.1 %all-to-all-start.1 = ((bf16[32,8,1792]{2,1,0:T(8,128)(2,1)}), bf16[32,8,1792]{2,1,0:T(8,128)(2,1)S(1)}, u32[]{:S(2)}, u32[]{:S(2)}) async-start(bf16[32,8,1792]{2,1,0:T(8,128)(2,1)} %bitcast.5), calls=%async_computation.1 | async-start | bytes 1835008 | tf_op jit(solution)/shard_map/all_to_all | solution.py:365
  59.4 0.1 collective-permute-start.13
  59.5 2.0 %collective-permute-start.12 = (bf16[128,1792]{1,0:T(8,128)(2,1)S(1)}, bf16[128,1792]{1,0:T(8,128)(2,1)}, u32[]{:S(2)}, u32[]{:S(2)}) collective-permute-start(bf16[128,1792]{1,0:T(8,128)(2,1)S(1)} %get-tuple-element.32.refs_0_), channel_id=1, source_target_pairs={{0,192},{32,224},{64,0},{96,32},{128,64},{160,96},{192,128},{224,1... | collective-permute-start | bytes 1376264 | tf_op jit(solution)/shard_map/ppermute | solution.py:30
  61.5 0.4 collective-permute-done.8.refs_1_
  61.9 2.5 %collective-permute-done.7.refs_0_ = bf16[128,1792]{1,0:T(8,128)(2,1)} collective-permute-done((bf16[128,1792]{1,0:T(8,128)(2,1)S(1)}, bf16[128,1792]{1,0:T(8,128)(2,1)}, u32[]{:S(2)}, u32[]{:S(2)}) %collective-permute-start.7) | collective-permute-done | bytes 458784 | tf_op jit(solution)/shard_map/ppermute | solution.py:30
  64.4 3.0 %collective-permute-start.11 = (bf16[128,1792]{1,0:T(8,128)(2,1)}, bf16[128,1792]{1,0:T(8,128)(2,1)}, u32[]{:S(2)}, u32[]{:S(2)}) collective-permute-start(bf16[128,1792]{1,0:T(8,128)(2,1)} %get-tuple-element.34.refs_2_), channel_id=1, source_target_pairs={{0,32},{32,0},{64,96},{96,64},{128,160},{160,128},{192,224},{224,1... | collective-permute-start | bytes 1376264 | tf_op jit(solution)/shard_map/ppermute | solution.py:30
  67.4 1.2 %collective-permute-start.10 = (bf16[128,1792]{1,0:T(8,128)(2,1)}, bf16[128,1792]{1,0:T(8,128)(2,1)}, u32[]{:S(2)}, u32[]{:S(2)}) collective-permute-start(bf16[128,1792]{1,0:T(8,128)(2,1)} %get-tuple-element.33.refs_1_), channel_id=1, source_target_pairs={{0,64},{32,96},{64,128},{96,160},{128,192},{160,224},{192,0},{224,... | collective-permute-start | bytes 1376264 | tf_op jit(solution)/shard_map/ppermute | solution.py:30
  68.6 1.3 %collective-permute-start.9 = (bf16[128,1792]{1,0:T(8,128)(2,1)}, bf16[128,1792]{1,0:T(8,128)(2,1)}, u32[]{:S(2)}, u32[]{:S(2)}) collective-permute-start(bf16[128,1792]{1,0:T(8,128)(2,1)} %get-tuple-element.33.refs_1_), channel_id=1, source_target_pairs={{0,192},{32,224},{64,0},{96,32},{128,64},{160,96},{192,128},{224,1... | collective-permute-start | bytes 1376264 | tf_op jit(solution)/shard_map/ppermute | solution.py:30
  69.9 0.2 dynamic-slice_reduce_fusion
  70.1 0.1 fusion.3
  70.2 0.1 reshape.115
  70.3 0.0 copy-start.1
  70.3 2.6 %collective-permute-done.13.refs_4_ = bf16[128,1792]{1,0:T(8,128)(2,1)} collective-permute-done((bf16[128,1792]{1,0:T(8,128)(2,1)S(1)}, bf16[128,1792]{1,0:T(8,128)(2,1)}, u32[]{:S(2)}, u32[]{:S(2)}) %collective-permute-start.13) | collective-permute-done | bytes 458784 | tf_op jit(solution)/shard_map/ppermute | solution.py:30
  72.9 0.1 collective-permute-done.12.refs_3_
  73.0 2.8 %join_columns.1.refs_7_ = bf16[128,14336]{1,0:T(8,128)(2,1)} custom-call(bf16[128,1792]{1,0:T(8,128)(2,1)S(1)} %get-tuple-element.32.refs_0_, bf16[128,1792]{1,0:T(8,128)(2,1)} %get-tuple-element.33.refs_1_, bf16[128,1792]{1,0:T(8,128)(2,1)} %get-tuple-element.34.refs_2_, bf16[128,1792]{1,0:T(8,128)(2,1)} %collective-permute-done.12.refs_3_, ...), custom_call_target="tpu_custom_call" | custom-call | bytes 4587520 | tf_op jit(solution)/shard_map/join_columns/pallas_call | solution.py:109
  75.9 7.5 %collective-permute-done.11.refs_2_ = bf16[128,1792]{1,0:T(8,128)(2,1)} collective-permute-done((bf16[128,1792]{1,0:T(8,128)(2,1)}, bf16[128,1792]{1,0:T(8,128)(2,1)}, u32[]{:S(2)}, u32[]{:S(2)}) %collective-permute-start.11) | collective-permute-done | bytes 458784 | tf_op jit(solution)/shard_map/ppermute | solution.py:30
  83.3 2.2 %all-to-all-done.1 = bf16[32,8,1792]{2,1,0:T(8,128)(2,1)S(1)} async-done(((bf16[32,8,1792]{2,1,0:T(8,128)(2,1)}), bf16[32,8,1792]{2,1,0:T(8,128)(2,1)S(1)}, u32[]{:S(2)}, u32[]{:S(2)}) %all-to-all-start.1) | async-done | bytes 917536 | tf_op jit(solution)/shard_map/all_to_all | solution.py:365
  85.6 0.1 broadcast_in_dim.6.refs_6_
  85.7 7.0 %finish.1 = (f32[256,1792]{1,0:T(8,128)}, f32[256,1792]{1,0:T(8,128)}, bf16[128,14336]{1,0:T(8,128)(2,1)}) custom-call(bf16[128,1792]{1,0:T(8,128)(2,1)} %collective-permute-done.9.refs_0_, bf16[128,1792]{1,0:T(8,128)(2,1)} %collective-permute-done.10.refs_1_, bf16[128,1792]{1,0:T(8,128)(2,1)} %collective-permute-done.11.refs_2_, ...), custom_call_target="tpu_custom_call", output_to_operand_aliasing={{2}: (7, {})} | custom-call | flops 4587520 | bytes 11010048 | tf_op jit(solution)/shard_map/finish/pallas_call | solution.py:172
  (16 shorter events, 0.1 us)
Async XLA Ops:
  0.6 8.5 %copy-start = (f32[1,32,8,1792]{3,2,1,0:T(8,128)S(1)}, f32[1,32,8,1792]{3,2,1,0:T(8,128)}, u32[]{:S(2)}) copy-start(f32[1,32,8,1792]{3,2,1,0:T(8,128)} %param.7) | copy-start | bytes 5505028
  0.6 8.5 %copy-start.2 = (f32[1,32,8,1792]{3,2,1,0:T(8,128)S(1)}, f32[1,32,8,1792]{3,2,1,0:T(8,128)}, u32[]{:S(2)}) copy-start(f32[1,32,8,1792]{3,2,1,0:T(8,128)} %param.6) | copy-start | bytes 5505028
  4.0 17.3 %collective-permute-start.2 = (bf16[128,1792]{1,0:T(8,128)(2,1)}, bf16[128,1792]{1,0:T(8,128)(2,1)S(1)}, u32[]{:S(2)}, u32[]{:S(2)}) collective-permute-start(bf16[128,1792]{1,0:T(8,128)(2,1)} %get-tuple-element.25), channel_id=1, source_target_pairs={{0,32},{32,0},{64,96},{96,64},{128,160},{160,128},{192,224},{224,1... | collective-permute-start | bytes 1376264 | tf_op jit(solution)/shard_map/ppermute | solution.py:30
  7.1 14.1 %collective-permute-start.3 = (bf16[128,1792]{1,0:T(8,128)(2,1)S(1)}, bf16[128,1792]{1,0:T(8,128)(2,1)S(1)}, u32[]{:S(2)}, u32[]{:S(2)}) collective-permute-start(bf16[128,1792]{1,0:T(8,128)(2,1)S(1)} %get-tuple-element.27), channel_id=1, source_target_pairs={{0,64},{32,96},{64,128},{96,160},{128,192},{160,224},{192,0},{224,... | collective-permute-start | bytes 1376264 | tf_op jit(solution)/shard_map/ppermute | solution.py:30
  8.7 12.6 %collective-permute-start.4 = (bf16[128,1792]{1,0:T(8,128)(2,1)S(1)}, bf16[128,1792]{1,0:T(8,128)(2,1)}, u32[]{:S(2)}, u32[]{:S(2)}) collective-permute-start(bf16[128,1792]{1,0:T(8,128)(2,1)S(1)} %get-tuple-element.28), channel_id=1, source_target_pairs={{0,192},{32,224},{64,0},{96,32},{128,64},{160,96},{192,128},{224,1... | collective-permute-start | bytes 1376264 | tf_op jit(solution)/shard_map/ppermute | solution.py:30
  10.3 35.1 %all-to-all-start = ((bf16[32,8,1792]{2,1,0:T(8,128)(2,1)}), bf16[32,8,1792]{2,1,0:T(8,128)(2,1)}, u32[]{:S(2)}, u32[]{:S(2)}) async-start(bf16[32,8,1792]{2,1,0:T(8,128)(2,1)} %fusion), calls=%async_computation | async-start | bytes 1835008 | tf_op jit(solution)/shard_map/all_to_all | solution.py:345
  19.1 27.7 %collective-permute-start = (bf16[128,1792]{1,0:T(8,128)(2,1)}, bf16[128,1792]{1,0:T(8,128)(2,1)}, u32[]{:S(2)}, u32[]{:S(2)}) collective-permute-start(bf16[128,1792]{1,0:T(8,128)(2,1)} %get-tuple-element.22), channel_id=1, source_target_pairs={{0,64},{32,96},{64,128},{96,160},{128,192},{160,224},{192,0},{224,... | collective-permute-start | bytes 1376264 | tf_op jit(solution)/shard_map/ppermute | solution.py:30
  20.8 26.1 %collective-permute-start.1 = (bf16[128,1792]{1,0:T(8,128)(2,1)}, bf16[128,1792]{1,0:T(8,128)(2,1)}, u32[]{:S(2)}, u32[]{:S(2)}) collective-permute-start(bf16[128,1792]{1,0:T(8,128)(2,1)} %get-tuple-element.23), channel_id=1, source_target_pairs={{0,192},{32,224},{64,0},{96,32},{128,64},{160,96},{192,128},{224,1... | collective-permute-start | bytes 1376264 | tf_op jit(solution)/shard_map/ppermute | solution.py:30
  21.2 3.4 %copy-start.4 = (s32[32,24]{0,1:T(8,128)S(1)}, s32[32,24]{0,1:T(8,128)}, u32[]{:S(2)}) copy-start(s32[32,24]{0,1:T(8,128)} %param.8) | copy-start | bytes 9220
  21.3 6.0 %copy-start.3 = (s32[32,32]{1,0:T(8,128)S(1)}, s32[32,32]{1,0:T(8,128)}, u32[]{:S(2)}) copy-start(s32[32,32]{1,0:T(8,128)} %param.9) | copy-start | bytes 12292
  22.6 24.3 %collective-permute-start.6 = (bf16[128,1792]{1,0:T(8,128)(2,1)S(1)}, bf16[128,1792]{1,0:T(8,128)(2,1)S(1)}, u32[]{:S(2)}, u32[]{:S(2)}) collective-permute-start(bf16[128,1792]{1,0:T(8,128)(2,1)S(1)} %get-tuple-element.30), channel_id=1, source_target_pairs={{0,32},{32,0},{64,96},{96,64},{128,160},{160,128},{192,224},{224,1... | collective-permute-start | bytes 1376264 | tf_op jit(solution)/shard_map/ppermute | solution.py:30
  24.9 21.9 %collective-permute-start.5 = (bf16[128,1792]{1,0:T(8,128)(2,1)S(1)}, bf16[128,1792]{1,0:T(8,128)(2,1)S(1)}, u32[]{:S(2)}, u32[]{:S(2)}) collective-permute-start(bf16[128,1792]{1,0:T(8,128)(2,1)S(1)} %get-tuple-element.29), channel_id=1, source_target_pairs={{0,128},{32,160},{64,192},{96,224},{128,0},{160,32},{192,64},{224,... | collective-permute-start | bytes 1376264 | tf_op jit(solution)/shard_map/ppermute | solution.py:30
  48.4 13.4 %collective-permute-start.8 = (bf16[128,1792]{1,0:T(8,128)(2,1)S(1)}, bf16[128,1792]{1,0:T(8,128)(2,1)}, u32[]{:S(2)}, u32[]{:S(2)}) collective-permute-start(bf16[128,1792]{1,0:T(8,128)(2,1)S(1)} %get-tuple-element.32.refs_0_), channel_id=1, source_target_pairs={{0,128},{32,160},{64,192},{96,224},{128,0},{160,32},{192,64},{224,... | collective-permute-start | bytes 1376264 | tf_op jit(solution)/shard_map/ppermute | solution.py:30
  50.8 13.6 %collective-permute-start.7 = (bf16[128,1792]{1,0:T(8,128)(2,1)S(1)}, bf16[128,1792]{1,0:T(8,128)(2,1)}, u32[]{:S(2)}, u32[]{:S(2)}) collective-permute-start(bf16[128,1792]{1,0:T(8,128)(2,1)S(1)} %get-tuple-element.32.refs_0_), channel_id=1, source_target_pairs={{0,32},{32,0},{64,96},{96,64},{128,160},{160,128},{192,224},{224,1... | collective-permute-start | bytes 1376264 | tf_op jit(solution)/shard_map/ppermute | solution.py:30
  54.3 31.3 %all-to-all-start.1 = ((bf16[32,8,1792]{2,1,0:T(8,128)(2,1)}), bf16[32,8,1792]{2,1,0:T(8,128)(2,1)S(1)}, u32[]{:S(2)}, u32[]{:S(2)}) async-start(bf16[32,8,1792]{2,1,0:T(8,128)(2,1)} %bitcast.5), calls=%async_computation.1 | async-start | bytes 1835008 | tf_op jit(solution)/shard_map/all_to_all | solution.py:365
  59.4 13.5 %collective-permute-start.13 = (bf16[128,1792]{1,0:T(8,128)(2,1)S(1)}, bf16[128,1792]{1,0:T(8,128)(2,1)}, u32[]{:S(2)}, u32[]{:S(2)}) collective-permute-start(bf16[128,1792]{1,0:T(8,128)(2,1)S(1)} %get-tuple-element.32.refs_0_), channel_id=1, source_target_pairs={{0,64},{32,96},{64,128},{96,160},{128,192},{160,224},{192,0},{224,... | collective-permute-start | bytes 1376264 | tf_op jit(solution)/shard_map/ppermute | solution.py:30
  59.5 13.5 %collective-permute-start.12 = (bf16[128,1792]{1,0:T(8,128)(2,1)S(1)}, bf16[128,1792]{1,0:T(8,128)(2,1)}, u32[]{:S(2)}, u32[]{:S(2)}) collective-permute-start(bf16[128,1792]{1,0:T(8,128)(2,1)S(1)} %get-tuple-element.32.refs_0_), channel_id=1, source_target_pairs={{0,192},{32,224},{64,0},{96,32},{128,64},{160,96},{192,128},{224,1... | collective-permute-start | bytes 1376264 | tf_op jit(solution)/shard_map/ppermute | solution.py:30
  64.4 18.9 %collective-permute-start.11 = (bf16[128,1792]{1,0:T(8,128)(2,1)}, bf16[128,1792]{1,0:T(8,128)(2,1)}, u32[]{:S(2)}, u32[]{:S(2)}) collective-permute-start(bf16[128,1792]{1,0:T(8,128)(2,1)} %get-tuple-element.34.refs_2_), channel_id=1, source_target_pairs={{0,32},{32,0},{64,96},{96,64},{128,160},{160,128},{192,224},{224,1... | collective-permute-start | bytes 1376264 | tf_op jit(solution)/shard_map/ppermute | solution.py:30
  67.4 15.9 %collective-permute-start.10 = (bf16[128,1792]{1,0:T(8,128)(2,1)}, bf16[128,1792]{1,0:T(8,128)(2,1)}, u32[]{:S(2)}, u32[]{:S(2)}) collective-permute-start(bf16[128,1792]{1,0:T(8,128)(2,1)} %get-tuple-element.33.refs_1_), channel_id=1, source_target_pairs={{0,64},{32,96},{64,128},{96,160},{128,192},{160,224},{192,0},{224,... | collective-permute-start | bytes 1376264 | tf_op jit(solution)/shard_map/ppermute | solution.py:30
  68.6 14.7 %collective-permute-start.9 = (bf16[128,1792]{1,0:T(8,128)(2,1)}, bf16[128,1792]{1,0:T(8,128)(2,1)}, u32[]{:S(2)}, u32[]{:S(2)}) collective-permute-start(bf16[128,1792]{1,0:T(8,128)(2,1)} %get-tuple-element.33.refs_1_), channel_id=1, source_target_pairs={{0,192},{32,224},{64,0},{96,32},{128,64},{160,96},{192,128},{224,1... | collective-permute-start | bytes 1376264 | tf_op jit(solution)/shard_map/ppermute | solution.py:30
  70.3 15.4 %copy-start.1 = (f32[1,32,8,1792]{3,2,1,0:T(8,128)S(1)}, f32[1,32,8,1792]{3,2,1,0:T(8,128)}, u32[]{:S(2)}) copy-start(f32[1,32,8,1792]{3,2,1,0:T(8,128)} %param.7) | copy-start | bytes 5505028
